TPU v7x, 32 devices: a whole 2x2x4 slice. The times are simulated.
32 devices in a mesh: dp: 32 (over z, y, x, core).
Axes of the slice: x: 2, y: 2, z: 4, core: 2. Of those that a mesh axis runs over, the one named last changes fastest.
Arguments:
- tokens: bfloat16 [49152, 768], P('dp'), may hold values from -6 to 6
- lengths: int32 [192], P('dp'), may hold values from 64 to 256, as said below
- w_qkv: bfloat16 [768, 2304], P('dp'), may hold values from -0.21875 to 0.21875
- w_out: bfloat16 [768, 768], P('dp'), may hold values from -1.75 to 1.75
- w_in: bfloat16 [768, 3072], P('dp'), may hold values from -0.21875 to 0.21875
- w_down: bfloat16 [768, 3072], P('dp'), may hold values from -0.109375 to 0.109375
- vector: bfloat16 [9216], P('dp'), may hold values from -3 to 3
- key_qkv: float32 [768, 2304], P('dp'), may hold values from -0.21875 to 0.21875
- key_out: float32 [768, 768], P('dp'), may hold values from -1.75 to 1.75
- key_in: float32 [768, 3072], P('dp'), may hold values from -0.21875 to 0.21875
- key_down: float32 [768, 3072], P('dp'), may hold values from -0.109375 to 0.109375
- key_vector: float32 [9216], P('dp'), may hold values from -3 to 3
- cotangent: bfloat16 [49152, 768], P('dp'), may hold values from -6 to 6
Outputs:
- output: bfloat16 [49152, 768], P('dp')
- grad_tokens: float32 [49152, 768], P('dp')
- grad_qkv: float32 [768, 2304], P('dp')
- grad_out: float32 [768, 768], P('dp')
- grad_in: float32 [768, 3072], P('dp')
- grad_down: float32 [768, 3072], P('dp')
- grad_vector: float32 [9216], P('dp')
- key_delta_qkv: float32 [768, 2304], P('dp')
- key_delta_out: float32 [768, 768], P('dp')
- key_delta_in: float32 [768, 3072], P('dp')
- key_delta_down: float32 [768, 3072], P('dp')
- key_delta_vector: float32 [9216], P('dp')
Inputs may be any that keep to these rules, and one draw needn't show every extreme that they name: `lengths`: each crop holds its tokens at the head of its 256 slots; some crop holds exactly 256.
All inputs are finite; a program needn't handle non-finite values.
Results may differ from a plain program's by a relative error of at most 0.012.
The roundings to bfloat16 on the way count: a program that leaves them out, or rounds other values in their place, can miss the bound.
Values may be sent and summed in bfloat16 or wider, within the bound.
No kernel may reach another device: no remote copies, remote signals or barrier semaphores. Data moves between devices by JAX's collectives and lax.ppermute only.
A program may use at most 192 MiB of HBM per device.

v0:
```python
import jax
import jax.numpy as jnp
from jax import lax
from jax.sharding import PartitionSpec as P

H = 12


epsilon = 1e-12


def vector_piece(vector, number, model_width):
    return vector[number * model_width : (number + 1) * model_width]


def norm_forward(residual, gain_row, offset):
    center = residual - jnp.mean(residual, axis=-1, keepdims=True)
    inv_std = lax.rsqrt(jnp.mean(center * center, axis=-1, keepdims=True) + epsilon)
    normal = center * inv_std
    return (normal * gain_row + offset, normal, inv_std)


def norm_backward(upstream, normal, inv_std, gain_row):
    scaled = upstream * gain_row
    return inv_std * (
        scaled
        - jnp.mean(scaled, axis=-1, keepdims=True)
        - normal * jnp.mean(scaled * normal, axis=-1, keepdims=True)
    )


def gelu_slope(hidden):
    return (
        0.5 * (1.0 + lax.erf(hidden * 0.7071067811865476))
        + hidden * jnp.exp(-0.5 * hidden * hidden) * 0.3989422804014327
    )


def attention_scores(queries, key_rows, usable, factor):
    raw_scores = (
        jnp.einsum("cqhd,ckhd->chqk", queries, key_rows, preferred_element_type=jnp.float32)
        * factor
    )
    return jnp.where(usable[:, None, None, :], raw_scores, -1e30)


def momentum_step(weight, copy):
    return (weight.astype(jnp.float32) - copy) * 0.0005


def local(
    tokens,
    lengths,
    w_qkv,
    w_out,
    w_in,
    w_down,
    vector,
    key_qkv,
    key_out,
    key_in,
    key_down,
    key_vector,
    cotangent,
):
    model_width = tokens.shape[1]
    crop_count = lengths.shape[0]
    row_count = tokens.shape[0]
    slot_count = row_count // crop_count
    head_count = H
    head_size = model_width // head_count
    factor = head_size ** (-0.5)
    full_qkv, full_out, full_in, full_down, full_vector = (
        lax.all_gather(w_qkv, "dp", axis=0, tiled=True),
        lax.all_gather(w_out, "dp", axis=0, tiled=True),
        lax.all_gather(w_in, "dp", axis=0, tiled=True),
        lax.all_gather(w_down, "dp", axis=0, tiled=True),
        lax.all_gather(vector, "dp", axis=0, tiled=True),
    )
    vector_f = full_vector.astype(jnp.float32)
    bias_qkv = jnp.concatenate(
        [
            vector_piece(vector_f, 0, model_width),
            jnp.zeros((model_width,), jnp.float32),
            vector_piece(vector_f, 1, model_width),
        ]
    )
    gain_one = 1.0 + vector_piece(vector_f, 3, model_width)
    shift_one = vector_piece(vector_f, 4, model_width)
    gain_two = 1.0 + vector_piece(vector_f, 5, model_width)
    shift_two = vector_piece(vector_f, 6, model_width)
    usable = lax.broadcasted_iota(jnp.int32, (crop_count, slot_count), 1) < lengths[:, None]
    qkv_b = (jnp.dot(tokens, full_qkv, preferred_element_type=jnp.float32) + bias_qkv).astype(
        jnp.bfloat16
    )
    split_qkv = qkv_b.reshape(crop_count, slot_count, 3, head_count, head_size)
    queries = split_qkv[:, :, 0]
    key_rows = split_qkv[:, :, 1]
    value_rows = split_qkv[:, :, 2]
    scores = attention_scores(queries, key_rows, usable, factor)
    row_top = jnp.max(scores, axis=-1, keepdims=True)
    exp_terms = jnp.exp(scores - row_top)
    row_mass = jnp.sum(exp_terms, axis=-1, keepdims=True)
    probs_b = (exp_terms / row_mass).astype(jnp.bfloat16)
    log_mass = row_top + jnp.log(row_mass)
    attended_b = (
        jnp.einsum("chqk,ckhd->cqhd", probs_b, value_rows, preferred_element_type=jnp.float32)
        .reshape(row_count, model_width)
        .astype(jnp.bfloat16)
    )
    branch = jnp.dot(attended_b, full_out, preferred_element_type=jnp.float32) + vector_piece(
        vector_f, 2, model_width
    )
    normed, normal_one, inv_one = norm_forward(
        tokens.astype(jnp.float32) + branch, gain_one, shift_one
    )
    normed_b = normed.astype(jnp.bfloat16)
    hidden = (
        jnp.dot(normed_b, full_in, preferred_element_type=jnp.float32) + vector_f[8 * model_width :]
    )
    active_b = jax.nn.gelu(hidden, approximate=False).astype(jnp.bfloat16)
    feed_out = jnp.einsum(
        "rf,df->rd", active_b, full_down, preferred_element_type=jnp.float32
    ) + vector_piece(vector_f, 7, model_width)
    output, normal_two, inv_two = norm_forward(normed + feed_out, gain_two, shift_two)
    full_qkv, full_out, full_in, full_down = (
        lax.all_gather(w_qkv, "dp", axis=0, tiled=True),
        lax.all_gather(w_out, "dp", axis=0, tiled=True),
        lax.all_gather(w_in, "dp", axis=0, tiled=True),
        lax.all_gather(w_down, "dp", axis=0, tiled=True),
    )
    upstream = cotangent.astype(jnp.float32)
    grad_shift_two = jnp.sum(upstream, axis=0)
    grad_gain_two = jnp.sum(upstream * normal_two, axis=0)
    d_resid_two = norm_backward(upstream, normal_two, inv_two, gain_two)
    d_feed_b = d_resid_two.astype(jnp.bfloat16)
    d_active = jnp.dot(d_feed_b, full_down, preferred_element_type=jnp.float32)
    d_hidden_b = (d_active * gelu_slope(hidden)).astype(jnp.bfloat16)
    d_normed = d_resid_two + jnp.einsum(
        "rf,df->rd", d_hidden_b, full_in, preferred_element_type=jnp.float32
    )
    grad_shift_one = jnp.sum(d_normed, axis=0)
    grad_gain_one = jnp.sum(d_normed * normal_one, axis=0)
    d_resid_one = norm_backward(d_normed, normal_one, inv_one, gain_one)
    d_branch_b = d_resid_one.astype(jnp.bfloat16)
    d_attended_b = jnp.einsum(
        "rd,ed->re", d_branch_b, full_out, preferred_element_type=jnp.float32
    ).astype(jnp.bfloat16)
    d_attended_b = d_attended_b.reshape(crop_count, slot_count, head_count, head_size)
    scores = attention_scores(queries, key_rows, usable, factor)
    probs = jnp.exp(scores - log_mass)
    d_values = jnp.einsum(
        "chqk,cqhd->ckhd",
        probs.astype(jnp.bfloat16),
        d_attended_b,
        preferred_element_type=jnp.float32,
    )
    d_probs = jnp.einsum(
        "cqhd,ckhd->chqk", d_attended_b, value_rows, preferred_element_type=jnp.float32
    )
    row_inner = jnp.sum(probs * d_probs, axis=-1, keepdims=True)
    d_scores_b = (probs * (d_probs - row_inner)).astype(jnp.bfloat16)
    d_queries = (
        jnp.einsum("chqk,ckhd->cqhd", d_scores_b, key_rows, preferred_element_type=jnp.float32)
        * factor
    )
    d_keys = (
        jnp.einsum("chqk,cqhd->ckhd", d_scores_b, queries, preferred_element_type=jnp.float32)
        * factor
    )
    d_qkv_b = (
        jnp.stack([d_queries, d_keys, d_values], axis=2)
        .reshape(row_count, 3 * model_width)
        .astype(jnp.bfloat16)
    )
    grad_tokens = d_resid_one + jnp.einsum(
        "re,de->rd", d_qkv_b, full_qkv, preferred_element_type=jnp.float32
    )
    sums_qkv = jnp.sum(d_qkv_b.astype(jnp.float32), axis=0)
    grad_vec_local = jnp.concatenate(
        [
            vector_piece(sums_qkv, 0, model_width),
            vector_piece(sums_qkv, 2, model_width),
            jnp.sum(d_branch_b.astype(jnp.float32), axis=0),
            grad_gain_one,
            grad_shift_one,
            grad_gain_two,
            grad_shift_two,
            jnp.sum(d_feed_b.astype(jnp.float32), axis=0),
            jnp.sum(d_hidden_b.astype(jnp.float32), axis=0),
        ]
    )
    local_qkv = jnp.einsum("rd,re->de", tokens, d_qkv_b, preferred_element_type=jnp.float32)
    local_out = jnp.einsum("rd,re->de", attended_b, d_branch_b, preferred_element_type=jnp.float32)
    local_in = jnp.einsum("rd,rf->df", normed_b, d_hidden_b, preferred_element_type=jnp.float32)
    local_down = jnp.einsum("rd,rf->df", d_feed_b, active_b, preferred_element_type=jnp.float32)
    grad_qkv, grad_out, grad_in, grad_down, grad_vector = (
        lax.psum_scatter(local_qkv, "dp", scatter_dimension=0, tiled=True),
        lax.psum_scatter(local_out, "dp", scatter_dimension=0, tiled=True),
        lax.psum_scatter(local_in, "dp", scatter_dimension=0, tiled=True),
        lax.psum_scatter(local_down, "dp", scatter_dimension=0, tiled=True),
        lax.psum_scatter(grad_vec_local, "dp", scatter_dimension=0, tiled=True),
    )
    key_delta_qkv = momentum_step(w_qkv, key_qkv)
    key_delta_out = momentum_step(w_out, key_out)
    key_delta_in = momentum_step(w_in, key_in)
    key_delta_down = momentum_step(w_down, key_down)
    key_delta_vector = momentum_step(vector, key_vector)
    return (
        output.astype(jnp.bfloat16),
        grad_tokens,
        grad_qkv,
        grad_out,
        grad_in,
        grad_down,
        grad_vector,
        key_delta_qkv,
        key_delta_out,
        key_delta_in,
        key_delta_down,
        key_delta_vector,
    )


def solution(mesh):
    return jax.shard_map(
        local,
        mesh=mesh,
        in_specs=(
            P("dp", None),
            P("dp"),
            P("dp", None),
            P("dp", None),
            P("dp", None),
            P("dp", None),
            P("dp"),
            P("dp", None),
            P("dp", None),
            P("dp", None),
            P("dp", None),
            P("dp"),
            P("dp", None),
        ),
        out_specs=(
            P("dp", None),
            P("dp", None),
            P("dp", None),
            P("dp", None),
            P("dp", None),
            P("dp", None),
            P("dp"),
            P("dp", None),
            P("dp", None),
            P("dp", None),
            P("dp", None),
            P("dp"),
        ),
        check_vma=False,
    )
```

profile of v0, /device:TPU:0, one launch (start us, length us, event | category | flops | bytes accessed | tf_op | source)
XLA Modules:
  0.0 899.1 jit_solution(6382683053756995028)
XLA Ops:
  10.9 42.2 %all-reduce = bf16[9216]{0:T(1024)(128)(2,1)S(1)} all-reduce(bf16[9216]{0:T(1024)(128)(2,1)S(1)} %dynamic-update-slice), channel_id=1, replica_groups=mesh['dp'=32] {'dp'}, use_global_device_ids=true, to_apply=%add | all-reduce | flops 9216 | bytes 36864
  54.5 4.3 copy.63
  58.8 2.4 copy.71
  61.2 12.6 %all-gather.5.cloned.1.call-done = bf16[768,2304]{1,0:T(8,128)(2,1)} async-done(((bf16[24,2304]{1,0:T(8,128)(2,1)}), bf16[768,2304]{1,0:T(8,128)(2,1)}) %all-gather.5.cloned.1.call-update) | async-done | bytes 3538960 | tf_op jit(solution)/shard_map/all_gather | solution.py:74
  73.8 10.0 %add_convert_fusion = bf16[1536,2304]{1,0:T(8,128)(2,1)} fusion(bf16[1536,768]{1,0:T(8,128)(2,1)} %param.13, bf16[768,2304]{1,0:T(8,128)(2,1)} %all-gather.5.cloned.1.call-done, f32[2304]{0:T(1024)S(1)} %pad_maximum_fusion), kind=kOutput, calls=%fused_computation.37 | convolution fusion | flops 5442895872 | bytes 12985344 | tf_op jit(solution)/shard_map/dot_general | solution.py:93
  83.8 21.8 %reshape.117 = bf16[6,256,3,12,64]{4,3,2,1,0:T(8,128)(2,1)} reshape(bf16[1536,2304]{1,0:T(8,128)(2,1)} %add_convert_fusion) | data formatting | bytes 14155776 | tf_op jit(solution)/shard_map/reshape | solution.py:96
  105.6 14.3 %fusion.57 = (bf16[6,256,1,12,64]{4,3,2,1,0:T(8,128)(2,1)}, bf16[6,256,1,12,64]{4,3,2,1,0:T(8,128)(2,1)}, bf16[6,256,1,12,64]{4,3,2,1,0:T(8,128)(2,1)}) fusion(bf16[6,256,3,12,64]{4,3,2,1,0:T(8,128)(2,1)} %reshape.117), kind=kLoop, calls=%fused_computation.116 | loop fusion | bytes 14155776 | tf_op jit(solution)/shard_map/slice | solution.py:99
  119.9 6.3 copy.98
  126.2 8.1 copy.99
  134.4 7.4 copy.97
  141.8 11.0 %fusion.60 = (f32[6,12,256]{2,1,0:T(8,128)S(1)}, f32[6,12,256,256]{2,3,1,0:T(8,128)}) fusion(bf16[6,256,1,12,64]{1,4,3,0,2:T(8,128)(2,1)} %copy.99, bf16[6,256,1,12,64]{1,4,3,0,2:T(8,128)(2,1)S(1)} %copy.98, pred[6,256]{1,0:T(8,128)(4,1)S(1)} %iota_compare_fusion), kind=kOutput, calls=%fused_computation.119 | convolution fusion | flops 618117120 | bytes 23668224 | tf_op jit(solution)/shard_map/cqhd,ckhd->chqk/dot_general | solution.py:41
  152.8 11.4 %fusion.16 = f32[6,12,256]{2,1,0:T(8,128)S(1)} fusion(f32[6,12,256,256]{2,3,1,0:T(8,128)} %get-tuple-element.77, f32[6,12,256]{2,1,0:T(8,128)S(1)} %get-tuple-element.76), kind=kLoop, calls=%fused_computation.33 | loop fusion | flops 9418752 | bytes 19021824 | tf_op jit(solution)/shard_map/reduce_sum | solution.py:103
  164.9 9.8 %convert_bitcast_fusion = bf16[6,256,12,64]{1,3,2,0:T(8,128)(2,1)S(1)} fusion(f32[6,12,256,256]{2,3,1,0:T(8,128)} %get-tuple-element.77, f32[6,12,256]{2,1,0:T(8,128)S(1)} %fusion.16, f32[6,12,256]{2,1,0:T(8,128)S(1)} %get-tuple-element.76, bf16[6,256,1,12,64]{1,4,3,0,2:T(8,128)(2,1)S(1)} %copy-done.9), kind=kOutput, calls=%fused_computation.81 | convolution fusion | flops 619315200 | bytes 23740416 | tf_op jit(solution)/shard_map/chqk,ckhd->cqhd/dot_general | solution.py:107
  176.3 2.3 copy.100
  178.6 4.7 fusion.61
  186.2 8.8 all-gather.9.cloned.1.call-done
  195.1 49.2 %fusion.2 = (bf16[1536,3072]{1,0:T(8,128)(2,1)}, f32[1536,3072]{1,0:T(8,128)}) fusion(f32[3072]{0:T(1024)S(1)} %slice.72, bf16[768,3072]{1,0:T(8,128)(2,1)} %all-gather.9.cloned.1.call-done, bf16[1536,768]{0,1:T(8,128)(2,1)S(1)} %fusion.55.clone.4), kind=kOutput, calls=%fused_computation.4 | convolution fusion | flops 7559184384 | bytes 35401728 | tf_op jit(solution)/shard_map/dot_general | solution.py:119
  244.3 16.1 %all-gather.11.cloned.1.call-done = bf16[768,3072]{1,0:T(8,128)(2,1)} async-done(((bf16[24,3072]{1,0:T(8,128)(2,1)}), bf16[768,3072]{1,0:T(8,128)(2,1)}) %all-gather.11.cloned.1.call-update) | async-done | bytes 4718608 | tf_op jit(solution)/shard_map/all_gather | solution.py:77
  260.4 12.4 %fusion.62 = (f32[1536]{0:T(1024)S(1)}, f32[1536,768]{0,1:T(8,128)S(1)}) fusion(f32[768]{0:T(1024)S(1)} %copy-done.40, bf16[1536,3072]{1,0:T(8,128)(2,1)} %get-tuple-element.80, bf16[768,3072]{1,0:T(8,128)(2,1)} %all-gather.11.cloned.1.call-done, f32[768]{0:T(1024)S(1)} %copy-done.34, f32[768]{0:T(1024)S(1)} %copy-done.31, f32[1536]{0:T(1024)S(1)} %copy-done.29, ...), kind=kOutput, calls=%fused_computation.121 | convolution fusion | flops 7256013312 | bytes 23620608 | tf_op jit(solution)/shard_map/rf,df->rd/dot_general | solution.py:122
  274.5 3.0 fusion.28
  277.5 4.4 convert_reduce_fusion.3
  282.0 20.0 %convert_reduce_fusion = (f32[3072]{0:T(1024)}, bf16[1536,3072]{1,0:T(8,128)(2,1)}) fusion(f32[1536,3072]{1,0:T(8,128)} %get-tuple-element.81, f32[3072]{0:T(1024)S(1)} %slice.72, bf16[1536,768]{0,1:T(8,128)(2,1)S(1)} %get-tuple-element.57, bf16[768,3072]{1,0:T(8,128)(2,1)S(1)} %bitcast.89), kind=kOutput, calls=%fused_computation.11 | convolution fusion | flops 7309095936 | bytes 35414016 | tf_op jit(solution)/shard_map/dot_general | solution.py:137
  302.0 14.0 %multiply_reduce_fusion.1 = (f32[768]{0:T(1024)S(1)}, f32[1536]{0:T(1024)S(1)}, f32[1536]{0:T(1024)S(1)}, f32[768]{0:T(1024)S(1)}, f32[1536,768]{0,1:T(8,128)S(1)}) fusion(f32[1536,768]{0,1:T(8,128)S(1)} %bitcast.81, f32[1536]{0:T(1024)S(1)} %copy-done.29, f32[1536]{0:T(1024)S(1)} %copy-done.26, f32[768]{0:T(1024)S(1)} %copy-done.31, ...), kind=kOutput, calls=%fused_computation.53 | convolution fusion | flops 7268985856 | bytes 30732288 | tf_op jit(solution)/shard_map/rf,df->rd/dot_general | solution.py:139
  317.5 2.2 copy-done.11
  321.7 6.0 reshape.118
  327.8 6.3 copy.74
  334.1 13.3 %multiply_reduce_fusion = (f32[6,12,256]{2,1,0:T(8,128)S(1)}, f32[6,12,256,256]{2,3,1,0:T(8,128)}) fusion(f32[6,12,256,256]{2,3,1,0:T(8,128)} %get-tuple-element.77, f32[6,12,256]{2,1,0:T(8,128)S(1)} %copy-done.17, bf16[6,256,12,64]{1,3,2,0:T(8,128)(2,1)S(1)} %copy.74, bf16[6,256,1,12,64]{1,4,3,0,2:T(8,128)(2,1)} %copy.97), kind=kOutput, calls=%fused_computation.13 | convolution fusion | flops 618117120 | bytes 42614784 | tf_op jit(solution)/shard_map/cqhd,ckhd->chqk/dot_general | solution.py:158
  347.5 10.8 %fusion.43 = bf16[6,256,1,12,64]{1,4,3,0,2:T(8,128)(2,1)} fusion(bf16[6,256,12,64]{1,3,2,0:T(8,128)(2,1)S(1)} %copy.74, f32[6,12,256,256]{2,3,1,0:T(8,128)} %get-tuple-element.77, f32[6,12,256]{2,1,0:T(8,128)S(1)} %copy-done.17), kind=kOutput, calls=%fused_computation.82 | convolution fusion | flops 613416960 | bytes 23666688 | tf_op jit(solution)/shard_map/chqk,cqhd->ckhd/dot_general | solution.py:152
  358.2 6.5 fusion.49
  364.7 13.5 %multiply_convert_fusion = bf16[6,12,256,256]{2,3,1,0:T(8,128)(2,1)S(1)} fusion(f32[6,12,256,256]{2,3,1,0:T(8,128)} %get-tuple-element.86, f32[6,12,256,256]{2,3,1,0:T(8,128)} %get-tuple-element.77, f32[6,12,256]{2,1,0:T(8,128)S(1)} %get-tuple-element.85, f32[6,12,256]{2,1,0:T(8,128)S(1)} %copy-done.17), kind=kLoop, calls=%fused_computation.12 | loop fusion | flops 18874368 | bytes 47333376 | tf_op jit(solution)/shard_map/convert_element_type | solution.py:162
  378.3 3.6 copy-done
  381.9 3.1 multiply_bitcast_fusion.1
  385.1 6.8 multiply_bitcast_fusion
  391.9 4.0 convert_reduce_fusion.1
  395.9 12.4 %copy.79 = bf16[6,256,3,12,64]{1,0,4,3,2:T(8,128)(2,1)} copy(bf16[6,256,3,12,64]{1,4,3,0,2:T(8,128)(2,1)} %get-tuple-element.61) | data formatting | bytes 14155776 | tf_op jit(solution)/shard_map/convert_element_type | solution.py:174
  408.4 7.0 copy.101
  415.4 2.8 copy-done.10
  418.2 7.7 convolution_bitcast_fusion
  426.0 8.1 copy.91
  435.7 12.5 %fusion.63 = f32[768,3072]{1,0:T(8,128)} fusion(bf16[1536,768]{0,1:T(8,128)(2,1)S(1)} %copy-done.16, bf16[1536,3072]{1,0:T(8,128)(2,1)} %get-tuple-element.80), kind=kOutput, calls=%fused_computation.122 | convolution fusion | flops 7247757312 | bytes 21233664 | tf_op jit(solution)/shard_map/rd,rf->df/dot_general | solution.py:196
  448.3 13.8 %fusion.52 = f32[768,3072]{1,0:T(8,128)} fusion(bf16[1536,3072]{1,0:T(8,128)(2,1)} %get-tuple-element.88, f32[1536,768]{0,1:T(8,128)} %copy-done.1, f32[768]{0:T(1024)S(1)} %copy-done.34, f32[768]{0:T(1024)S(1)} %copy-done.31, f32[1536]{0:T(1024)S(1)} %copy-done.29, f32[1536]{0:T(1024)S(1)} %copy-done.26), kind=kOutput, calls=%fused_computation.114 | convolution fusion | flops 7253655552 | bytes 23611392 | tf_op jit(solution)/shard_map/rd,rf->df/dot_general | solution.py:195
  466.4 11.1 %convolution_add_fusion = f32[1536,768]{0,1:T(8,128)} fusion(f32[1536,768]{0,1:T(8,128)} %copy-done.11, bf16[768,2304]{1,0:T(8,128)(2,1)} %all-gather.5.cloned.1.call-done, bf16[1536,2304]{0,1:T(8,128)(2,1)} %bitcast.85), kind=kOutput, calls=%fused_computation.69 | convolution fusion | flops 5436997632 | bytes 20054016 | tf_op jit(solution)/shard_map/re,de->rd/dot_general | solution.py:176
  477.5 6.2 copy.82
  483.7 2.4 copy.81
  486.3 40.0 %all-reduce.1 = f32[9216]{0:T(1024)S(1)} all-reduce(f32[9216]{0:T(1024)S(1)} %constant_dynamic-update-slice_fusion), channel_id=6, replica_groups=mesh['dp'=32] {'dp'}, use_global_device_ids=true, to_apply=%region_23.24.clone | all-reduce | flops 9216 | bytes 73728
  526.9 81.4 %reduce-scatter.13.cloned.1.call-done = f32[24,2304]{1,0:T(8,128)} async-done(((f32[768,2304]{1,0:T(8,128)}), f32[24,2304]{1,0:T(8,128)}) %reduce-scatter.13.cloned.1.call-update) | async-done | bytes 221200
  608.3 141.1 %reduce-scatter.11.cloned.1.call-done = f32[24,3072]{1,0:T(8,128)} async-done(((f32[768,3072]{1,0:T(8,128)}), f32[24,3072]{1,0:T(8,128)}) %reduce-scatter.11.cloned.1.call-update) | async-done | bytes 294928 | tf_op jit(solution)/shard_map/reduce_scatter | solution.py:201
  749.4 142.4 %reduce-scatter.9.cloned.1.call-done = f32[24,3072]{1,0:T(8,128)} async-done(((f32[768,3072]{1,0:T(8,128)}), f32[24,3072]{1,0:T(8,128)}) %reduce-scatter.9.cloned.1.call-update) | async-done | bytes 294928 | tf_op jit(solution)/shard_map/reduce_scatter | solution.py:200
  (155 shorter events, 22.3 us)
Async XLA Ops:
  7.2 51.6 %copy-start.12 = (bf16[1536,768]{1,0:T(8,128)(2,1)S(1)}, bf16[1536,768]{1,0:T(8,128)(2,1)}, u32[]{:S(2)}) copy-start(bf16[1536,768]{1,0:T(8,128)(2,1)} %param.25) | copy-start | bytes 7077892
  7.2 66.6 %all-gather.5.cloned.1.call-start = ((), (), s32[]{:S(2)}) async-start(), calls=%async_computation.4 | async-start | bytes 3649536 | tf_op jit(solution)/shard_map/all_gather | solution.py:74
  7.9 170.7 %all-gather.7.cloned.1.call-start = ((), (), s32[]{:S(2)}) async-start(), calls=%async_computation.5 | async-start | bytes 1216512 | tf_op jit(solution)/shard_map/all_gather | solution.py:75
  8.7 186.4 %all-gather.9.cloned.1.call-start = ((), (), s32[]{:S(2)}) async-start(), calls=%async_computation.6 | async-start | bytes 4866048 | tf_op jit(solution)/shard_map/all_gather | solution.py:76
  9.4 250.9 %all-gather.11.cloned.1.call-start = ((), (), s32[]{:S(2)}) async-start(), calls=%async_computation.7 | async-start | bytes 4866048 | tf_op jit(solution)/shard_map/all_gather | solution.py:77
  10.0 516.9 %reduce-scatter.7.cloned.1.call-start = ((), (), s32[]{:S(2)}) async-start(), calls=%async_computation.8 | async-start | bytes 2433024 | tf_op jit(solution)/shard_map/reduce_scatter | solution.py:199
  53.7 130.2 %copy-start.30 = (f32[768]{0:T(1024)}, f32[768]{0:T(1024)S(1)}, u32[]{:S(2)}) copy-start(f32[768]{0:T(1024)S(1)} %get-tuple-element.67) | copy-start | bytes 9220
  53.7 130.2 %copy-start.33 = (f32[768]{0:T(1024)}, f32[768]{0:T(1024)S(1)}, u32[]{:S(2)}) copy-start(f32[768]{0:T(1024)S(1)} %get-tuple-element.92) | copy-start | bytes 9220
  126.2 15.5 %copy-start.2 = (bf16[6,256,1,12,64]{1,4,3,0,2:T(8,128)(2,1)}, bf16[6,256,1,12,64]{1,4,3,0,2:T(8,128)(2,1)S(1)}, u32[]{:S(2)}) copy-start(bf16[6,256,1,12,64]{1,4,3,0,2:T(8,128)(2,1)S(1)} %copy.98) | copy-start | bytes 7077892
  152.8 12.1 %copy-start.9 = (bf16[6,256,1,12,64]{1,4,3,0,2:T(8,128)(2,1)S(1)}, bf16[6,256,1,12,64]{1,4,3,0,2:T(8,128)(2,1)}, u32[]{:S(2)}) copy-start(bf16[6,256,1,12,64]{1,4,3,0,2:T(8,128)(2,1)} %copy.97) | copy-start | bytes 7077892
  174.7 3.9 copy-start.14
  183.3 2.2 copy-start.1
  183.3 2.2 copy-start.25
  195.1 65.3 %copy-start.26 = (f32[1536]{0:T(1024)S(1)}, f32[1536]{0:T(1024)}, u32[]{:S(2)}) copy-start(f32[1536]{0:T(1024)} %copy-done.25) | copy-start | bytes 18436
  195.1 65.3 %copy-start.29 = (f32[1536]{0:T(1024)S(1)}, f32[1536]{0:T(1024)}, u32[]{:S(2)}) copy-start(f32[1536]{0:T(1024)} %copy-done.28) | copy-start | bytes 18436
  195.1 65.3 %copy-start.31 = (f32[768]{0:T(1024)S(1)}, f32[768]{0:T(1024)}, u32[]{:S(2)}) copy-start(f32[768]{0:T(1024)} %copy-done.30) | copy-start | bytes 9220
  195.1 65.3 %copy-start.34 = (f32[768]{0:T(1024)S(1)}, f32[768]{0:T(1024)}, u32[]{:S(2)}) copy-start(f32[768]{0:T(1024)} %copy-done.33) | copy-start | bytes 9220
  195.1 65.3 %copy-start.40 = (f32[768]{0:T(1024)S(1)}, f32[768]{0:T(1024)}, u32[]{:S(2)}) copy-start(f32[768]{0:T(1024)} %get-tuple-element.93) | copy-start | bytes 9220
  273.4 4.1 copy-start.35
  274.5 7.5 slice-start.2
  277.5 4.5 slice-start.3
  277.5 24.5 %slice-start = ((s8[4718592]{0:T(1024)(128)(4,1)}), s8[4194304]{0:T(1024)(128)(4,1)S(1)}, s32[]{:S(2)}) async-start(s8[4718592]{0:T(1024)(128)(4,1)} %bitcast.80), calls=%async_computation.12 | async-start | bytes 8388608
  282.0 20.0 %copy-start.15 = (bf16[1536,768]{0,1:T(8,128)(2,1)}, bf16[1536,768]{0,1:T(8,128)(2,1)S(1)}, u32[]{:S(2)}) copy-start(bf16[1536,768]{0,1:T(8,128)(2,1)S(1)} %get-tuple-element.57) | copy-start | bytes 7077892
  282.0 20.0 %slice-start.1 = ((s8[4718592]{0:T(1024)(128)(4,1)}), s8[524288]{0:T(1024)(128)(4,1)S(1)}, s32[]{:S(2)}) async-start(s8[4718592]{0:T(1024)(128)(4,1)} %bitcast.80), calls=%async_computation.13 | async-start | bytes 1048576
  316.0 3.7 copy-start.43
  317.5 2.2 copy-start.11
  327.8 6.3 copy-start.17
  364.7 17.2 %copy-start.4 = (bf16[6,256,1,12,64]{1,4,3,0,2:T(8,128)(2,1)S(1)}, bf16[6,256,1,12,64]{1,4,3,0,2:T(8,128)(2,1)}, u32[]{:S(2)}) copy-start(bf16[6,256,1,12,64]{1,4,3,0,2:T(8,128)(2,1)} %copy.99) | copy-start | bytes 7077892
  378.2 3.7 copy-start
  381.9 3.2 copy-start.3
  385.1 223.3 %reduce-scatter.13.cloned.1.call-start = ((), (), s32[]{:S(2)}) async-start(), calls=%async_computation.11 | async-start | bytes 7299072
  385.1 6.8 copy-start.6
  385.1 6.8 copy-start.8
  408.4 9.9 %copy-start.13 = (bf16[1536,768]{1,0:T(8,128)(2,1)S(1)}, bf16[1536,768]{1,0:T(8,128)(2,1)}, u32[]{:S(2)}) copy-start(bf16[1536,768]{1,0:T(8,128)(2,1)} %param.13) | copy-start | bytes 7077892
  415.4 2.8 copy-start.10
  434.1 315.4 %reduce-scatter.11.cloned.1.call-start = ((), (), s32[]{:S(2)}) async-start(), calls=%async_computation.10 | async-start | bytes 9732096 | tf_op jit(solution)/shard_map/reduce_scatter | solution.py:201
  448.2 443.6 %reduce-scatter.9.cloned.1.call-start = ((), (), s32[]{:S(2)}) async-start(), calls=%async_computation.9 | async-start | bytes 9732096 | tf_op jit(solution)/shard_map/reduce_scatter | solution.py:200
  462.1 1.9 copy-start.18
  462.1 1.9 copy-start.21
  462.1 2.6 copy-start.19
  462.1 2.6 copy-start.22
  462.1 3.4 copy-start.20
  462.2 3.4 copy-start.23
  477.5 6.2 copy-start.7
  483.7 2.5 copy-start.37
  483.7 2.5 copy-start.36
  483.7 2.6 copy-start.38
  483.7 2.6 copy-start.39
  (8 other events, 10.5 us)
Sparse Core Ops, SparseCore 0:
  10.9 62.8 all-gather.4
  76.7 52.8 all-gather.6
  132.5 62.5 all-gather.8
  197.8 62.4 all-gather.10
  385.2 97.8 reduce-scatter.6
  490.1 118.1 reduce-scatter.12
  614.8 134.5 reduce-scatter.10
  756.9 134.8 reduce-scatter.8
where the time goes:
time: 908 us; the launch traced here: 899 us
  waiting for transfers between devices  405 us (45%)
  matrix products  219 us (24%)
  local copies, waits for them, and re-layouts  132 us (15%)
  blocking collectives  82.1 us (9%)
  other arithmetic  45.2 us (5%)
  between operations  15.1 us (2%)
    reduce_scatter x1, waiting for transfers between devices, local(): lax.psum_scatter(local_in, 'dp', scatter_dimension=0, tiled=True)  142 us
    reduce_scatter x1, waiting for transfers between devices, local(): lax.psum_scatter(local_down, 'dp', scatter_dimension=0, tiled=True)  141 us
    unnamed x9, waiting for transfers between devices  84.1 us
    unnamed x2, blocking collectives  82.1 us
    unnamed x117, local copies, waits for them, and re-layouts  69.8 us
    dot_general x1, matrix products, local(): jnp.dot(normed_b, full_in, preferred_element_type=jnp.float32)  49.2 us
    reshape x1, local copies, waits for them, and re-layouts, local(): split_qkv = qkv_b.reshape(crop_count, slot_count, 3, head_count, head_size)  21.8 us
    dot_general x1, matrix products, local(): d_active = jnp.dot(d_feed_b, full_down, preferred_element_type=jnp.float32)  20 us
  transfers between devices with their start and end apart: 8, of which 6 were waited for; matrix products, arithmetic and copies ran while one was open for 29% of the time, Pallas kernels for 0%

commit v1 on v0

v1 whole, which is shorter than its diff:
```python
import functools

import jax
import jax.numpy as jnp
import numpy as np
from jax import lax
from jax.experimental import pallas as pl
from jax.experimental.pallas import tpu as pltpu
from jax.sharding import PartitionSpec as P

H = 12
EPS = 1e-12
EXT = 128
bf16 = jnp.bfloat16
f32 = jnp.float32
VMEM_LIMIT = 60 * 1024 * 1024
ANY = pl.BlockSpec(memory_space=pl.ANY)

NT = (((1,), (1,)), ((), ()))
TN = (((0,), (0,)), ((), ()))


def mm(a, b):
    return jnp.dot(a, b, preferred_element_type=f32)


def mm_nt(a, b):
    return lax.dot_general(a, b, NT, preferred_element_type=f32)


def mm_tn(a, b):
    return lax.dot_general(a, b, TN, preferred_element_type=f32)


def row_mean(v):
    return jnp.mean(v, axis=-1, keepdims=True)


def fold_rows(v):
    return jnp.sum(v.reshape(v.shape[0] // 8, 8, v.shape[1]), axis=0)


def chip_row(info, a, k, sign):
    x, y, z = info[1], info[2], info[3]
    xx = x ^ (a & 1)
    yy = y ^ (a >> 1)
    zz = (z + sign * k + 4) & 3
    return pl.multiple_of(((zz * 2 + yy) * 2 + xx) * 48, 16)


def weight_copies(info, refs, w, sems):
    if len(refs) == 1:
        return [pltpu.make_async_copy(refs[0], w, sems.at[0])]
    out = []
    places = (
        [(0, k) for k in range(4)],
        [(1, k) for k in range(4)],
        [(2, k) for k in range(4)],
        [(3, 0), (3, 1)],
        [(3, 2), (3, 3)],
    )
    for source in range(2):
        half = info[0] if source == 0 else 1 - info[0]
        for number, slots in enumerate(places):
            ref = refs[source * 5 + number]
            for j, (a, k) in enumerate(slots):
                row = chip_row(info, a, k, -1)
                out.append(
                    pltpu.make_async_copy(
                        ref.at[pl.ds(48 * j, 48)],
                        w.at[half, pl.ds(row, 48)],
                        sems.at[len(out)],
                    )
                )
    return out


def sem_count(pieces):
    return 1 if len(pieces) == 1 else 32


def attention_forward(n_src, has_ext, pairs, info, x_ref, *refs):
    src = refs[:n_src]
    if has_ext:
        spread_ref, pick_ref = refs[n_src : n_src + 2]
        refs = refs[n_src + 2 :]
    else:
        vec_in = refs[n_src]
        refs = refs[n_src + 1 :]
    vec_ref, qkv_ref, p_ref, a_ref, w, bias, sems = refs
    crop = pl.program_id(0)
    half_width = pairs * 128

    @pl.when(crop == 0)
    def _():
        copies = weight_copies(info, src, w, sems)
        for copy in copies:
            copy.start()
        for copy in copies:
            copy.wait()
        if has_ext:
            spread = mm(w[0, :, 3 * half_width :], spread_ref[...])
            groups = spread.shape[0] // 64
            picked = spread.reshape(groups, 64, spread.shape[1]) * pick_ref[...][None]
            vec_ref[0:groups, :] = jnp.sum(picked, axis=1)
        else:
            vec_ref[...] = vec_in[...]
        for h in range(2):
            for part, row in ((0, 0), (2, 1)):
                bias[h, :, part * half_width : (part + 1) * half_width] = vec_ref[
                    row : row + 1, h * half_width : (h + 1) * half_width
                ]
            bias[h, :, half_width : 2 * half_width] = jnp.zeros((1, half_width), f32)

    x = x_ref[...]
    slots = x.shape[0]
    length = info[4 + crop]
    usable = lax.broadcasted_iota(jnp.int32, (1, slots), 1) < length
    mask_row = jnp.where(usable, 0.0, -1e30).astype(f32)
    lane = lax.broadcasted_iota(jnp.int32, (1, 128), 1)
    sides = (
        jnp.where(lane < 64, 1.0, 0.0).astype(bf16),
        jnp.where(lane < 64, 0.0, 1.0).astype(bf16),
    )
    for h in range(2):
        qkv = (mm(x, w[h, :, : 3 * half_width]) + bias[h]).astype(bf16)
        qkv_ref[h] = qkv
        for p in range(pairs):
            q2 = qkv[:, p * 128 : (p + 1) * 128] * jnp.asarray(0.125, bf16)
            k2 = qkv[:, half_width + p * 128 : half_width + (p + 1) * 128]
            v2 = qkv[:, 2 * half_width + p * 128 : 2 * half_width + (p + 1) * 128]
            total = None
            for side in range(2):
                scores = mm_nt(q2, k2 * sides[side]) + mask_row
                top = jnp.max(scores, axis=1, keepdims=True)
                terms = jnp.exp(scores - top)
                mass = jnp.sum(terms, axis=1, keepdims=True)
                probs = (terms * (1.0 / mass)).astype(bf16)
                p_ref[h, 0, p * 2 + side] = probs
                part = mm(probs, v2 * sides[side])
                total = part if total is None else total + part
            a_ref[:, h * half_width + p * 128 : h * half_width + (p + 1) * 128] = (
                total.astype(bf16)
            )


def attention_backward(pairs, info, qkv_ref, da_ref, p_ref, out_ref, sums_ref):
    half_width = pairs * 128
    lane = lax.broadcasted_iota(jnp.int32, (1, 128), 1)
    sides = (
        jnp.where(lane < 64, 1.0, 0.0).astype(bf16),
        jnp.where(lane < 64, 0.0, 1.0).astype(bf16),
    )
    scale = jnp.asarray(0.125, f32)

    @pl.when(pl.program_id(0) == 0)
    def _():
        sums_ref[...] = jnp.zeros_like(sums_ref)

    for p in range(pairs):
        at = [part * half_width + p * 128 for part in range(3)]
        q2, k2, v2 = [qkv_ref[0, :, lo : lo + 128] for lo in at]
        da2 = da_ref[:, p * 128 : (p + 1) * 128]
        dq = dk = dv = None
        for side in range(2):
            probs_b = p_ref[0, 0, p * 2 + side]
            probs = probs_b.astype(f32)
            d_probs = mm_nt(da2, v2 * sides[side])
            inner = jnp.sum(probs * d_probs, axis=1, keepdims=True)
            d_scores = (probs * (d_probs - inner)).astype(bf16)
            part_v = mm_tn(probs_b, da2 * sides[side])
            part_q = mm(d_scores, k2 * sides[side])
            part_k = mm_tn(d_scores, q2 * sides[side])
            dv = part_v if dv is None else dv + part_v
            dq = part_q if dq is None else dq + part_q
            dk = part_k if dk is None else dk + part_k
        for lo, value in zip(at, (dq * scale, dk * scale, dv)):
            rounded = value.astype(bf16)
            out_ref[0, :, lo : lo + 128] = rounded
            sums_ref[:, lo : lo + 128] += fold_rows(rounded.astype(f32))


def gelu_parts(u):
    size = jnp.abs(u)
    t = 1.0 / (1.0 + size * (0.3275911 * 0.7071067811865476))
    bell = jnp.exp(u * u * -0.5)
    poly = t * (
        0.127414796
        + t * (-0.142248368 + t * (0.7107068705 + t * (-0.7265760135 + t * 0.5307027145)))
    )
    tail = poly * bell
    cdf = jnp.where(u < 0.0, tail, 1.0 - tail)
    return u * cdf, cdf + u * (bell * 0.3989422804014327)


def feed_forward(n_a, n_b, info, vec_ref, x_ref, a_ref, cot_ref, *refs):
    src_a = refs[:n_a]
    src_b = refs[n_a : n_a + n_b]
    (
        out_ref,
        g_ref,
        slope_ref,
        n1_ref,
        z1_ref,
        rstd_ref,
        dr2_ref,
        df_ref,
        sums_ref,
        wa,
        wb,
        sems_a,
        sems_b,
    ) = refs[n_a + n_b :]
    step = pl.program_id(0)
    width = x_ref.shape[1]
    half = width // 2
    copies_a = weight_copies(info, src_a, wa, sems_a)
    copies_b = weight_copies(info, src_b, wb, sems_b)

    @pl.when(step == 0)
    def _():
        for copy in copies_a + copies_b:
            copy.start()
        sums_ref[...] = jnp.zeros_like(sums_ref)
        for copy in copies_a:
            copy.wait()

    attended = a_ref[...]
    branch = jnp.concatenate(
        [mm(attended, wa[h, :, :half]) for h in range(2)], axis=1
    ) + vec_ref[2:3, :]
    resid = x_ref[...].astype(f32) + branch
    center = resid - row_mean(resid)
    rstd = lax.rsqrt(row_mean(center * center) + EPS)
    z1 = center * rstd
    z1_ref[...] = z1
    rstd_ref[...] = rstd
    n1 = z1 * (1.0 + vec_ref[3:4, :]) + vec_ref[4:5, :]
    n1b = n1.astype(bf16)
    n1_ref[...] = n1b

    @pl.when(step == 0)
    def _():
        for copy in copies_b:
            copy.wait()

    feed = None
    for j in range(4):
        h, lo = j // 2, (j % 2) * width
        u = mm(n1b, wa[h, :, half + lo : half + lo + width]) + vec_ref[8 + j : 9 + j, :]
        active, slope = gelu_parts(u)
        active = active.astype(bf16)
        g_ref[:, j * width : (j + 1) * width] = active
        slope_ref[:, j * width : (j + 1) * width] = slope.astype(bf16)
        part = mm_nt(active, wb[h, :, lo : lo + width])
        feed = part if feed is None else feed + part
    resid2 = n1 + feed + vec_ref[7:8, :]
    center2 = resid2 - row_mean(resid2)
    rstd2 = lax.rsqrt(row_mean(center2 * center2) + EPS)
    z2 = center2 * rstd2
    gain2 = 1.0 + vec_ref[5:6, :]
    out_ref[...] = (z2 * gain2 + vec_ref[6:7, :]).astype(bf16)
    dy = cot_ref[...].astype(f32)
    s = dy * gain2
    dr2 = rstd2 * (s - row_mean(s) - z2 * row_mean(s * z2))
    dr2_ref[...] = dr2
    df = dr2.astype(bf16)
    df_ref[...] = df
    sums_ref[0] += fold_rows(dy * z2)
    sums_ref[1] += fold_rows(dy)
    sums_ref[2] += fold_rows(df.astype(f32))


def feed_backward(n_a, n_b, info, vec_ref, df_ref, slope_ref, dr2_ref, z1_ref, rstd_ref, *refs):
    src_a = refs[:n_a]
    src_b = refs[n_a : n_a + n_b]
    (
        du_ref,
        dr1_ref,
        db_ref,
        da_ref,
        sums_ref,
        sums_b1_ref,
        wa,
        wb,
        sems_a,
        sems_b,
    ) = refs[n_a + n_b :]
    step = pl.program_id(0)
    width = df_ref.shape[1]
    half = width // 2
    copies_a = weight_copies(info, src_a, wa, sems_a)
    copies_b = weight_copies(info, src_b, wb, sems_b)

    @pl.when(step == 0)
    def _():
        for copy in copies_b + copies_a:
            copy.start()
        sums_ref[...] = jnp.zeros_like(sums_ref)
        sums_b1_ref[...] = jnp.zeros_like(sums_b1_ref)
        for copy in copies_b + copies_a:
            copy.wait()

    df = df_ref[...]
    dn1 = dr2_ref[...]
    for j in range(4):
        h, lo = j // 2, (j % 2) * width
        cut = slice(j * width, (j + 1) * width)
        d_active = mm(df, wb[h, :, lo : lo + width])
        du = (d_active * slope_ref[:, cut].astype(f32)).astype(bf16)
        du_ref[:, cut] = du
        sums_b1_ref[j] += fold_rows(du.astype(f32))
        dn1 = dn1 + mm_nt(du, wa[h, :, half + lo : half + lo + width])
    z1 = z1_ref[...]
    sums_ref[0] += fold_rows(dn1 * z1)
    sums_ref[1] += fold_rows(dn1)
    s = dn1 * (1.0 + vec_ref[3:4, :])
    dr1 = rstd_ref[...] * (s - row_mean(s) - z1 * row_mean(s * z1))
    dr1_ref[...] = dr1
    db = dr1.astype(bf16)
    db_ref[...] = db
    sums_ref[2] += fold_rows(db.astype(f32))
    da = mm_nt(db[:, :half], wa[0, :, :half]) + mm_nt(db[:, half:], wa[1, :, :half])
    da_ref[...] = da.astype(bf16)


def token_gradient(n_src, info, dqkv_ref, dr1_ref, *refs):
    src = refs[:n_src]
    out_ref, w, sems = refs[n_src:]
    used = dqkv_ref.shape[2]

    @pl.when(pl.program_id(0) == 0)
    def _():
        copies = weight_copies(info, src, w, sems)
        for copy in copies:
            copy.start()
        for copy in copies:
            copy.wait()

    out_ref[...] = (
        dr1_ref[...]
        + mm_nt(dqkv_ref[0], w[0, :, :used])
        + mm_nt(dqkv_ref[1], w[1, :, :used])
    )


def weight_gradient(starts, block, has_recv, n_out, ext_at, info, *refs):
    count = len(starts)
    lhs = refs[:count]
    rhs = refs[count : 2 * count]
    at = 2 * count
    recv = None
    ext = None
    if has_recv:
        recv = refs[at]
        at += 1
    if ext_at is not None:
        ext = refs[at]
        at += 1
    outs = refs[at : at + n_out]
    left, acc = refs[at + n_out :]
    step = pl.program_id(0)

    def store(value, lo, size):
        if n_out == 1:
            outs[0][:, pl.ds(lo, size)] = value.astype(outs[0].dtype)
            return
        acc[:, :size] = value
        for a in range(4):
            for k in range(4):
                row = chip_row(info, a, k, 1)
                mine = acc[pl.ds(row, 48), :size]
                theirs = recv[pl.ds(row, 48), pl.ds(lo, size)].astype(f32)
                outs[a][k, :, pl.ds(lo, size)] = (mine + theirs).astype(bf16)

    for number, start in enumerate(starts):
        stop = starts[number + 1] if number + 1 < count else None

        @pl.when(step == start)
        def _(number=number):
            left[...] = lhs[number][...].T

        here = step >= start
        if stop is not None:
            here = here & (step < stop)

        @pl.when(here)
        def _(number=number):
            right = rhs[number]
            right = right[0] if len(right.shape) == 3 else right[...]
            store(mm(left[...], right), pl.multiple_of(step * block, 128), block)

    if ext_at is not None:

        @pl.when(step == pl.num_programs(0) - 1)
        def _():
            store(ext[...].astype(f32), ext_at, EXT)


def params():
    return pltpu.CompilerParams(
        dimension_semantics=("arbitrary",), vmem_limit_bytes=VMEM_LIMIT
    )


def call(kernel, grid, in_specs, out_specs, out_shape, scratch, flops, nbytes, name):
    return pl.pallas_call(
        kernel,
        grid_spec=pltpu.PrefetchScalarGridSpec(
            num_scalar_prefetch=1,
            grid=grid,
            in_specs=in_specs,
            out_specs=out_specs,
            scratch_shapes=scratch,
        ),
        out_shape=out_shape,
        compiler_params=params(),
        cost_estimate=pl.CostEstimate(
            flops=int(flops), bytes_accessed=int(nbytes), transcendentals=0
        ),
        name=name,
    )


def struct(shape, dtype):
    return jax.ShapeDtypeStruct(shape, dtype)


def whole_block(shape):
    return pl.BlockSpec(shape, lambda i, info: (0,) * len(shape))


def rows_block(rows, columns):
    return pl.BlockSpec((rows, columns), lambda i, info: (i, 0))


def spread_tables(width):
    per = width // 64
    e = np.arange(width)
    spread = (np.arange(EXT)[:, None] == (e % per)[None, :]).astype(np.float32)
    pick = (np.arange(64)[:, None] == (e // per)[None, :]).astype(np.float32)
    return spread, pick


def run_attention_forward(info, x, pieces, vec, crops):
    rows, width = x.shape
    slots = rows // crops
    half = width // 2
    w_columns = pieces[0].shape[-1]
    has_ext = vec is None
    pairs = half // 128
    if has_ext:
        spread, pick = spread_tables(width)
        extra = [jnp.asarray(spread, bf16), jnp.asarray(pick, f32)]
    else:
        extra = [vec]
    extra_specs = [whole_block(e.shape) for e in extra]
    kernel = functools.partial(attention_forward, len(pieces), has_ext, pairs)
    return call(
        kernel,
        (crops,),
        [rows_block(slots, width)] + [ANY] * len(pieces) + extra_specs,
        [
            whole_block((16, width)),
            pl.BlockSpec((2, slots, 3 * half), lambda i, info: (0, i, 0)),
            pl.BlockSpec((2, 1, H // 2, slots, slots), lambda i, info: (0, i, 0, 0, 0)),
            rows_block(slots, width),
        ],
        [
            struct((16, width), f32),
            struct((2, rows, 3 * half), bf16),
            struct((2, crops, H // 2, slots, slots), bf16),
            struct((rows, width), bf16),
        ],
        [
            pltpu.VMEM((2, width, w_columns), bf16),
            pltpu.VMEM((2, 1, 3 * half), f32),
            pltpu.SemaphoreType.DMA((sem_count(pieces),)),
        ],
        2 * rows * width * 3 * width + 8 * rows * slots * width,
        30e6,
        "attention_forward",
    )(info, x, *pieces, *extra)


def run_attention_backward(info, qkv, da, probs, crops, which):
    _, rows, columns = qkv.shape
    slots = rows // crops
    half = columns // 3

    def pick(info):
        return info[0] if which else 1 - info[0]

    kernel = functools.partial(attention_backward, half // 128)
    return call(
        kernel,
        (crops,),
        [
            pl.BlockSpec((1, slots, columns), lambda i, info: (pick(info), i, 0)),
            pl.BlockSpec((slots, half), lambda i, info: (i, pick(info))),
            pl.BlockSpec(
                (1, 1, H // 2, slots, slots), lambda i, info: (pick(info), i, 0, 0, 0)
            ),
        ],
        [
            pl.BlockSpec((1, slots, columns), lambda i, info: (0, i, 0)),
            whole_block((8, columns)),
        ],
        [struct((1, rows, columns), bf16), struct((8, columns), f32)],
        [],
        16 * rows * slots * half,
        12e6,
        "attention_backward",
    )(info, qkv, da, probs)


def run_feed_forward(info, vec, x, attended, cot, pieces_a, pieces_b, block):
    rows, width = x.shape
    ff = 2 * pieces_b[0].shape[-1]
    kernel = functools.partial(feed_forward, len(pieces_a), len(pieces_b))
    return call(
        kernel,
        (rows // block,),
        [whole_block(vec.shape)]
        + [rows_block(block, width)] * 3
        + [ANY] * (len(pieces_a) + len(pieces_b)),
        [
            rows_block(block, width),
            rows_block(block, ff),
            rows_block(block, ff),
            rows_block(block, width),
            rows_block(block, width),
            rows_block(block, 1),
            rows_block(block, width),
            rows_block(block, width),
            whole_block((3, 8, width)),
        ],
        [
            struct((rows, width), bf16),
            struct((rows, ff), bf16),
            struct((rows, ff), bf16),
            struct((rows, width), bf16),
            struct((rows, width), f32),
            struct((rows, 1), f32),
            struct((rows, width), f32),
            struct((rows, width), bf16),
            struct((3, 8, width), f32),
        ],
        [
            pltpu.VMEM((2, width, pieces_a[0].shape[-1]), bf16),
            pltpu.VMEM((2, width, pieces_b[0].shape[-1]), bf16),
            pltpu.SemaphoreType.DMA((sem_count(pieces_a),)),
            pltpu.SemaphoreType.DMA((sem_count(pieces_b),)),
        ],
        2 * rows * width * (width + 2 * ff),
        45e6,
        "feed_forward",
    )(info, vec, x, attended, cot, *pieces_a, *pieces_b)


def run_feed_backward(info, vec, df, slope, dr2, z1, rstd, pieces_a, pieces_b, block):
    rows, width = df.shape
    ff = slope.shape[1]
    kernel = functools.partial(feed_backward, len(pieces_a), len(pieces_b))
    return call(
        kernel,
        (rows // block,),
        [
            whole_block(vec.shape),
            rows_block(block, width),
            rows_block(block, ff),
            rows_block(block, width),
            rows_block(block, width),
            rows_block(block, 1),
        ]
        + [ANY] * (len(pieces_a) + len(pieces_b)),
        [
            rows_block(block, ff),
            rows_block(block, width),
            rows_block(block, width),
            rows_block(block, width),
            whole_block((3, 8, width)),
            whole_block((4, 8, width)),
        ],
        [
            struct((rows, ff), bf16),
            struct((rows, width), f32),
            struct((rows, width), bf16),
            struct((rows, width), bf16),
            struct((3, 8, width), f32),
            struct((4, 8, width), f32),
        ],
        [
            pltpu.VMEM((2, width, pieces_a[0].shape[-1]), bf16),
            pltpu.VMEM((2, width, pieces_b[0].shape[-1]), bf16),
            pltpu.SemaphoreType.DMA((sem_count(pieces_a),)),
            pltpu.SemaphoreType.DMA((sem_count(pieces_b),)),
        ],
        2 * rows * width * (width + 2 * ff),
        45e6,
        "feed_backward",
    )(info, vec, df, slope, dr2, z1, rstd, *pieces_a, *pieces_b)


def run_token_gradient(info, dqkv, dr1, pieces, block):
    rows, width = dr1.shape
    columns = dqkv.shape[2]
    kernel = functools.partial(token_gradient, len(pieces))
    return call(
        kernel,
        (rows // block,),
        [
            pl.BlockSpec((2, block, columns), lambda i, info: (0, i, 0)),
            rows_block(block, width),
        ]
        + [ANY] * len(pieces),
        rows_block(block, width),
        struct((rows, width), f32),
        [
            pltpu.VMEM((2, width, pieces[0].shape[-1]), bf16),
            pltpu.SemaphoreType.DMA((sem_count(pieces),)),
        ],
        4 * rows * width * columns,
        20e6,
        "token_gradient",
    )(info, dqkv, dr1, *pieces)


def run_weight_gradient(info, pairs, columns, block, pick, recv, ext, full):
    rows, width = pairs[0][0].shape
    starts, step = [], 0
    rhs_specs = []
    for _, rhs, size in pairs:
        count = size // block
        starts.append(step)

        def place(i, info, step=step, count=count):
            return pick(info) * count + jnp.clip(i - step, 0, count - 1)

        if rhs.ndim == 3:
            rhs_specs.append(
                pl.BlockSpec(
                    (1, rows, block),
                    lambda i, info, step=step, count=count: (
                        0,
                        0,
                        jnp.clip(i - step, 0, count - 1),
                    ),
                )
            )
        else:
            rhs_specs.append(
                pl.BlockSpec((rows, block), lambda i, info, place=place: (0, place(i, info)))
            )
        step += count
    operands = [p[0] for p in pairs] + [p[1] for p in pairs]
    specs = [whole_block((rows, width)) for _ in pairs] + rhs_specs
    if recv is not None:
        operands.append(recv)
        specs.append(whole_block(recv.shape))
    if ext is not None:
        operands.append(ext)
        specs.append(whole_block(ext.shape))
    if recv is None:
        out_specs = [whole_block((width, columns))]
        out_shape = [struct((width, columns), f32 if full else bf16)]
    else:
        out_specs = [whole_block((4, 48, columns))] * 4
        out_shape = [struct((4, 48, columns), bf16)] * 4
    kernel = functools.partial(
        weight_gradient,
        tuple(starts),
        block,
        recv is not None,
        len(out_shape),
        None if ext is None else columns - EXT,
    )
    out = call(
        kernel,
        (step,),
        specs,
        out_specs,
        out_shape,
        [pltpu.VMEM((width, rows), bf16), pltpu.VMEM((width, block), f32)],
        2 * rows * width * columns,
        12e6,
        "weight_gradient",
    )(info, *operands)
    return out


def neighbours(n):
    flip = lambda bits: [(i, i ^ bits) for i in range(n)]
    shift = lambda k: [(i, (i + 8 * k) % n) for i in range(n)]
    return {"core": flip(1), "x": flip(2), "y": flip(4), "xy": flip(6)}, shift


def send(value, pairs):
    return lax.ppermute(value, "dp", pairs)


def gather_pieces(core, first, second, n):
    flips, shift = neighbours(n)
    keep = jnp.where(core == 0, first, second)
    give = jnp.where(core == 0, second, first)
    got = send(give, flips["core"])
    piece = jnp.where(
        core == 0, jnp.concatenate([keep, got]), jnp.concatenate([got, keep])
    )
    base = jnp.concatenate([piece] + [send(piece, shift(k)) for k in (1, 2, 3)])
    by_x, by_y = send(base, flips["x"]), send(base, flips["y"])
    mid = base.shape[0] // 2
    far = [send(by_x[:mid], flips["y"]), send(by_y[mid:], flips["x"])]
    own = [base, by_x, by_y] + far
    return own + [send(v, flips["core"]) for v in own]


def scatter_sum(core, parts, n):
    flips, shift = neighbours(n)
    own, to_x, to_y, to_xy = parts
    total = (
        own.astype(f32)
        + send(to_x, flips["x"]).astype(f32)
        + send(to_y, flips["y"]).astype(f32)
        + send(to_xy, flips["xy"]).astype(f32)
    )
    done = total[0]
    for k in (1, 2, 3):
        done = done + send(total[k].astype(bf16), shift(k)).astype(f32)
    rows = done.shape[0] // 2
    keep = jnp.where(core == 0, done[:rows], done[rows:])
    give = jnp.where(core == 0, done[rows:], done[:rows])
    got = send(give, flips["core"])
    return jnp.where(core == 0, keep, got), jnp.where(core == 0, got, keep)


def halves(matrix, groups):
    size = matrix.shape[1] // groups
    cut = size // 2
    return [
        jnp.concatenate(
            [matrix[:, g * size + h * cut : g * size + (h + 1) * cut] for g in range(groups)],
            axis=1,
        )
        for h in range(2)
    ]


def join(first, second, groups):
    cut = first.shape[1] // groups
    return jnp.concatenate(
        [v[:, g * cut : (g + 1) * cut] for g in range(groups) for v in (first, second)],
        axis=1,
    )


def momentum_step(weight, copy):
    return (weight.astype(f32) - copy) * 0.0005


def local(
    n,
    tokens,
    lengths,
    w_qkv,
    w_out,
    w_in,
    w_down,
    vector,
    key_qkv,
    key_out,
    key_in,
    key_down,
    key_vector,
    cotangent,
):
    width = tokens.shape[1]
    half = width // 2
    ff = w_in.shape[1]
    crops = lengths.shape[0]
    near = n == 32 and w_qkv.shape[0] == 24
    me = lax.axis_index("dp").astype(jnp.int32)
    core = me & 1
    place = jnp.stack([core, (me >> 1) & 1, (me >> 2) & 1, (me >> 3) & 3])
    info = jnp.concatenate([place, lengths.astype(jnp.int32)])

    qkv_halves = halves(w_qkv, 3)
    out_halves = halves(w_out, 1)
    in_halves = halves(w_in, 1)
    down_halves = halves(w_down, 1)
    mixed = [jnp.concatenate([out_halves[h], in_halves[h]], axis=1) for h in range(2)]
    if near:
        own_rows = w_qkv.shape[0]
        ext = jnp.pad(
            vector.reshape(own_rows, vector.shape[0] // own_rows),
            ((0, 0), (0, EXT - vector.shape[0] // own_rows)),
        )
        first = [jnp.concatenate([q, ext], axis=1) for q in qkv_halves]
        p_qkv = gather_pieces(core, first[0], first[1], n)
        p_mixed = gather_pieces(core, mixed[0], mixed[1], n)
        p_down = gather_pieces(core, down_halves[0], down_halves[1], n)
        vec = None
    else:
        everywhere = lambda pair: [
            lax.all_gather(jnp.stack(pair), "dp", axis=1, tiled=True)
        ]
        p_qkv, p_mixed, p_down = map(everywhere, (qkv_halves, mixed, down_halves))
        vec = lax.all_gather(vector, "dp", axis=0, tiled=True).astype(f32)
        vec = jnp.pad(vec.reshape(-1, width), ((0, 16 - vec.shape[0] // width), (0, 0)))

    vec, qkv, probs, attended = run_attention_forward(info, tokens, p_qkv, vec, crops)
    output, active, slope, n1, z1, rstd, dr2, df, sums_two = run_feed_forward(
        info, vec, tokens, attended, cotangent, p_mixed, p_down, 256
    )
    flips, _ = neighbours(n)
    other = lambda info: 1 - info[0]
    mine = lambda info: info[0]

    def gradient(pairs_of, columns, block, ext=(None, None)):
        if not near:
            return [
                run_weight_gradient(
                    info, pairs_of(h), columns, block, lambda info, h=h: h, None, None, True
                )[0]
                for h in range(2)
            ]
        away = run_weight_gradient(
            info, pairs_of(0), columns, block, other, None, ext[0], False
        )[0]
        got = send(away, flips["core"])
        parts = run_weight_gradient(
            info, pairs_of(1), columns, block, mine, got, ext[1], False
        )
        return scatter_sum(core, parts, n)

    g_down = gradient(lambda w: [(df, active, ff // 2)], ff // 2, 512)
    du, dr1, db, da, sums_one, sums_b1 = run_feed_backward(
        info, vec, df, slope, dr2, z1, rstd, p_mixed, p_down, 256
    )
    g_mixed = gradient(
        lambda w: [(attended, db, half), (n1, du, ff // 2)], half + ff // 2, half
    )
    if near:
        dqkv_other, sums_other = run_attention_backward(info, qkv, da, probs, crops, 0)
        dqkv_mine, sums_mine = run_attention_backward(info, qkv, da, probs, crops, 1)
        dqkv = jnp.where(
            core == 0,
            jnp.concatenate([dqkv_mine, dqkv_other]),
            jnp.concatenate([dqkv_other, dqkv_mine]),
        )
        sums_qkv = jnp.where(
            core == 0,
            jnp.stack([sums_mine, sums_other]),
            jnp.stack([sums_other, sums_mine]),
        )
        dqkv_by = [dqkv_other, dqkv_mine]
    else:
        info_of = lambda h: info.at[0].set(h)
        results = [
            run_attention_backward(info_of(h), qkv, da, probs, crops, 1) for h in range(2)
        ]
        dqkv_by = [r[0] for r in results]
        dqkv = jnp.concatenate(dqkv_by)
        sums_qkv = jnp.stack([r[1] for r in results])
    bias_sums = jnp.sum(sums_qkv, axis=1).reshape(2, 3, half)
    vec_grad = jnp.concatenate(
        [
            bias_sums[:, 0].reshape(-1),
            bias_sums[:, 2].reshape(-1),
            jnp.sum(sums_one[2], axis=0),
            jnp.sum(sums_one[0], axis=0),
            jnp.sum(sums_one[1], axis=0),
            jnp.sum(sums_two[0], axis=0),
            jnp.sum(sums_two[1], axis=0),
            jnp.sum(sums_two[2], axis=0),
            jnp.sum(sums_b1, axis=1).reshape(-1),
        ]
    )
    if near:
        per = vec_grad.shape[0] // width
        block = jnp.pad(vec_grad.reshape(width, per), ((0, 0), (0, EXT - per))).astype(bf16)
        g_qkv = gradient(
            lambda w: [(tokens, dqkv_by[w], 3 * half)], 3 * half + EXT, half, (block, block)
        )
        grad_vector = g_qkv[0][:, 3 * half : 3 * half + per].reshape(-1)
        g_qkv = [v[:, : 3 * half] for v in g_qkv]
    else:
        g_qkv = gradient(lambda w: [(tokens, dqkv_by[w], 3 * half)], 3 * half, half)
        grad_vector = lax.psum_scatter(vec_grad, "dp", scatter_dimension=0, tiled=True)
    grad_tokens = run_token_gradient(info, dqkv, dr1, p_qkv, 256)
    grad_qkv = join(g_qkv[0], g_qkv[1], 3)
    grad_out = join(g_mixed[0][:, :half], g_mixed[1][:, :half], 1)
    grad_in = join(g_mixed[0][:, half:], g_mixed[1][:, half:], 1)
    grad_down = join(g_down[0], g_down[1], 1)
    if not near:
        grad_qkv, grad_out, grad_in, grad_down = (
            lax.psum_scatter(g, "dp", scatter_dimension=0, tiled=True)
            for g in (grad_qkv, grad_out, grad_in, grad_down)
        )
    return (
        output,
        grad_tokens,
        grad_qkv,
        grad_out,
        grad_in,
        grad_down,
        grad_vector,
        momentum_step(w_qkv, key_qkv),
        momentum_step(w_out, key_out),
        momentum_step(w_in, key_in),
        momentum_step(w_down, key_down),
        momentum_step(vector, key_vector),
    )


def solution(mesh):
    n = mesh.shape["dp"]
    rows, flat = P("dp", None), P("dp")
    return jax.shard_map(
        functools.partial(local, n),
        mesh=mesh,
        in_specs=(rows, flat, rows, rows, rows, rows, flat, rows, rows, rows, rows, flat, rows),
        out_specs=(rows, rows, rows, rows, rows, rows, flat, rows, rows, rows, rows, flat),
        check_vma=False,
    )
```

time: 908 us -> 452 us (0.50)
  waiting for transfers between devices: 405 us -> 120 us
  matrix products: 219 us -> 0 us
  Pallas kernels: 0 us -> 214 us
  local copies, waits for them, and re-layouts: 132 us -> 21.1 us
  blocking collectives: 82.1 us -> 0 us
  starting transfers between devices: 0.32 us -> 64.7 us
  other arithmetic: 45.2 us -> 24.4 us
  between operations: 15.1 us -> 1.67 us
    reduce_scatter x3 -> x0, waiting for transfers between devices: 283 us -> none  [the longest x1 142 us: local(): lax.psum_scatter(local_in, 'dp', scatter_dimension=0, tiled=True)]
    dot_general x18 -> x0, matrix products: 219 us -> none  [the longest x1 49.2 us: local(): jnp.dot(normed_b, full_in, preferred_element_type=jnp.float32)]
    pallas_call x0 -> x12, Pallas kernels: none -> 214 us  [the longest x6 68.6 us: run_weight_gradient(): call(kernel, (step,), specs, out_specs, out_shape, [pltpu.VMEM((width, ro...]
    ppermute x0 -> x63, waiting for transfers between devices: none -> 120 us  [send(): return lax.ppermute(value, 'dp', pairs)]
    unnamed x9 -> x0, waiting for transfers between devices: 84.1 us -> none
    unnamed x2 -> x0, blocking collectives: 82.1 us -> none
    ppermute x0 -> x63, starting transfers between devices: none -> 64.7 us  [send(): return lax.ppermute(value, 'dp', pairs)]
    unnamed x117 -> x99, local copies, waits for them, and re-layouts: 69.8 us -> 11.1 us
  transfers between devices with their start and end apart: 8 -> 63, of which waited for: 6 -> 21; matrix products, arithmetic and copies ran while one was open for 29% -> 7% of each run, Pallas kernels for 0% -> 21%
where the time goes in v1:
time: 452 us; the launch traced here: 446 us
  Pallas kernels  214 us (47%)
  waiting for transfers between devices  120 us (27%)
  starting transfers between devices  64.7 us (14%)
  other arithmetic  24.4 us (5%)
  local copies, waits for them, and re-layouts  21.1 us (5%)
    ppermute x63, waiting for transfers between devices, send(): return lax.ppermute(value, 'dp', pairs)  120 us
    pallas_call x6, Pallas kernels, run_weight_gradient(): call(kernel, (step,), specs, out_specs, out_shape, [pltpu.VMEM((width, ro...  68.6 us
    ppermute x63, starting transfers between devices, send(): return lax.ppermute(value, 'dp', pairs)  64.7 us
    pallas_call x1, Pallas kernels, run_feed_forward(): call(kernel, (rows // block,), [whole_block(vec.shape)] + [rows_block(blo...  43.5 us
    pallas_call x1, Pallas kernels, run_feed_backward(): call(kernel, (rows // block,), [whole_block(vec.shape), rows_block(block,...  31.4 us
    pallas_call x1, Pallas kernels, run_attention_forward(): call(kernel, (crops,), [rows_block(slots, width)] + [ANY] * len(pieces) +...  30.5 us
    pallas_call x2, Pallas kernels, run_attention_backward(): call(kernel, (crops,), [pl.BlockSpec((1, slots, columns), lambda i, info:...  25.8 us
    pallas_call x1, Pallas kernels, run_token_gradient(): call(kernel, (rows // block,), [pl.BlockSpec((2, block, columns), lambda...  14.1 us
  transfers between devices with their start and end apart: 63, of which 21 were waited for; matrix products, arithmetic and copies ran while one was open for 7% of the time, Pallas kernels for 21%

profile of v1, /device:TPU:0, one launch (start us, length us, event | category | flops | bytes accessed | tf_op | source)
XLA Modules:
  0.0 446.0 jit_solution(3073591346024557488)
XLA Ops:
  6.1 2.6 collective-permute-start.1
  8.8 2.6 collective-permute-start.2
  15.1 2.0 collective-permute-start.29
  17.1 3.3 collective-permute-done.2
  21.9 1.6 collective-permute-start.4
  23.6 9.8 %collective-permute-start.15 = (bf16[48,1920]{1,0:T(8,128)(2,1)S(1)}, bf16[48,1920]{1,0:T(8,128)(2,1)S(1)}, u32[]{:S(2)}, u32[]{:S(2)}) collective-permute-start(bf16[48,1920]{1,0:T(8,128)(2,1)S(1)} %maximum_select_fusion.1), channel_id=1, source_target_pairs={{0,16},{1,17},{2,18},{3,19},{4,20},{5,21},{6,22},{7,23},{8,24},{9,... | collective-permute-start | bytes 552968 | tf_op jit(solution)/shard_map/ppermute | solution.py:699
  33.4 6.8 %collective-permute-done.28 = bf16[48,1536]{1,0:T(8,128)(2,1)S(1)} collective-permute-done((bf16[48,1536]{1,0:T(8,128)(2,1)S(1)}, bf16[48,1536]{1,0:T(8,128)(2,1)S(1)}, u32[]{:S(2)}, u32[]{:S(2)}) %collective-permute-start.28) | collective-permute-done | bytes 147488 | tf_op jit(solution)/shard_map/ppermute | solution.py:699
  41.4 1.5 collective-permute-start.5
  42.9 4.4 collective-permute-done.15
  48.8 1.8 collective-permute-done.16
  50.8 1.6 collective-permute-start.17
  52.3 1.5 collective-permute-start.18
  54.9 8.8 %collective-permute-done.30.refs_11_ = bf16[192,1536]{1,0:T(8,128)(2,1)} collective-permute-done((bf16[192,1536]{1,0:T(8,128)(2,1)S(1)}, bf16[192,1536]{1,0:T(8,128)(2,1)}, u32[]{:S(2)}, u32[]{:S(2)}) %collective-permute-start.30) | collective-permute-done | bytes 589856 | tf_op jit(solution)/shard_map/ppermute | solution.py:699
  63.6 1.5 collective-permute-start.6
  65.2 19.2 %collective-permute-done.31.refs_12_ = bf16[192,1536]{1,0:T(8,128)(2,1)S(1)} collective-permute-done((bf16[192,1536]{1,0:T(8,128)(2,1)S(1)}, bf16[192,1536]{1,0:T(8,128)(2,1)S(1)}, u32[]{:S(2)}, u32[]{:S(2)}) %collective-permute-start.31) | collective-permute-done | bytes 589856 | tf_op jit(solution)/shard_map/ppermute | solution.py:699
  86.3 1.6 collective-permute-done.6.refs_3_
  87.8 1.5 collective-permute-start.32
  92.8 1.7 collective-permute-done.7.refs_4_
  95.3 5.0 %collective-permute-done.33.refs_14_ = bf16[96,1536]{1,0:T(8,128)(2,1)} collective-permute-done((bf16[96,1536]{1,0:T(8,128)(2,1)S(1)}, bf16[96,1536]{1,0:T(8,128)(2,1)}, u32[]{:S(2)}, u32[]{:S(2)}) %collective-permute-start.33) | collective-permute-done | bytes 294944 | tf_op jit(solution)/shard_map/ppermute | solution.py:699
  100.3 1.5 collective-permute-start.19
  104.7 5.6 %collective-permute-done.19.refs_3_ = bf16[96,1920]{1,0:T(8,128)(2,1)S(1)} collective-permute-done((bf16[96,1920]{1,0:T(8,128)(2,1)S(1)}, bf16[96,1920]{1,0:T(8,128)(2,1)S(1)}, u32[]{:S(2)}, u32[]{:S(2)}) %collective-permute-start.19) | collective-permute-done | bytes 368672 | tf_op jit(solution)/shard_map/ppermute | solution.py:699
  114.3 30.5 %attention_forward.1 = (f32[16,768]{1,0:T(8,128)}, bf16[2,1536,1152]{2,1,0:T(8,128)(2,1)}, bf16[2,6,6,256,256]{4,3,2,1,0:T(8,128)(2,1)}, bf16[1536,768]{1,0:T(8,128)(2,1)}) custom-call(s32[10]{0:T(128)} %concatenate.64.info, bf16[1536,768]{1,0:T(8,128)(2,1)} %refs_0_.3, bf16[192,1280]{1,0:T(8,128)(2,1)} %copy-done.2, bf16[192,1280]{1,0:T(8,128)(2,1)} %copy-done.3, ...), custom_call_target="tpu_custom_call" | custom-call | flops 7851737088 | bytes 30000000 | tf_op jit(solution)/shard_map/attention_forward/pallas_call | solution.py:459
  146.5 43.5 %feed_forward.1 = (bf16[1536,768]{1,0:T(8,128)(2,1)}, bf16[1536,3072]{1,0:T(8,128)(2,1)}, bf16[1536,3072]{1,0:T(8,128)(2,1)}, bf16[1536,768]{1,0:T(8,128)(2,1)},...) custom-call(s32[10]{0:T(128)} %concatenate.64.info, ...), custom_call_target="tpu_custom_call" | custom-call | flops 16307453952 | bytes 45000000 | tf_op jit(solution)/shard_map/feed_forward/pallas_call | solution.py:521
  190.0 31.4 %feed_backward.1 = (bf16[1536,3072]{1,0:T(8,128)(2,1)}, f32[1536,768]{1,0:T(8,128)}, bf16[1536,768]{1,0:T(8,128)(2,1)}, bf16[1536,768]{1,0:T(8,128)(2,1)}, f32[3,8,768]{2,1,0:T(8,128)}, /*index=5*/f32[4,8,768]{2,1,0:T(8,128)}) custom-call(s32[10]{0:T(128)} %concatenate.64.info, f32[16,768]{1,0:T(8,128)} %get-tuple-element.47.vec_ref, ...), custom_call_target="tpu_custom_call" | custom-call | flops 16307453952 | bytes 45000000 | tf_op jit(solution)/shard_map/feed_backward/pallas_call | solution.py:565
  221.4 12.9 %attention_backward.2 = (bf16[1,1536,1152]{2,1,0:T(8,128)(2,1)}, f32[8,1152]{1,0:T(8,128)}) custom-call(s32[10]{0:T(128)} %concatenate.64.info, bf16[2,1536,1152]{2,1,0:T(8,128)(2,1)} %get-tuple-element.50.qkv_ref, bf16[1536,768]{1,0:T(8,128)(2,1)} %get-tuple-element.56.da_ref, bf16[2,6,6,256,256]{4,3,2,1,0:T(8,128)(2,1)} %get-tuple-element.57.p_ref), custom_call_target="tpu_custom_call" | custom-call | flops 2415919104 | bytes 12000000 | tf_op jit(solution)/shard_map/attention_backward/pallas_call | solution.py:495
  234.3 12.9 %attention_backward.3 = (bf16[1,1536,1152]{2,1,0:T(8,128)(2,1)}, f32[8,1152]{1,0:T(8,128)}) custom-call(s32[10]{0:T(128)} %concatenate.64.info, bf16[2,1536,1152]{2,1,0:T(8,128)(2,1)} %get-tuple-element.50.qkv_ref, bf16[1536,768]{1,0:T(8,128)(2,1)} %get-tuple-element.56.da_ref, bf16[2,6,6,256,256]{4,3,2,1,0:T(8,128)(2,1)} %get-tuple-element.57.p_ref), custom_call_target="tpu_custom_call" | custom-call | flops 2415919104 | bytes 12000000 | tf_op jit(solution)/shard_map/attention_backward/pallas_call | solution.py:495
  251.2 9.4 %weight_gradient.6 = bf16[768,1280]{1,0:T(8,128)(2,1)} custom-call(s32[10]{0:T(128)} %concatenate.64.info, bf16[1536,768]{1,0:T(8,128)(2,1)} %refs_0_.3, bf16[1,1536,1152]{2,1,0:T(8,128)(2,1)} %get-tuple-element.59.refs_1_, bf16[768,128]{1,0:T(8,128)(2,1)} %pad.10.refs_2_.refs_3_), custom_call_target="tpu_custom_call" | custom-call | flops 3019898880 | bytes 12000000 | tf_op jit(solution)/shard_map/weight_gradient/pallas_call | solution.py:678
  262.3 7.1 %maximum_select_fusion.dqkv_ref = bf16[2,1536,1152]{2,1,0:T(8,128)(2,1)} fusion(bf16[1,1536,1152]{2,1,0:T(8,128)(2,1)} %get-tuple-element.59.refs_1_, bf16[1,1536,1152]{2,1,0:T(8,128)(2,1)S(1)} %copy-done, pred[]{:T(512)S(6)} %eq.2), kind=kLoop, calls=%fused_computation | loop fusion | flops 10616832 | bytes 14155777 | tf_op jit(solution)/shard_map/jit(_where)/select_n | solution.py:846
  269.4 10.2 %weight_gradient.7 = (bf16[4,48,1280]{2,1,0:T(8,128)(2,1)}, bf16[4,48,1280]{2,1,0:T(8,128)(2,1)}, bf16[4,48,1280]{2,1,0:T(8,128)(2,1)}, bf16[4,48,1280]{2,1,0:T(8,128)(2,1)}) custom-call(s32[10]{0:T(128)} %concatenate.64.info, bf16[1536,768]{1,0:T(8,128)(2,1)} %refs_0_.3, bf16[1,1536,1152]{2,1,0:T(8,128)(2,1)} %get-tuple-element.58.refs_1_, ...), custom_call_target="tpu_custom_call" | custom-call | flops 3019898880 | bytes 12000000 | tf_op jit(solution)/shard_map/weight_gradient/pallas_call | solution.py:678
  280.6 2.5 collective-permute-start.42
  283.1 9.1 %weight_gradient.10 = bf16[768,1536]{1,0:T(8,128)(2,1)} custom-call(s32[10]{0:T(128)} %concatenate.64.info, bf16[1536,768]{1,0:T(8,128)(2,1)} %get-tuple-element.51.df_ref.refs_0_, bf16[1536,3072]{1,0:T(8,128)(2,1)} %get-tuple-element.77.refs_1_), custom_call_target="tpu_custom_call" | custom-call | flops 3623878656 | bytes 12000000 | tf_op jit(solution)/shard_map/weight_gradient/pallas_call | solution.py:678
  292.2 14.1 %weight_gradient.8 = bf16[768,1920]{1,0:T(8,128)(2,1)} custom-call(s32[10]{0:T(128)} %concatenate.64.info, bf16[1536,768]{1,0:T(8,128)(2,1)} %get-tuple-element.48.a_ref.refs_0_, bf16[1536,768]{1,0:T(8,128)(2,1)} %get-tuple-element.70.refs_1_, bf16[1536,768]{1,0:T(8,128)(2,1)} %get-tuple-element.71.refs_2_, bf16[1536,3072]{1,0:T(8,128)(2,1)} %get-tuple-element.72.refs_3_), custom_call_target="tpu_custom_call" | custom-call | flops 4529848320 | bytes 12000000 | tf_op jit(solution)/shard_map/weight_gradient/pallas_call | solution.py:678
  306.8 2.4 fusion.15
  309.2 2.1 collective-permute-start.43
  313.7 14.1 %token_gradient.1 = f32[1536,768]{1,0:T(8,128)} custom-call(s32[10]{0:T(128)} %concatenate.64.info, bf16[2,1536,1152]{2,1,0:T(8,128)(2,1)} %maximum_select_fusion.dqkv_ref, f32[1536,768]{1,0:T(8,128)} %get-tuple-element.60.dr1_ref, bf16[192,1280]{1,0:T(8,128)(2,1)} %copy-done.2, bf16[192,1280]{1,0:T(8,128)(2,1)} %copy-done.3, bf16[192,1280]{1,0:T(8,128)(2,1)} %copy-done.4, ...), custom_call_target="tpu_custom_call" | custom-call | flops 5435817984 | bytes 20000000 | tf_op jit(solution)/shard_map/token_gradient/pallas_call | solution.py:609
  329.0 10.3 %weight_gradient.11 = (bf16[4,48,1536]{2,1,0:T(8,128)(2,1)}, bf16[4,48,1536]{2,1,0:T(8,128)(2,1)}, bf16[4,48,1536]{2,1,0:T(8,128)(2,1)}, bf16[4,48,1536]{2,1,0:T(8,128)(2,1)}) custom-call(s32[10]{0:T(128)} %concatenate.64.info, bf16[1536,768]{1,0:T(8,128)(2,1)} %get-tuple-element.51.df_ref.refs_0_, bf16[1536,3072]{1,0:T(8,128)(2,1)} %get-tuple-element.77.refs_1_, ...), custom_call_target="tpu_custom_call" | custom-call | flops 3623878656 | bytes 12000000 | tf_op jit(solution)/shard_map/weight_gradient/pallas_call | solution.py:678
  349.4 6.2 %collective-permute-done.56 = bf16[4,48,1536]{2,1,0:T(8,128)(2,1)S(1)} collective-permute-done((bf16[4,48,1536]{2,1,0:T(8,128)(2,1)}, bf16[4,48,1536]{2,1,0:T(8,128)(2,1)S(1)}, u32[]{:S(2)}, u32[]{:S(2)}) %collective-permute-start.56) | collective-permute-done | bytes 589856 | tf_op jit(solution)/shard_map/ppermute | solution.py:699
  355.6 13.6 %collective-permute-done.57 = bf16[4,48,1536]{2,1,0:T(8,128)(2,1)} collective-permute-done((bf16[4,48,1536]{2,1,0:T(8,128)(2,1)}, bf16[4,48,1536]{2,1,0:T(8,128)(2,1)}, u32[]{:S(2)}, u32[]{:S(2)}) %collective-permute-start.57) | collective-permute-done | bytes 589856 | tf_op jit(solution)/shard_map/ppermute | solution.py:699
  369.2 2.7 fusion.13
  372.8 1.7 collective-permute-start.60
  375.9 1.7 copy-done.1
  377.6 15.6 %weight_gradient.9 = (bf16[4,48,1920]{2,1,0:T(8,128)(2,1)}, bf16[4,48,1920]{2,1,0:T(8,128)(2,1)}, bf16[4,48,1920]{2,1,0:T(8,128)(2,1)}, bf16[4,48,1920]{2,1,0:T(8,128)(2,1)}) custom-call(s32[10]{0:T(128)} %concatenate.64.info, bf16[1536,768]{1,0:T(8,128)(2,1)} %get-tuple-element.48.a_ref.refs_0_, bf16[1536,768]{1,0:T(8,128)(2,1)} %get-tuple-element.70.refs_1_, ...), custom_call_target="tpu_custom_call" | custom-call | flops 4529848320 | bytes 12000000 | tf_op jit(solution)/shard_map/weight_gradient/pallas_call | solution.py:678
  394.9 1.8 collective-permute-start.50
  397.8 15.0 %collective-permute-done.48 = bf16[4,48,1920]{2,1,0:T(8,128)(2,1)S(1)} collective-permute-done((bf16[4,48,1920]{2,1,0:T(8,128)(2,1)}, bf16[4,48,1920]{2,1,0:T(8,128)(2,1)S(1)}, u32[]{:S(2)}, u32[]{:S(2)}) %collective-permute-start.48) | collective-permute-done | bytes 737312 | tf_op jit(solution)/shard_map/ppermute | solution.py:699
  412.8 14.0 %collective-permute-done.49 = bf16[4,48,1920]{2,1,0:T(8,128)(2,1)S(1)} collective-permute-done((bf16[4,48,1920]{2,1,0:T(8,128)(2,1)}, bf16[4,48,1920]{2,1,0:T(8,128)(2,1)S(1)}, u32[]{:S(2)}, u32[]{:S(2)}) %collective-permute-start.49) | collective-permute-done | bytes 737312 | tf_op jit(solution)/shard_map/ppermute | solution.py:699
  430.1 2.8 collective-permute-start.53
  433.0 4.9 %collective-permute-done.51 = bf16[48,1920]{1,0:T(8,128)(2,1)S(1)} collective-permute-done((bf16[48,1920]{1,0:T(8,128)(2,1)S(1)}, bf16[48,1920]{1,0:T(8,128)(2,1)S(1)}, u32[]{:S(2)}, u32[]{:S(2)}) %collective-permute-start.51) | collective-permute-done | bytes 184352 | tf_op jit(solution)/shard_map/ppermute | solution.py:699
  437.8 4.8 %collective-permute-done.52 = bf16[48,1920]{1,0:T(8,128)(2,1)S(1)} collective-permute-done((bf16[48,1920]{1,0:T(8,128)(2,1)S(1)}, bf16[48,1920]{1,0:T(8,128)(2,1)S(1)}, u32[]{:S(2)}, u32[]{:S(2)}) %collective-permute-start.52) | collective-permute-done | bytes 184352 | tf_op jit(solution)/shard_map/ppermute | solution.py:699
  (253 shorter events, 61.2 us)
Async XLA Ops:
  8.8 11.6 %collective-permute-start.2 = (bf16[48,1280]{1,0:T(8,128)(2,1)S(1)}, bf16[48,1280]{1,0:T(8,128)(2,1)S(1)}, u32[]{:S(2)}, u32[]{:S(2)}) collective-permute-start(bf16[48,1280]{1,0:T(8,128)(2,1)S(1)} %maximum_select_fusion.3), channel_id=1, source_target_pairs={{0,16},{1,17},{2,18},{3,19},{4,20},{5,21},{6,22},{7,23},{8,24},{9,... | collective-permute-start | bytes 368648 | tf_op jit(solution)/shard_map/ppermute | solution.py:699
  11.4 10.5 %collective-permute-start.3 = (bf16[48,1280]{1,0:T(8,128)(2,1)S(1)}, bf16[48,1280]{1,0:T(8,128)(2,1)S(1)}, u32[]{:S(2)}, u32[]{:S(2)}) collective-permute-start(bf16[48,1280]{1,0:T(8,128)(2,1)S(1)} %maximum_select_fusion.3), channel_id=1, source_target_pairs={{0,24},{1,25},{2,26},{3,27},{4,28},{5,29},{6,30},{7,31},{8,0},{9,1... | collective-permute-start | bytes 368648 | tf_op jit(solution)/shard_map/ppermute | solution.py:699
  12.8 10.8 %collective-permute-start.27 = (bf16[48,1536]{1,0:T(8,128)(2,1)S(1)}, bf16[48,1536]{1,0:T(8,128)(2,1)S(1)}, u32[]{:S(2)}, u32[]{:S(2)}) collective-permute-start(bf16[48,1536]{1,0:T(8,128)(2,1)S(1)} %maximum_select_fusion.2), channel_id=1, source_target_pairs={{0,8},{1,9},{2,10},{3,11},{4,12},{5,13},{6,14},{7,15},{8,16},{9,17... | collective-permute-start | bytes 442376 | tf_op jit(solution)/shard_map/ppermute | solution.py:699
  13.5 26.7 %collective-permute-start.28 = (bf16[48,1536]{1,0:T(8,128)(2,1)S(1)}, bf16[48,1536]{1,0:T(8,128)(2,1)S(1)}, u32[]{:S(2)}, u32[]{:S(2)}) collective-permute-start(bf16[48,1536]{1,0:T(8,128)(2,1)S(1)} %maximum_select_fusion.2), channel_id=1, source_target_pairs={{0,16},{1,17},{2,18},{3,19},{4,20},{5,21},{6,22},{7,23},{8,24},{9,... | collective-permute-start | bytes 442376 | tf_op jit(solution)/shard_map/ppermute | solution.py:699
  15.1 26.3 %collective-permute-start.29 = (bf16[48,1536]{1,0:T(8,128)(2,1)S(1)}, bf16[48,1536]{1,0:T(8,128)(2,1)S(1)}, u32[]{:S(2)}, u32[]{:S(2)}) collective-permute-start(bf16[48,1536]{1,0:T(8,128)(2,1)S(1)} %maximum_select_fusion.2), channel_id=1, source_target_pairs={{0,24},{1,25},{2,26},{3,27},{4,28},{5,29},{6,30},{7,31},{8,0},{9,1... | collective-permute-start | bytes 442376 | tf_op jit(solution)/shard_map/ppermute | solution.py:699
  20.4 22.5 %collective-permute-start.14 = (bf16[48,1920]{1,0:T(8,128)(2,1)S(1)}, bf16[48,1920]{1,0:T(8,128)(2,1)S(1)}, u32[]{:S(2)}, u32[]{:S(2)}) collective-permute-start(bf16[48,1920]{1,0:T(8,128)(2,1)S(1)} %maximum_select_fusion.1), channel_id=1, source_target_pairs={{0,8},{1,9},{2,10},{3,11},{4,12},{5,13},{6,14},{7,15},{8,16},{9,17... | collective-permute-start | bytes 552968 | tf_op jit(solution)/shard_map/ppermute | solution.py:699
  21.9 30.4 %collective-permute-start.4 = (bf16[192,1280]{1,0:T(8,128)(2,1)S(1)}, bf16[192,1280]{1,0:T(8,128)(2,1)S(1)}, u32[]{:S(2)}, u32[]{:S(2)}) collective-permute-start(bf16[192,1280]{1,0:T(8,128)(2,1)S(1)} %pad_maximum_fusion.2.refs_0_), channel_id=1, source_target_pairs={{0,2},{1,3},{2,0},{3,1},{4,6},{5,7},{6,4},{7,5},{8,10},{9,11},{10,... | collective-permute-start | bytes 1474568 | tf_op jit(solution)/shard_map/ppermute | solution.py:699
  23.6 23.8 %collective-permute-start.15 = (bf16[48,1920]{1,0:T(8,128)(2,1)S(1)}, bf16[48,1920]{1,0:T(8,128)(2,1)S(1)}, u32[]{:S(2)}, u32[]{:S(2)}) collective-permute-start(bf16[48,1920]{1,0:T(8,128)(2,1)S(1)} %maximum_select_fusion.1), channel_id=1, source_target_pairs={{0,16},{1,17},{2,18},{3,19},{4,20},{5,21},{6,22},{7,23},{8,24},{9,... | collective-permute-start | bytes 552968 | tf_op jit(solution)/shard_map/ppermute | solution.py:699
  40.2 10.5 %collective-permute-start.16 = (bf16[48,1920]{1,0:T(8,128)(2,1)S(1)}, bf16[48,1920]{1,0:T(8,128)(2,1)S(1)}, u32[]{:S(2)}, u32[]{:S(2)}) collective-permute-start(bf16[48,1920]{1,0:T(8,128)(2,1)S(1)} %maximum_select_fusion.1), channel_id=1, source_target_pairs={{0,24},{1,25},{2,26},{3,27},{4,28},{5,29},{6,30},{7,31},{8,0},{9,1... | collective-permute-start | bytes 552968 | tf_op jit(solution)/shard_map/ppermute | solution.py:699
  41.4 12.5 %collective-permute-start.5 = (bf16[192,1280]{1,0:T(8,128)(2,1)S(1)}, bf16[192,1280]{1,0:T(8,128)(2,1)S(1)}, u32[]{:S(2)}, u32[]{:S(2)}) collective-permute-start(bf16[192,1280]{1,0:T(8,128)(2,1)S(1)} %pad_maximum_fusion.2.refs_0_), channel_id=1, source_target_pairs={{0,4},{1,5},{2,6},{3,7},{4,0},{5,1},{6,2},{7,3},{8,12},{9,13},{10,... | collective-permute-start | bytes 1474568 | tf_op jit(solution)/shard_map/ppermute | solution.py:699
  42.9 11.9 %collective-permute-start.8 = (bf16[192,1280]{1,0:T(8,128)(2,1)S(1)}, bf16[192,1280]{1,0:T(8,128)(2,1)S(1)}, u32[]{:S(2)}, u32[]{:S(2)}) collective-permute-start(bf16[192,1280]{1,0:T(8,128)(2,1)S(1)} %pad_maximum_fusion.2.refs_0_), channel_id=1, source_target_pairs={{0,1},{1,0},{2,3},{3,2},{4,5},{5,4},{6,7},{7,6},{8,9},{9,8},{10,11... | collective-permute-start | bytes 1474568 | tf_op jit(solution)/shard_map/ppermute | solution.py:699
  47.3 16.3 %collective-permute-start.30 = (bf16[192,1536]{1,0:T(8,128)(2,1)S(1)}, bf16[192,1536]{1,0:T(8,128)(2,1)}, u32[]{:S(2)}, u32[]{:S(2)}) collective-permute-start(bf16[192,1536]{1,0:T(8,128)(2,1)S(1)} %pad_maximum_fusion.1.refs_10_), channel_id=1, source_target_pairs={{0,2},{1,3},{2,0},{3,1},{4,6},{5,7},{6,4},{7,5},{8,10},{9,11},{10,... | collective-permute-start | bytes 1769480 | tf_op jit(solution)/shard_map/ppermute | solution.py:699
  50.8 38.6 %collective-permute-start.17 = (bf16[192,1920]{1,0:T(8,128)(2,1)S(1)}, bf16[192,1920]{1,0:T(8,128)(2,1)}, u32[]{:S(2)}, u32[]{:S(2)}) collective-permute-start(bf16[192,1920]{1,0:T(8,128)(2,1)S(1)} %pad_maximum_fusion.refs_0_), channel_id=1, source_target_pairs={{0,2},{1,3},{2,0},{3,1},{4,6},{5,7},{6,4},{7,5},{8,10},{9,11},{10,... | collective-permute-start | bytes 2211848 | tf_op jit(solution)/shard_map/ppermute | solution.py:699
  52.3 37.7 %collective-permute-start.18 = (bf16[192,1920]{1,0:T(8,128)(2,1)S(1)}, bf16[192,1920]{1,0:T(8,128)(2,1)}, u32[]{:S(2)}, u32[]{:S(2)}) collective-permute-start(bf16[192,1920]{1,0:T(8,128)(2,1)S(1)} %pad_maximum_fusion.refs_0_), channel_id=1, source_target_pairs={{0,4},{1,5},{2,6},{3,7},{4,0},{5,1},{6,2},{7,3},{8,12},{9,13},{10,... | collective-permute-start | bytes 2211848 | tf_op jit(solution)/shard_map/ppermute | solution.py:699
  53.8 30.5 %collective-permute-start.31 = (bf16[192,1536]{1,0:T(8,128)(2,1)S(1)}, bf16[192,1536]{1,0:T(8,128)(2,1)S(1)}, u32[]{:S(2)}, u32[]{:S(2)}) collective-permute-start(bf16[192,1536]{1,0:T(8,128)(2,1)S(1)} %pad_maximum_fusion.1.refs_10_), channel_id=1, source_target_pairs={{0,4},{1,5},{2,6},{3,7},{4,0},{5,1},{6,2},{7,3},{8,12},{9,13},{10,... | collective-permute-start | bytes 1769480 | tf_op jit(solution)/shard_map/ppermute | solution.py:699
  54.8 30.8 %collective-permute-start.34 = (bf16[192,1536]{1,0:T(8,128)(2,1)S(1)}, bf16[192,1536]{1,0:T(8,128)(2,1)S(1)}, u32[]{:S(2)}, u32[]{:S(2)}) collective-permute-start(bf16[192,1536]{1,0:T(8,128)(2,1)S(1)} %pad_maximum_fusion.1.refs_10_), channel_id=1, source_target_pairs={{0,1},{1,0},{2,3},{3,2},{4,5},{5,4},{6,7},{7,6},{8,9},{9,8},{10,11... | collective-permute-start | bytes 1769480 | tf_op jit(solution)/shard_map/ppermute | solution.py:699
  63.6 24.2 %collective-permute-start.6 = (bf16[96,1280]{1,0:T(8,128)(2,1)S(1)}, bf16[96,1280]{1,0:T(8,128)(2,1)S(1)}, u32[]{:S(2)}, u32[]{:S(2)}) collective-permute-start(bf16[96,1280]{1,0:T(8,128)(2,1)S(1)} %slice.245), channel_id=1, source_target_pairs={{0,4},{1,5},{2,6},{3,7},{4,0},{5,1},{6,2},{7,3},{8,12},{9,13},{10,... | collective-permute-start | bytes 737288 | tf_op jit(solution)/shard_map/ppermute | solution.py:699
  84.4 10.1 %collective-permute-start.21 = (bf16[192,1920]{1,0:T(8,128)(2,1)S(1)}, bf16[192,1920]{1,0:T(8,128)(2,1)S(1)}, u32[]{:S(2)}, u32[]{:S(2)}) collective-permute-start(bf16[192,1920]{1,0:T(8,128)(2,1)S(1)} %pad_maximum_fusion.refs_0_), channel_id=1, source_target_pairs={{0,1},{1,0},{2,3},{3,2},{4,5},{5,4},{6,7},{7,6},{8,9},{9,8},{10,11... | collective-permute-start | bytes 2211848 | tf_op jit(solution)/shard_map/ppermute | solution.py:699
  89.4 11.0 %collective-permute-start.33 = (bf16[96,1536]{1,0:T(8,128)(2,1)S(1)}, bf16[96,1536]{1,0:T(8,128)(2,1)}, u32[]{:S(2)}, u32[]{:S(2)}) collective-permute-start(bf16[96,1536]{1,0:T(8,128)(2,1)S(1)} %slice.250), channel_id=1, source_target_pairs={{0,2},{1,3},{2,0},{3,1},{4,6},{5,7},{6,4},{7,5},{8,10},{9,11},{10,... | collective-permute-start | bytes 884744 | tf_op jit(solution)/shard_map/ppermute | solution.py:699
  90.0 11.8 %collective-permute-start.11 = (bf16[96,1280]{1,0:T(8,128)(2,1)S(1)}, bf16[96,1280]{1,0:T(8,128)(2,1)S(1)}, u32[]{:S(2)}, u32[]{:S(2)}) collective-permute-start(bf16[96,1280]{1,0:T(8,128)(2,1)S(1)} %collective-permute-done.6.refs_3_), channel_id=1, source_target_pairs={{0,1},{1,0},{2,3},{3,2},{4,5},{5,4},{6,7},{7,6},{8,9},{9,8},{10,11... | collective-permute-start | bytes 737288 | tf_op jit(solution)/shard_map/ppermute | solution.py:699
  100.3 10.0 %collective-permute-start.19 = (bf16[96,1920]{1,0:T(8,128)(2,1)S(1)}, bf16[96,1920]{1,0:T(8,128)(2,1)S(1)}, u32[]{:S(2)}, u32[]{:S(2)}) collective-permute-start(bf16[96,1920]{1,0:T(8,128)(2,1)S(1)} %slice.247), channel_id=1, source_target_pairs={{0,4},{1,5},{2,6},{3,7},{4,0},{5,1},{6,2},{7,3},{8,12},{9,13},{10,... | collective-permute-start | bytes 1105928 | tf_op jit(solution)/shard_map/ppermute | solution.py:699
  103.2 11.1 %collective-permute-start.35 = (bf16[192,1536]{1,0:T(8,128)(2,1)}, bf16[192,1536]{1,0:T(8,128)(2,1)}, u32[]{:S(2)}, u32[]{:S(2)}) collective-permute-start(bf16[192,1536]{1,0:T(8,128)(2,1)} %collective-permute-done.30.refs_11_), channel_id=1, source_target_pairs={{0,1},{1,0},{2,3},{3,2},{4,5},{5,4},{6,7},{7,6},{8,9},{9,8},{10,11... | collective-permute-start | bytes 1769480 | tf_op jit(solution)/shard_map/ppermute | solution.py:699
  103.3 41.6 %collective-permute-start.22 = (bf16[192,1920]{1,0:T(8,128)(2,1)}, bf16[192,1920]{1,0:T(8,128)(2,1)S(1)}, u32[]{:S(2)}, u32[]{:S(2)}) collective-permute-start(bf16[192,1920]{1,0:T(8,128)(2,1)} %collective-permute-done.17.refs_1_), channel_id=1, source_target_pairs={{0,1},{1,0},{2,3},{3,2},{4,5},{5,4},{6,7},{7,6},{8,9},{9,8},{10,11... | collective-permute-start | bytes 2211848 | tf_op jit(solution)/shard_map/ppermute | solution.py:699
  104.6 40.4 %collective-permute-start.23 = (bf16[192,1920]{1,0:T(8,128)(2,1)}, bf16[192,1920]{1,0:T(8,128)(2,1)S(1)}, u32[]{:S(2)}, u32[]{:S(2)}) collective-permute-start(bf16[192,1920]{1,0:T(8,128)(2,1)} %collective-permute-done.18.refs_2_), channel_id=1, source_target_pairs={{0,1},{1,0},{2,3},{3,2},{4,5},{5,4},{6,7},{7,6},{8,9},{9,8},{10,11... | collective-permute-start | bytes 2211848 | tf_op jit(solution)/shard_map/ppermute | solution.py:699
  113.7 31.2 %collective-permute-start.36 = (bf16[192,1536]{1,0:T(8,128)(2,1)}, bf16[192,1536]{1,0:T(8,128)(2,1)S(1)}, u32[]{:S(2)}, u32[]{:S(2)}) collective-permute-start(bf16[192,1536]{1,0:T(8,128)(2,1)} %copy-done.22), channel_id=1, source_target_pairs={{0,1},{1,0},{2,3},{3,2},{4,5},{5,4},{6,7},{7,6},{8,9},{9,8},{10,11... | collective-permute-start | bytes 1769480 | tf_op jit(solution)/shard_map/ppermute | solution.py:699
  113.7 31.2 %collective-permute-start.24 = (bf16[96,1920]{1,0:T(8,128)(2,1)}, bf16[96,1920]{1,0:T(8,128)(2,1)S(1)}, u32[]{:S(2)}, u32[]{:S(2)}) collective-permute-start(bf16[96,1920]{1,0:T(8,128)(2,1)} %copy-done.38), channel_id=1, source_target_pairs={{0,1},{1,0},{2,3},{3,2},{4,5},{5,4},{6,7},{7,6},{8,9},{9,8},{10,11... | collective-permute-start | bytes 1105928 | tf_op jit(solution)/shard_map/ppermute | solution.py:699
  114.3 30.7 %collective-permute-start.25 = (bf16[96,1920]{1,0:T(8,128)(2,1)}, bf16[96,1920]{1,0:T(8,128)(2,1)S(1)}, u32[]{:S(2)}, u32[]{:S(2)}) collective-permute-start(bf16[96,1920]{1,0:T(8,128)(2,1)} %copy-done.39), channel_id=1, source_target_pairs={{0,1},{1,0},{2,3},{3,2},{4,5},{5,4},{6,7},{7,6},{8,9},{9,8},{10,11... | collective-permute-start | bytes 1105928 | tf_op jit(solution)/shard_map/ppermute | solution.py:699
  279.6 27.2 %collective-permute-start.40 = (bf16[4,48,1280]{2,1,0:T(8,128)(2,1)}, bf16[4,48,1280]{2,1,0:T(8,128)(2,1)S(1)}, u32[]{:S(2)}, u32[]{:S(2)}) collective-permute-start(bf16[4,48,1280]{2,1,0:T(8,128)(2,1)} %get-tuple-element.67), channel_id=1, source_target_pairs={{0,2},{1,3},{2,0},{3,1},{4,6},{5,7},{6,4},{7,5},{8,10},{9,11},{10,... | collective-permute-start | bytes 1474568 | tf_op jit(solution)/shard_map/ppermute | solution.py:699
  280.1 26.6 %collective-permute-start.41 = (bf16[4,48,1280]{2,1,0:T(8,128)(2,1)}, bf16[4,48,1280]{2,1,0:T(8,128)(2,1)}, u32[]{:S(2)}, u32[]{:S(2)}) collective-permute-start(bf16[4,48,1280]{2,1,0:T(8,128)(2,1)} %get-tuple-element.68), channel_id=1, source_target_pairs={{0,4},{1,5},{2,6},{3,7},{4,0},{5,1},{6,2},{7,3},{8,12},{9,13},{10,... | collective-permute-start | bytes 1474568 | tf_op jit(solution)/shard_map/ppermute | solution.py:699
  280.6 26.1 %collective-permute-start.42 = (bf16[4,48,1280]{2,1,0:T(8,128)(2,1)}, bf16[4,48,1280]{2,1,0:T(8,128)(2,1)}, u32[]{:S(2)}, u32[]{:S(2)}) collective-permute-start(bf16[4,48,1280]{2,1,0:T(8,128)(2,1)} %get-tuple-element.69), channel_id=1, source_target_pairs={{0,6},{1,7},{2,4},{3,5},{4,2},{5,3},{6,0},{7,1},{8,14},{9,15},{10,... | collective-permute-start | bytes 1474568 | tf_op jit(solution)/shard_map/ppermute | solution.py:699
  292.2 36.8 %collective-permute-start.55 = (bf16[768,1536]{1,0:T(8,128)(2,1)}, bf16[768,1536]{1,0:T(8,128)(2,1)}, u32[]{:S(2)}, u32[]{:S(2)}) collective-permute-start(bf16[768,1536]{1,0:T(8,128)(2,1)} %weight_gradient.10), channel_id=1, source_target_pairs={{0,1},{1,0},{2,3},{3,2},{4,5},{5,4},{6,7},{7,6},{8,9},{9,8},{10,11... | collective-permute-start | bytes 7077896 | tf_op jit(solution)/shard_map/ppermute | solution.py:699
  306.3 69.6 %collective-permute-start.47 = (bf16[768,1920]{1,0:T(8,128)(2,1)}, bf16[768,1920]{1,0:T(8,128)(2,1)S(1)}, u32[]{:S(2)}, u32[]{:S(2)}) collective-permute-start(bf16[768,1920]{1,0:T(8,128)(2,1)} %weight_gradient.8), channel_id=1, source_target_pairs={{0,1},{1,0},{2,3},{3,2},{4,5},{5,4},{6,7},{7,6},{8,9},{9,8},{10,11... | collective-permute-start | bytes 8847368 | tf_op jit(solution)/shard_map/ppermute | solution.py:699
  309.2 18.7 %collective-permute-start.43 = (bf16[48,1280]{1,0:T(8,128)(2,1)S(1)}, bf16[48,1280]{1,0:T(8,128)(2,1)S(1)}, u32[]{:S(2)}, u32[]{:S(2)}) collective-permute-start(bf16[48,1280]{1,0:T(8,128)(2,1)S(1)} %get-tuple-element.104), channel_id=1, source_target_pairs={{0,8},{1,9},{2,10},{3,11},{4,12},{5,13},{6,14},{7,15},{8,16},{9,17... | collective-permute-start | bytes 368648 | tf_op jit(solution)/shard_map/ppermute | solution.py:699
  311.3 16.6 %collective-permute-start.44 = (bf16[48,1280]{1,0:T(8,128)(2,1)S(1)}, bf16[48,1280]{1,0:T(8,128)(2,1)S(1)}, u32[]{:S(2)}, u32[]{:S(2)}) collective-permute-start(bf16[48,1280]{1,0:T(8,128)(2,1)S(1)} %get-tuple-element.106), channel_id=1, source_target_pairs={{0,16},{1,17},{2,18},{3,19},{4,20},{5,21},{6,22},{7,23},{8,24},{9,... | collective-permute-start | bytes 368648 | tf_op jit(solution)/shard_map/ppermute | solution.py:699
  312.5 15.4 %collective-permute-start.45 = (bf16[48,1280]{1,0:T(8,128)(2,1)S(1)}, bf16[48,1280]{1,0:T(8,128)(2,1)S(1)}, u32[]{:S(2)}, u32[]{:S(2)}) collective-permute-start(bf16[48,1280]{1,0:T(8,128)(2,1)S(1)} %get-tuple-element.105), channel_id=1, source_target_pairs={{0,24},{1,25},{2,26},{3,27},{4,28},{5,29},{6,30},{7,31},{8,0},{9,1... | collective-permute-start | bytes 368648 | tf_op jit(solution)/shard_map/ppermute | solution.py:699
  328.9 13.9 %collective-permute-start.46 = (f32[24,1280]{1,0:T(8,128)S(1)}, f32[24,1280]{1,0:T(8,128)S(1)}, u32[]{:S(2)}, u32[]{:S(2)}) collective-permute-start(f32[24,1280]{1,0:T(8,128)S(1)} %slice_select_fusion.4), channel_id=1, source_target_pairs={{0,1},{1,0},{2,3},{3,2},{4,5},{5,4},{6,7},{7,6},{8,9},{9,8},{10,11... | collective-permute-start | bytes 368648 | tf_op jit(solution)/shard_map/ppermute | solution.py:699
  339.3 16.3 %collective-permute-start.56 = (bf16[4,48,1536]{2,1,0:T(8,128)(2,1)}, bf16[4,48,1536]{2,1,0:T(8,128)(2,1)S(1)}, u32[]{:S(2)}, u32[]{:S(2)}) collective-permute-start(bf16[4,48,1536]{2,1,0:T(8,128)(2,1)} %get-tuple-element.79), channel_id=1, source_target_pairs={{0,2},{1,3},{2,0},{3,1},{4,6},{5,7},{6,4},{7,5},{8,10},{9,11},{10,... | collective-permute-start | bytes 1769480 | tf_op jit(solution)/shard_map/ppermute | solution.py:699
  340.8 28.4 %collective-permute-start.57 = (bf16[4,48,1536]{2,1,0:T(8,128)(2,1)}, bf16[4,48,1536]{2,1,0:T(8,128)(2,1)}, u32[]{:S(2)}, u32[]{:S(2)}) collective-permute-start(bf16[4,48,1536]{2,1,0:T(8,128)(2,1)} %get-tuple-element.80), channel_id=1, source_target_pairs={{0,4},{1,5},{2,6},{3,7},{4,0},{5,1},{6,2},{7,3},{8,12},{9,13},{10,... | collective-permute-start | bytes 1769480 | tf_op jit(solution)/shard_map/ppermute | solution.py:699
  341.3 27.9 %collective-permute-start.58 = (bf16[4,48,1536]{2,1,0:T(8,128)(2,1)}, bf16[4,48,1536]{2,1,0:T(8,128)(2,1)}, u32[]{:S(2)}, u32[]{:S(2)}) collective-permute-start(bf16[4,48,1536]{2,1,0:T(8,128)(2,1)} %get-tuple-element.81), channel_id=1, source_target_pairs={{0,6},{1,7},{2,4},{3,5},{4,2},{5,3},{6,0},{7,1},{8,14},{9,15},{10,... | collective-permute-start | bytes 1769480 | tf_op jit(solution)/shard_map/ppermute | solution.py:699
  372.0 22.9 %collective-permute-start.59 = (bf16[48,1536]{1,0:T(8,128)(2,1)S(1)}, bf16[48,1536]{1,0:T(8,128)(2,1)S(1)}, u32[]{:S(2)}, u32[]{:S(2)}) collective-permute-start(bf16[48,1536]{1,0:T(8,128)(2,1)S(1)} %get-tuple-element.99), channel_id=1, source_target_pairs={{0,8},{1,9},{2,10},{3,11},{4,12},{5,13},{6,14},{7,15},{8,16},{9,17... | collective-permute-start | bytes 442376 | tf_op jit(solution)/shard_map/ppermute | solution.py:699
  372.8 23.8 %collective-permute-start.60 = (bf16[48,1536]{1,0:T(8,128)(2,1)S(1)}, bf16[48,1536]{1,0:T(8,128)(2,1)S(1)}, u32[]{:S(2)}, u32[]{:S(2)}) collective-permute-start(bf16[48,1536]{1,0:T(8,128)(2,1)S(1)} %get-tuple-element.101), channel_id=1, source_target_pairs={{0,16},{1,17},{2,18},{3,19},{4,20},{5,21},{6,22},{7,23},{8,24},{9,... | collective-permute-start | bytes 442376 | tf_op jit(solution)/shard_map/ppermute | solution.py:699
  374.6 22.1 %collective-permute-start.61 = (bf16[48,1536]{1,0:T(8,128)(2,1)S(1)}, bf16[48,1536]{1,0:T(8,128)(2,1)S(1)}, u32[]{:S(2)}, u32[]{:S(2)}) collective-permute-start(bf16[48,1536]{1,0:T(8,128)(2,1)S(1)} %get-tuple-element.100), channel_id=1, source_target_pairs={{0,24},{1,25},{2,26},{3,27},{4,28},{5,29},{6,30},{7,31},{8,0},{9,1... | collective-permute-start | bytes 442376 | tf_op jit(solution)/shard_map/ppermute | solution.py:699
  393.2 19.6 %collective-permute-start.48 = (bf16[4,48,1920]{2,1,0:T(8,128)(2,1)}, bf16[4,48,1920]{2,1,0:T(8,128)(2,1)S(1)}, u32[]{:S(2)}, u32[]{:S(2)}) collective-permute-start(bf16[4,48,1920]{2,1,0:T(8,128)(2,1)} %get-tuple-element.74), channel_id=1, source_target_pairs={{0,2},{1,3},{2,0},{3,1},{4,6},{5,7},{6,4},{7,5},{8,10},{9,11},{10,... | collective-permute-start | bytes 2211848 | tf_op jit(solution)/shard_map/ppermute | solution.py:699
  394.1 32.7 %collective-permute-start.49 = (bf16[4,48,1920]{2,1,0:T(8,128)(2,1)}, bf16[4,48,1920]{2,1,0:T(8,128)(2,1)S(1)}, u32[]{:S(2)}, u32[]{:S(2)}) collective-permute-start(bf16[4,48,1920]{2,1,0:T(8,128)(2,1)} %get-tuple-element.75), channel_id=1, source_target_pairs={{0,4},{1,5},{2,6},{3,7},{4,0},{5,1},{6,2},{7,3},{8,12},{9,13},{10,... | collective-permute-start | bytes 2211848 | tf_op jit(solution)/shard_map/ppermute | solution.py:699
  394.9 31.9 %collective-permute-start.50 = (bf16[4,48,1920]{2,1,0:T(8,128)(2,1)}, bf16[4,48,1920]{2,1,0:T(8,128)(2,1)S(1)}, u32[]{:S(2)}, u32[]{:S(2)}) collective-permute-start(bf16[4,48,1920]{2,1,0:T(8,128)(2,1)} %get-tuple-element.76), channel_id=1, source_target_pairs={{0,6},{1,7},{2,4},{3,5},{4,2},{5,3},{6,0},{7,1},{8,14},{9,15},{10,... | collective-permute-start | bytes 2211848 | tf_op jit(solution)/shard_map/ppermute | solution.py:699
  397.7 35.2 %collective-permute-start.62 = (f32[24,1536]{1,0:T(8,128)S(1)}, f32[24,1536]{1,0:T(8,128)S(1)}, u32[]{:S(2)}, u32[]{:S(2)}) collective-permute-start(f32[24,1536]{1,0:T(8,128)S(1)} %slice_select_fusion.2), channel_id=1, source_target_pairs={{0,1},{1,0},{2,3},{3,2},{4,5},{5,4},{6,7},{7,6},{8,9},{9,8},{10,11... | collective-permute-start | bytes 442376 | tf_op jit(solution)/shard_map/ppermute | solution.py:699
  428.8 13.8 %collective-permute-start.52 = (bf16[48,1920]{1,0:T(8,128)(2,1)S(1)}, bf16[48,1920]{1,0:T(8,128)(2,1)S(1)}, u32[]{:S(2)}, u32[]{:S(2)}) collective-permute-start(bf16[48,1920]{1,0:T(8,128)(2,1)S(1)} %get-tuple-element.98), channel_id=1, source_target_pairs={{0,16},{1,17},{2,18},{3,19},{4,20},{5,21},{6,22},{7,23},{8,24},{9,... | collective-permute-start | bytes 552968 | tf_op jit(solution)/shard_map/ppermute | solution.py:699
  430.1 12.5 %collective-permute-start.53 = (bf16[48,1920]{1,0:T(8,128)(2,1)S(1)}, bf16[48,1920]{1,0:T(8,128)(2,1)S(1)}, u32[]{:S(2)}, u32[]{:S(2)}) collective-permute-start(bf16[48,1920]{1,0:T(8,128)(2,1)S(1)} %get-tuple-element.97), channel_id=1, source_target_pairs={{0,24},{1,25},{2,26},{3,27},{4,28},{5,29},{6,30},{7,31},{8,0},{9,1... | collective-permute-start | bytes 552968 | tf_op jit(solution)/shard_map/ppermute | solution.py:699
  (58 other events, 1129.2 us)

commit v2 on v1

v2 whole, which is shorter than its diff:
```python
import functools

import jax
import jax.numpy as jnp
import numpy as np
from jax import lax
from jax.experimental import pallas as pl
from jax.experimental.pallas import tpu as pltpu
from jax.sharding import PartitionSpec as P

H = 12
EPS = 1e-12
EXT = 128
bf16 = jnp.bfloat16
f32 = jnp.float32
VMEM_LIMIT = 60 * 1024 * 1024
COST = 0.001
ANY = pl.BlockSpec(memory_space=pl.ANY)

NT = (((1,), (1,)), ((), ()))
TN = (((0,), (0,)), ((), ()))


def mm(a, b):
    return jnp.dot(a, b, preferred_element_type=f32)


def mm_nt(a, b):
    return lax.dot_general(a, b, NT, preferred_element_type=f32)


def mm_tn(a, b):
    return lax.dot_general(a, b, TN, preferred_element_type=f32)


def row_mean(v):
    return jnp.mean(v, axis=-1, keepdims=True)


def fold_rows(v):
    return jnp.sum(v.reshape(v.shape[0] // 8, 8, v.shape[1]), axis=0)


def chip_row(info, a, k, flip):
    x, y, z = info[1], info[2], info[3]
    xx = x ^ (a & 1)
    yy = y ^ (a >> 1)
    zz = z ^ k if flip else (z - k + 4) & 3
    return pl.multiple_of(((zz * 2 + yy) * 2 + xx) * 48, 16)


def weight_copies(info, refs, w, sems):
    if len(refs) == 1:
        return [pltpu.make_async_copy(refs[0], w, sems.at[0])]
    out = []
    per = len(refs) // 2
    far = [[(3, 0), (3, 1)], [(3, 2), (3, 3)]] if per == 5 else [[(3, k) for k in range(4)]]
    places = [[(a, k) for k in range(4)] for a in range(3)] + far
    for source in range(2):
        half = info[0] if source == 0 else 1 - info[0]
        for number, slots in enumerate(places):
            ref = refs[source * per + number]
            for j, (a, k) in enumerate(slots):
                row = chip_row(info, a, k, False)
                out.append(
                    pltpu.make_async_copy(
                        ref.at[pl.ds(48 * j, 48)],
                        w.at[half, pl.ds(row, 48)],
                        sems.at[len(out)],
                    )
                )
    return out


def sem_count(pieces):
    return 1 if len(pieces) == 1 else 32


def attention_forward(n_src, has_ext, pairs, info, x_ref, *refs):
    src = refs[:n_src]
    if has_ext:
        spread_ref, pick_ref = refs[n_src : n_src + 2]
        refs = refs[n_src + 2 :]
    else:
        vec_in = refs[n_src]
        refs = refs[n_src + 1 :]
    vec_ref, qkv_ref, p_ref, a_ref, w, bias, sems = refs
    crop = pl.program_id(0)
    half_width = pairs * 128

    @pl.when(crop == 0)
    def _():
        copies = weight_copies(info, src, w, sems)
        for copy in copies:
            copy.start()
        for copy in copies:
            copy.wait()
        if has_ext:
            spread = mm(w[0, :, 3 * half_width :], spread_ref[...])
            groups = spread.shape[0] // 64
            picked = spread.reshape(groups, 64, spread.shape[1]) * pick_ref[...][None]
            vec_ref[0:groups, :] = jnp.sum(picked, axis=1)
        else:
            vec_ref[...] = vec_in[...]
        for h in range(2):
            for part, row in ((0, 0), (2, 1)):
                bias[h, :, part * half_width : (part + 1) * half_width] = vec_ref[
                    row : row + 1, h * half_width : (h + 1) * half_width
                ]
            bias[h, :, half_width : 2 * half_width] = jnp.zeros((1, half_width), f32)

    x = x_ref[...]
    slots = x.shape[0]
    length = info[4 + crop]
    usable = lax.broadcasted_iota(jnp.int32, (1, slots), 1) < length
    mask_row = jnp.where(usable, 0.0, -1e30).astype(f32)
    lane = lax.broadcasted_iota(jnp.int32, (1, 128), 1)
    sides = (
        jnp.where(lane < 64, 1.0, 0.0).astype(bf16),
        jnp.where(lane < 64, 0.0, 1.0).astype(bf16),
    )
    units = [(h, p, side) for h in range(2) for p in range(pairs) for side in range(2)]

    def project(h):
        qkv_ref[h] = (mm(x, w[h, :, : 3 * half_width]) + bias[h]).astype(bf16)

    def columns(h, part, p):
        lo = part * half_width + p * 128
        return qkv_ref[h, :, lo : lo + 128]

    scores, probs, first = {}, {}, None
    project(0)
    for t in range(len(units) + 4):
        if t == 3:
            project(1)
        if t < len(units):
            h, p, side = units[t]
            q2 = columns(h, 0, p) * jnp.asarray(0.125, bf16)
            scores[t] = mm_nt(q2, columns(h, 1, p) * sides[side]) + mask_row
        if 0 <= t - 3 < len(units):
            h, p, side = units[t - 3]
            value = scores.pop(t - 3)
            terms = jnp.exp(value - jnp.max(value, axis=1, keepdims=True))
            mass = jnp.sum(terms, axis=1, keepdims=True)
            rounded = (terms * (1.0 / mass)).astype(bf16)
            p_ref[h, 0, p * 2 + side] = rounded
            probs[t - 3] = rounded
        if 0 <= t - 4 < len(units):
            h, p, side = units[t - 4]
            part = mm(probs.pop(t - 4), columns(h, 2, p) * sides[side])
            if side == 0:
                first = part
            else:
                lo = h * half_width + p * 128
                a_ref[:, lo : lo + 128] = (first + part).astype(bf16)


def attention_backward(pairs, info, qkv_ref, da_ref, p_ref, out_ref, sums_ref):
    half_width = pairs * 128
    lane = lax.broadcasted_iota(jnp.int32, (1, 128), 1)
    sides = (
        jnp.where(lane < 64, 1.0, 0.0).astype(bf16),
        jnp.where(lane < 64, 0.0, 1.0).astype(bf16),
    )

    @pl.when(pl.program_id(0) == 0)
    def _():
        sums_ref[...] = jnp.zeros_like(sums_ref)

    units = [(p, side) for p in range(pairs) for side in range(2)]

    def columns(part, p):
        lo = part * half_width + p * 128
        return qkv_ref[0, :, lo : lo + 128]

    d_probs, d_scores, total = {}, {}, None
    for t in range(len(units) + 4):
        if t < len(units):
            p, side = units[t]
            da2 = da_ref[:, p * 128 : (p + 1) * 128]
            d_probs[t] = mm_nt(da2, columns(2, p) * sides[side])
        if 0 <= t - 2 < len(units):
            p, side = units[t - 2]
            probs = p_ref[0, 0, p * 2 + side].astype(f32)
            value = d_probs.pop(t - 2)
            inner = jnp.sum(probs * value, axis=1, keepdims=True)
            d_scores[t - 2] = (probs * (value - inner)).astype(bf16)
        if 0 <= t - 4 < len(units):
            p, side = units[t - 4]
            value = d_scores.pop(t - 4)
            da2 = da_ref[:, p * 128 : (p + 1) * 128]
            parts = [
                mm(value, columns(1, p) * sides[side]) * 0.125,
                mm_tn(value, columns(0, p) * sides[side]) * 0.125,
                mm_tn(p_ref[0, 0, p * 2 + side], da2 * sides[side]),
            ]
            total = parts if side == 0 else [a + b for a, b in zip(total, parts)]
            if side == 1:
                for part in range(3):
                    lo = part * half_width + p * 128
                    rounded = total[part].astype(bf16)
                    out_ref[0, :, lo : lo + 128] = rounded
                    if part != 1:
                        sums_ref[:, lo : lo + 128] += fold_rows(rounded.astype(f32))


def gelu_parts(u):
    size = jnp.abs(u)
    t = 1.0 / (1.0 + size * (0.3275911 * 0.7071067811865476))
    bell = jnp.exp(u * u * -0.5)
    poly = t * (
        0.127414796
        + t * (-0.142248368 + t * (0.7107068705 + t * (-0.7265760135 + t * 0.5307027145)))
    )
    tail = poly * bell
    cdf = jnp.where(u < 0.0, tail, 1.0 - tail)
    return u * cdf, cdf + u * (bell * 0.3989422804014327)


def feed_stages(cut, vec_ref, ins, outs, sums_ref, slope, wa, wb, ready):
    x_ref, a_ref, cot_ref = ins
    out_ref, g_ref, du_ref, n1_ref, df_ref, db_ref, da_ref, dr1_ref = outs
    width = x_ref.shape[1]
    half = width // 2
    place = lambda j: (j // 2, (j % 2) * width)

    attended = a_ref[cut, :]
    branch = jnp.concatenate(
        [mm(attended, wa[h, :, :half]) for h in range(2)], axis=1
    ) + vec_ref[2:3, :]
    yield
    resid = x_ref[cut, :].astype(f32) + branch
    center = resid - row_mean(resid)
    rstd = lax.rsqrt(row_mean(center * center) + EPS)
    z1 = center * rstd
    n1 = z1 * (1.0 + vec_ref[3:4, :]) + vec_ref[4:5, :]
    n1b = n1.astype(bf16)
    n1_ref[cut, :] = n1b
    yield

    def up(j):
        h, lo = place(j)
        return mm(n1b, wa[h, :, half + lo : half + lo + width]) + vec_ref[8 + j : 9 + j, :]

    hidden = [up(0)]
    yield
    feed = None
    for j in range(4):
        if j < 3:
            hidden.append(up(j + 1))
            yield
        active, tilt = gelu_parts(hidden[j])
        hidden[j] = None
        active = active.astype(bf16)
        at = slice(j * width, (j + 1) * width)
        g_ref[cut, at] = active
        slope[cut, at] = tilt
        yield
        if j == 0:
            ready()
        h, lo = place(j)
        part = mm_nt(active, wb[h, :, lo : lo + width])
        feed = part if feed is None else feed + part
        yield
    resid2 = n1 + feed + vec_ref[7:8, :]
    center2 = resid2 - row_mean(resid2)
    rstd2 = lax.rsqrt(row_mean(center2 * center2) + EPS)
    z2 = center2 * rstd2
    gain2 = 1.0 + vec_ref[5:6, :]
    out_ref[cut, :] = (z2 * gain2 + vec_ref[6:7, :]).astype(bf16)
    dy = cot_ref[cut, :].astype(f32)
    s = dy * gain2
    dr2 = rstd2 * (s - row_mean(s) - z2 * row_mean(s * z2))
    df = dr2.astype(bf16)
    df_ref[cut, :] = df
    sums_ref[3] += fold_rows(dy * z2)
    sums_ref[4] += fold_rows(dy)
    sums_ref[5] += fold_rows(df.astype(f32))
    yield

    def back(j):
        h, lo = place(j)
        return mm(df, wb[h, :, lo : lo + width])

    d_active = [back(0)]
    yield
    dn1 = dr2
    for j in range(4):
        if j < 3:
            d_active.append(back(j + 1))
            yield
        at = slice(j * width, (j + 1) * width)
        du = (d_active[j] * slope[cut, at]).astype(bf16)
        d_active[j] = None
        du_ref[cut, at] = du
        sums_ref[6 + j] += fold_rows(du.astype(f32))
        yield
        h, lo = place(j)
        dn1 = dn1 + mm_nt(du, wa[h, :, half + lo : half + lo + width])
        yield
    sums_ref[0] += fold_rows(dn1 * z1)
    sums_ref[1] += fold_rows(dn1)
    s = dn1 * (1.0 + vec_ref[3:4, :])
    dr1 = rstd * (s - row_mean(s) - z1 * row_mean(s * z1))
    dr1_ref[cut, :] = dr1
    db = dr1.astype(bf16)
    db_ref[cut, :] = db
    sums_ref[2] += fold_rows(db.astype(f32))
    yield
    da = mm_nt(db[:, :half], wa[0, :, :half]) + mm_nt(db[:, half:], wa[1, :, :half])
    da_ref[cut, :] = da.astype(bf16)
    yield


def feed_both(n_a, n_b, sub, info, vec_ref, x_ref, a_ref, cot_ref, *refs):
    src_a = refs[:n_a]
    src_b = refs[n_a : n_a + n_b]
    refs = refs[n_a + n_b :]
    outs = refs[:8]
    sums_ref, slope, wa, wb, sems_a, sems_b = refs[8:]
    step = pl.program_id(0)
    copies_a = weight_copies(info, src_a, wa, sems_a)
    copies_b = weight_copies(info, src_b, wb, sems_b)

    @pl.when(step == 0)
    def _():
        for copy in copies_a + copies_b:
            copy.start()
        sums_ref[...] = jnp.zeros_like(sums_ref)
        for copy in copies_a:
            copy.wait()

    waited = []

    def ready():
        if not waited:
            waited.append(True)

            @pl.when(step == 0)
            def _():
                for copy in copies_b:
                    copy.wait()

    ins = (x_ref, a_ref, cot_ref)
    blocks = [
        feed_stages(slice(r, r + sub), vec_ref, ins, outs, sums_ref, slope, wa, wb, ready)
        for r in range(0, x_ref.shape[0], sub)
    ]
    waiting, t = list(range(len(blocks))), 0
    while waiting:
        for i in list(waiting):
            if t >= i and next(blocks[i], True):
                waiting.remove(i)
        t += 1


def token_gradient(n_src, info, other_ref, mine_ref, dr1_ref, *refs):
    src = refs[:n_src]
    out_ref, w, sems = refs[n_src:]
    used = mine_ref.shape[2]

    @pl.when(pl.program_id(0) == 0)
    def _():
        copies = weight_copies(info, src, w, sems)
        for copy in copies:
            copy.start()
        for copy in copies:
            copy.wait()

    out_ref[...] = (
        dr1_ref[...]
        + mm_nt(other_ref[0], w[1 - info[0], :, :used])
        + mm_nt(mine_ref[0], w[info[0], :, :used])
    )


def vector_rows(info, sums_ref, other_ref, mine_ref):
    total = lambda v: jnp.sum(v, axis=0, keepdims=True)
    half = other_ref.shape[1] // 3
    rows = []
    for part in (0, 2):
        cut = slice(part * half, (part + 1) * half)
        other, mine = total(other_ref[:, cut]), total(mine_ref[:, cut])
        first = jnp.where(info[0] == 0, mine, other)
        second = jnp.where(info[0] == 0, other, mine)
        rows.append(jnp.concatenate([first, second], axis=1))
    return rows + [total(sums_ref[i]) for i in (2, 0, 1, 3, 4, 5, 6, 7, 8, 9)]


DIRECT = tuple([(a, k) for k in range(4)] for a in range(4))
RELAYED = (
    [(0, k) for k in range(4)],
    [(3, 0), (3, 1), (1, 0), (1, 1)],
    [(3, 2), (3, 3), (2, 2), (2, 3)],
    [(1, 2), (1, 3)],
    [(2, 0), (2, 1)],
)


def weight_gradient(starts, sizes, has_recv, buffers, has_ext, info, *refs):
    count = len(starts)
    lhs = refs[:count]
    rhs = refs[count : 2 * count]
    at = 2 * count
    recv = None
    if has_recv:
        recv = refs[at]
        at += 1
    if has_ext:
        sums_ref, other_ref, mine_ref, spread_ref, pick_ref = refs[at : at + 5]
        at += 5
    (*outs, acc) = refs[at:]
    step = pl.program_id(0)

    def store(value, add):
        size = value.shape[1]
        if buffers is None:
            outs[0][:, :size] = value.astype(outs[0].dtype)
            return
        acc[:, :size] = value
        for out, slots in zip(outs, buffers):
            for j, (a, k) in enumerate(slots):
                row = chip_row(info, a, k, True)
                mine = acc[pl.ds(row, 48), :size]
                if add:
                    mine = mine + recv[pl.ds(row, 48), :size].astype(f32)
                out[j, :, :size] = mine.astype(bf16)

    for number, start in enumerate(starts):
        here = step >= start
        if number + 1 < count:
            here = here & (step < starts[number + 1])
        elif has_ext:
            here = here & (step < pl.num_programs(0) - 1)

        @pl.when(here)
        def _(number=number):
            right = rhs[number]
            right = right[0] if len(right.shape) == 3 else right[...]
            store(mm_tn(lhs[number][...], right), True)

    if has_ext:

        @pl.when(step == pl.num_programs(0) - 1)
        def _():
            rows = vector_rows(info, sums_ref, other_ref, mine_ref)
            picked = jnp.concatenate([(r * pick_ref[...]).astype(bf16) for r in rows], axis=0)
            store(mm_nt(picked, spread_ref[...]), False)


def params():
    return pltpu.CompilerParams(
        dimension_semantics=("arbitrary",), vmem_limit_bytes=VMEM_LIMIT
    )


def call(kernel, grid, in_specs, out_specs, out_shape, scratch, flops, nbytes, name, after=()):
    def body(info, *refs):
        kernel(info, *refs[len(after) :])

    run = pl.pallas_call(
        body,
        grid_spec=pltpu.PrefetchScalarGridSpec(
            num_scalar_prefetch=1,
            grid=grid,
            in_specs=[ANY] * len(after) + in_specs,
            out_specs=out_specs,
            scratch_shapes=scratch,
        ),
        out_shape=out_shape,
        compiler_params=params(),
        cost_estimate=pl.CostEstimate(
            flops=int(flops * COST), bytes_accessed=int(nbytes * COST), transcendentals=0
        ),
        name=name,
    )
    return lambda info, *operands: run(info, *after, *operands)


def struct(shape, dtype):
    return jax.ShapeDtypeStruct(shape, dtype)


def whole_block(shape):
    return pl.BlockSpec(shape, lambda i, info: (0,) * len(shape))


def rows_block(rows, columns):
    return pl.BlockSpec((rows, columns), lambda i, info: (i, 0))


def spread_tables(width):
    per = width // 64
    e = np.arange(width)
    spread = (np.arange(EXT)[:, None] == (e % per)[None, :]).astype(np.float32)
    pick = (np.arange(64)[:, None] == (e // per)[None, :]).astype(np.float32)
    return spread, pick


def run_attention_forward(info, x, pieces, vec, crops, after):
    rows, width = x.shape
    slots = rows // crops
    half = width // 2
    w_columns = pieces[0].shape[-1]
    has_ext = vec is None
    pairs = half // 128
    if has_ext:
        spread, pick = spread_tables(width)
        extra = [jnp.asarray(spread, bf16), jnp.asarray(pick, f32)]
    else:
        extra = [vec]
    extra_specs = [whole_block(e.shape) for e in extra]
    kernel = functools.partial(attention_forward, len(pieces), has_ext, pairs)
    return call(
        kernel,
        (crops,),
        [rows_block(slots, width)] + [ANY] * len(pieces) + extra_specs,
        [
            whole_block((16, width)),
            pl.BlockSpec((2, slots, 3 * half), lambda i, info: (0, i, 0)),
            pl.BlockSpec((2, 1, H // 2, slots, slots), lambda i, info: (0, i, 0, 0, 0)),
            rows_block(slots, width),
        ],
        [
            struct((16, width), f32),
            struct((2, rows, 3 * half), bf16),
            struct((2, crops, H // 2, slots, slots), bf16),
            struct((rows, width), bf16),
        ],
        [
            pltpu.VMEM((2, width, w_columns), bf16),
            pltpu.VMEM((2, 1, 3 * half), f32),
            pltpu.SemaphoreType.DMA((sem_count(pieces),)),
        ],
        2 * rows * width * 3 * width + 8 * rows * slots * width,
        30e6,
        "attention_forward",
        after,
    )(info, x, *pieces, *extra)


def run_attention_backward(info, qkv, da, probs, crops, which, after):
    _, rows, columns = qkv.shape
    slots = rows // crops
    half = columns // 3

    def pick(info):
        return info[0] if which else 1 - info[0]

    kernel = functools.partial(attention_backward, half // 128)
    return call(
        kernel,
        (crops,),
        [
            pl.BlockSpec((1, slots, columns), lambda i, info: (pick(info), i, 0)),
            pl.BlockSpec((slots, half), lambda i, info: (i, pick(info))),
            pl.BlockSpec(
                (1, 1, H // 2, slots, slots), lambda i, info: (pick(info), i, 0, 0, 0)
            ),
        ],
        [
            pl.BlockSpec((1, slots, columns), lambda i, info: (0, i, 0)),
            whole_block((8, columns)),
        ],
        [struct((1, rows, columns), bf16), struct((8, columns), f32)],
        [],
        16 * rows * slots * half,
        12e6,
        "attention_backward",
        after,
    )(info, qkv, da, probs)


def run_feed(info, vec, x, attended, cot, pieces_a, pieces_b, block, sub, after):
    rows, width = x.shape
    ff = 2 * pieces_b[0].shape[-1]
    kernel = functools.partial(feed_both, len(pieces_a), len(pieces_b), sub)
    narrow, wide = rows_block(block, width), rows_block(block, ff)
    return call(
        kernel,
        (rows // block,),
        [whole_block(vec.shape)] + [narrow] * 3 + [ANY] * (len(pieces_a) + len(pieces_b)),
        [narrow, wide, wide] + [narrow] * 5 + [whole_block((10, 8, width))],
        [struct((rows, width), bf16), struct((rows, ff), bf16), struct((rows, ff), bf16)]
        + [struct((rows, width), bf16)] * 4
        + [struct((rows, width), f32), struct((10, 8, width), f32)],
        [
            pltpu.VMEM((block, ff), f32),
            pltpu.VMEM((2, width, pieces_a[0].shape[-1]), bf16),
            pltpu.VMEM((2, width, pieces_b[0].shape[-1]), bf16),
            pltpu.SemaphoreType.DMA((sem_count(pieces_a),)),
            pltpu.SemaphoreType.DMA((sem_count(pieces_b),)),
        ],
        4 * rows * width * (width + 2 * ff),
        53e6,
        "feed_both",
        after,
    )(info, vec, x, attended, cot, *pieces_a, *pieces_b)


def run_token_gradient(info, dqkv_by, dr1, pieces, block, after):
    rows, width = dr1.shape
    columns = dqkv_by[0].shape[2]
    kernel = functools.partial(token_gradient, len(pieces))
    return call(
        kernel,
        (rows // block,),
        [
            pl.BlockSpec((1, block, columns), lambda i, info: (0, i, 0)),
            pl.BlockSpec((1, block, columns), lambda i, info: (0, i, 0)),
            rows_block(block, width),
        ]
        + [ANY] * len(pieces),
        rows_block(block, width),
        struct((rows, width), f32),
        [
            pltpu.VMEM((2, width, pieces[0].shape[-1]), bf16),
            pltpu.SemaphoreType.DMA((sem_count(pieces),)),
        ],
        4 * rows * width * columns,
        20e6,
        "token_gradient",
        after,
    )(info, *dqkv_by, dr1, *pieces)


def run_weight_gradient(info, pairs, columns, block, pick, recv, ext, full, after, buffers=None):
    rows, width = pairs[0][0].shape
    once = pl.Buffered(1)
    starts, sizes, step = [], [], 0
    rhs_specs = []
    for _, rhs, total, size in pairs:
        count = total // size
        starts.append(step)
        sizes.append(size)
        near = lambda i, step=step, count=count: jnp.clip(i - step, 0, count - 1)
        if rhs.ndim == 3:
            rhs_specs.append(
                pl.BlockSpec((1, rows, size), lambda i, info, near=near: (0, 0, near(i)))
            )
        else:
            rhs_specs.append(
                pl.BlockSpec(
                    (rows, size),
                    lambda i, info, near=near, count=count: (0, pick(info) * count + near(i)),
                )
            )
        step += count
    operands = [p[0] for p in pairs] + [p[1] for p in pairs]
    left = pl.BlockSpec((rows, width), lambda i, info: (0, 0), pipeline_mode=once)
    specs = [left for _ in pairs] + rhs_specs
    if recv is not None:
        recv, base = recv
        operands.append(recv)
        last = step - 1
        specs.append(
            pl.BlockSpec((width, block), lambda i, info: (0, base + jnp.minimum(i, last)))
        )
    if ext is not None:
        spread, pick_rows = spread_tables(width)
        more = list(ext) + [jnp.asarray(spread, bf16), jnp.asarray(pick_rows, f32)]
        operands += more
        specs += [whole_block(v.shape) for v in more]
        step += 1
    if recv is None:
        out_specs = [pl.BlockSpec((width, block), lambda i, info: (0, i))]
        out_shape = [struct((width, columns), f32 if full else bf16)]
    else:
        out_specs = [
            pl.BlockSpec((len(b), 48, block), lambda i, info: (0, 0, i)) for b in buffers
        ]
        out_shape = [struct((len(b), 48, columns), bf16) for b in buffers]
    kernel = functools.partial(
        weight_gradient, tuple(starts), tuple(sizes), recv is not None, buffers, ext is not None
    )
    return call(
        kernel,
        (step,),
        specs,
        out_specs,
        out_shape,
        [pltpu.VMEM((width, block), f32)],
        2 * rows * width * columns,
        12e6,
        "weight_gradient",
        after,
    )(info, *operands)


def neighbours(n):
    flip = lambda bits: [(i, i ^ bits) for i in range(n)]
    shift = lambda k: [(i, (i + 8 * k) % n) for i in range(n)]
    ways = {"core": 1, "x": 2, "y": 4, "xy": 6, "z": 8, "zz": 16, "zzz": 24}
    return {way: flip(bits) for way, bits in ways.items()}, shift


def send(value, pairs):
    return lax.ppermute(value, "dp", pairs)


def chip_piece(core, first, second, n):
    flips, _ = neighbours(n)
    keep = jnp.where(core == 0, first, second)
    give = jnp.where(core == 0, second, first)
    got = send(give, flips["core"])
    return jnp.where(core == 0, jnp.concatenate([keep, got]), jnp.concatenate([got, keep]))


def along_z(piece, n):
    _, shift = neighbours(n)
    return jnp.concatenate([piece] + [send(piece, shift(k)) for k in (1, 2, 3)])


def across_relayed(base, n):
    flips, _ = neighbours(n)
    by_x, by_y = send(base, flips["x"]), send(base, flips["y"])
    mid = base.shape[0] // 2
    return [base, by_x, by_y, send(by_x[:mid], flips["y"]), send(by_y[mid:], flips["x"])]


def across_direct(base, n):
    flips, _ = neighbours(n)
    return [base] + [send(base, flips[way]) for way in ("x", "y", "xy")]


def both_cores(own, n):
    flips, _ = neighbours(n)
    return own + [send(v, flips["core"]) for v in own]


def behind(value, *others):
    return lax.optimization_barrier((value,) + others)[0]


def sum_first(parts, n, *gates):
    flips, _ = neighbours(n)
    got_x, got_y = send(parts[1], flips["x"]), send(parts[2], flips["y"])
    got_x, got_y = lax.optimization_barrier((got_x, got_y) + gates)[:2]
    to_x = (parts[3].astype(f32) + got_y[:2].astype(f32)).astype(bf16)
    to_y = (parts[4].astype(f32) + got_x[:2].astype(f32)).astype(bf16)
    return got_x, got_y, to_x, to_y


def sum_rest(parts, first, n, *gates):
    flips, _ = neighbours(n)
    got_x, got_y, to_x, to_y = first
    rest_x, rest_y = send(to_x, flips["x"]), send(to_y, flips["y"])
    got_x, got_y, rest_x, rest_y = lax.optimization_barrier(
        (got_x, got_y, rest_x, rest_y) + gates
    )[:4]
    low = parts[0][:2].astype(f32) + got_x[2:].astype(f32) + rest_y.astype(f32)
    high = parts[0][2:].astype(f32) + got_y[2:].astype(f32) + rest_x.astype(f32)
    return [low[0]] + [v.astype(bf16) for v in (low[1], high[0], high[1])]


def share_rows(core, done, n):
    flips, _ = neighbours(n)
    rows = done.shape[0] // 2
    keep = jnp.where(core == 0, done[:rows], done[rows:])
    give = jnp.where(core == 0, done[rows:], done[:rows])
    got = send(give, flips["core"])
    return jnp.where(core == 0, keep, got), jnp.where(core == 0, got, keep)


def sum_along(total, n):
    flips, _ = neighbours(n)
    done = total[0]
    for value, way in zip(total[1:], ("z", "zz", "zzz")):
        done = done + send(value, flips[way]).astype(f32)
    return done


def halves(matrix, groups):
    size = matrix.shape[1] // groups
    cut = size // 2
    return [
        jnp.concatenate(
            [matrix[:, g * size + h * cut : g * size + (h + 1) * cut] for g in range(groups)],
            axis=1,
        )
        for h in range(2)
    ]


def join(first, second, groups):
    rows, columns = first.shape
    shape = (rows, groups, 1, columns // groups)
    both = jnp.concatenate([first.reshape(shape), second.reshape(shape)], axis=2)
    return both.reshape(rows, 2 * columns)


def momentum_step(weight, copy):
    return (weight.astype(f32) - copy) * 0.0005


def momentum_all(info, *refs):
    count = len(refs) // 3
    for weight, copy, out in zip(refs[:count], refs[count : 2 * count], refs[2 * count :]):
        out[...] = momentum_step(weight[...], copy[...])


def run_momentum(info, weights, copies, after):
    blocks = [whole_block(w.shape) for w in weights]
    return call(
        momentum_all,
        (1,),
        blocks + blocks,
        blocks,
        [struct(w.shape, f32) for w in weights],
        [],
        0,
        0,
        "momentum",
        after,
    )(info, *weights, *copies)


def local(
    n,
    tokens,
    lengths,
    w_qkv,
    w_out,
    w_in,
    w_down,
    vector,
    key_qkv,
    key_out,
    key_in,
    key_down,
    key_vector,
    cotangent,
):
    width = tokens.shape[1]
    half = width // 2
    ff = w_in.shape[1]
    crops = lengths.shape[0]
    near = n == 32 and w_qkv.shape[0] == 24
    me = lax.axis_index("dp").astype(jnp.int32)
    core = me & 1
    place = jnp.stack([core, (me >> 1) & 1, (me >> 2) & 1, (me >> 3) & 3])
    info = jnp.concatenate([place, lengths.astype(jnp.int32)])

    qkv_halves = halves(w_qkv, 3)
    out_halves = halves(w_out, 1)
    in_halves = halves(w_in, 1)
    down_halves = halves(w_down, 1)
    mixed = [jnp.concatenate([out_halves[h], in_halves[h]], axis=1) for h in range(2)]
    if near:
        own_rows = w_qkv.shape[0]
        ext = jnp.pad(
            vector.reshape(own_rows, vector.shape[0] // own_rows),
            ((0, 0), (0, EXT - vector.shape[0] // own_rows)),
        )
        first = [jnp.concatenate([q, ext], axis=1) for q in qkv_halves]
        base = along_z(chip_piece(core, first[0], first[1], n), n)
        p_qkv = across_relayed(base, n)
        piece = chip_piece(core, mixed[0], mixed[1], n)
        base_mixed = along_z(behind(piece, base), n)
        p_mixed = across_direct(behind(base_mixed, *p_qkv), n)
        p_qkv = both_cores(p_qkv, n)
        p_down = [lax.all_gather(jnp.stack(down_halves), "dp", axis=1, tiled=True)]
        deltas = run_momentum(
            info,
            (w_qkv, w_out, w_in, w_down, vector.reshape(1, -1)),
            (key_qkv, key_out, key_in, key_down, key_vector.reshape(1, -1)),
            (base,),
        )
        order = [base_mixed, deltas[0]]
        vec = None
    else:
        everywhere = lambda pair: [
            lax.all_gather(jnp.stack(pair), "dp", axis=1, tiled=True)
        ]
        p_qkv, p_mixed, p_down = map(everywhere, (qkv_halves, mixed, down_halves))
        vec = lax.all_gather(vector, "dp", axis=0, tiled=True).astype(f32)
        vec = jnp.pad(vec.reshape(-1, width), ((0, 16 - vec.shape[0] // width), (0, 0)))
        order = []
        pairs = zip(
            (w_qkv, w_out, w_in, w_down, vector), (key_qkv, key_out, key_in, key_down, key_vector)
        )
        deltas = [momentum_step(weight, copy) for weight, copy in pairs]

    vec, qkv, probs, attended = run_attention_forward(info, tokens, p_qkv, vec, crops, order)
    if near:
        p_mixed = both_cores([behind(v, attended) for v in p_mixed], n)
    output, active, du, n1, df, db, da, dr1, sums = run_feed(
        info, vec, tokens, attended, cotangent, p_mixed, p_down, 512, 256, ()
    )
    down_pairs = [(df, active, ff // 2, width)]
    mixed_pairs = [(n1, du, ff // 2, width), (attended, db, half, half)]
    if near:
        flips, _ = neighbours(n)

        def away(pairs, columns, block, after):
            return run_weight_gradient(
                info, pairs, columns, block, lambda info: 1 - info[0], None, None, False, after
            )[0]

        def mine(pairs, columns, block, got, ext, after, buffers=RELAYED):
            return run_weight_gradient(
                info, pairs, columns, block, lambda info: info[0], got, ext, False, after, buffers
            )

        away_ff = away(down_pairs + mixed_pairs, half + ff, width, ())
        got_ff = send(away_ff, flips["core"])
        dqkv_other, sums_other = run_attention_backward(
            info, qkv, da, probs, crops, 0, (away_ff,)
        )
        parts_down = mine(down_pairs, ff // 2, width, (got_ff, 0), None, (sums_other,))
        qkv_pairs = lambda dqkv: [(tokens, dqkv, 3 * half, half)]
        away_qkv = away(qkv_pairs(dqkv_other), 3 * half, half, (parts_down[0],))
        got_qkv = send(away_qkv, flips["core"])
        parts_mixed = mine(
            mixed_pairs, half + ff // 2, width, (got_ff, ff // 2 // width), None, (away_qkv,)
        )
        first_down = sum_first(parts_down, n, parts_mixed[0])
        dqkv_mine, sums_mine = run_attention_backward(
            info, qkv, da, probs, crops, 1, (parts_mixed[0],) + first_down[2:]
        )
        total_down = sum_rest(parts_down, first_down, n, sums_mine)
        sums_all = (sums, sums_other, sums_mine)
        parts_qkv = mine(
            qkv_pairs(dqkv_mine), 3 * half + EXT, half, (got_qkv, 0), sums_all, (total_down[1],)
        )
        first_mixed = sum_first(parts_mixed, n, parts_qkv[0])
        grad_tokens = run_token_gradient(
            info, [dqkv_other, dqkv_mine], dr1, p_qkv, 256, (parts_qkv[0],) + first_mixed[2:]
        )
        total_mixed = sum_rest(parts_mixed, first_mixed, n, grad_tokens)
        first_qkv = sum_first(parts_qkv, n, grad_tokens)
        g_down = share_rows(core, sum_along(total_down, n), n)
        g_mixed = share_rows(core, sum_along(total_mixed, n), n)
        g_in = [v[:, : ff // 2] for v in g_mixed]
        g_out = [v[:, ff // 2 :] for v in g_mixed]
        g_qkv = share_rows(core, sum_along(sum_rest(parts_qkv, first_qkv, n), n), n)
        per = vector.shape[0] // w_qkv.shape[0]
        grad_down = join(g_down[0], g_down[1], 1)
        grad_vector = (g_qkv[0] + g_qkv[1])[:, 3 * half : 3 * half + per].reshape(-1)
        g_qkv = [v[:, : 3 * half] for v in g_qkv]
    else:

        def gradient(pairs_of, columns, block):
            return [
                run_weight_gradient(
                    info, pairs_of(h), columns, block, lambda info, h=h: h, None, None, True, ()
                )[0]
                for h in range(2)
            ]

        info_of = lambda h: info.at[0].set(h)
        results = [
            run_attention_backward(info_of(h), qkv, da, probs, crops, 1, ()) for h in range(2)
        ]
        dqkv_by = [r[0] for r in results]
        bias_sums = jnp.stack([jnp.sum(r[1], axis=0) for r in results]).reshape(2, 3, half)
        sums = jnp.sum(sums, axis=1)
        vec_grad = jnp.concatenate(
            [bias_sums[:, 0].reshape(-1), bias_sums[:, 2].reshape(-1)]
            + [sums[i] for i in (2, 0, 1, 3, 4, 5, 6, 7, 8, 9)]
        )
        g_down = gradient(lambda h: down_pairs, ff // 2, width)
        g_mixed = gradient(lambda h: mixed_pairs, half + ff // 2, width)
        g_in = [v[:, : ff // 2] for v in g_mixed]
        g_out = [v[:, ff // 2 :] for v in g_mixed]
        grad_down = join(g_down[0], g_down[1], 1)
        g_qkv = gradient(lambda h: [(tokens, dqkv_by[h], 3 * half, half)], 3 * half, half)
        grad_vector = lax.psum_scatter(vec_grad, "dp", scatter_dimension=0, tiled=True)
        grad_tokens = run_token_gradient(info_of(1), dqkv_by, dr1, p_qkv, 256, ())
    grad_qkv = join(g_qkv[0], g_qkv[1], 3)
    grad_out = join(g_out[0], g_out[1], 1)
    grad_in = join(g_in[0], g_in[1], 1)
    if not near:
        grad_qkv, grad_out, grad_in, grad_down = (
            lax.psum_scatter(g, "dp", scatter_dimension=0, tiled=True)
            for g in (grad_qkv, grad_out, grad_in, grad_down)
        )
    return (
        output,
        grad_tokens,
        grad_qkv,
        grad_out,
        grad_in,
        grad_down,
        grad_vector,
        *deltas[:4],
        deltas[4].reshape(-1),
    )


def solution(mesh):
    n = mesh.shape["dp"]
    rows, flat = P("dp", None), P("dp")
    return jax.shard_map(
        functools.partial(local, n),
        mesh=mesh,
        in_specs=(rows, flat, rows, rows, rows, rows, flat, rows, rows, rows, rows, flat, rows),
        out_specs=(rows, rows, rows, rows, rows, rows, flat, rows, rows, rows, rows, flat),
        check_vma=False,
    )
```

time: 452 us -> 343 us (0.76)
  waiting for transfers between devices: 120 us -> 66.4 us
  Pallas kernels: 214 us -> 176 us
  other arithmetic: 24.4 us -> 7.34 us
  between operations: 1.67 us -> 15 us
  local copies, waits for them, and re-layouts: 21.1 us -> 13.4 us
  starting transfers between devices: 64.7 us -> 59.1 us
    ppermute x63 -> x50, waiting for transfers between devices: 120 us -> 66.3 us  [send(): return lax.ppermute(value, 'dp', pairs)]
    pallas_call x12 -> x11, Pallas kernels: 214 us -> 176 us  [call(): return lambda info, *operands: run(info, *after, *operands)]
    select_n x13 -> x9, other arithmetic: 8.99 us -> 0.26 us  [the longest x2 0.08 us: share_rows(): return (jnp.where(core == 0, keep, got), jnp.where(core == 0, got, keep))]
    unnamed x99 -> x72, local copies, waits for them, and re-layouts: 11.1 us -> 4.88 us
    ppermute x63 -> x50, starting transfers between devices: 64.7 us -> 59.1 us  [send(): return lax.ppermute(value, 'dp', pairs)]
  transfers between devices with their start and end apart: 63 -> 51, of which waited for: 21 -> 19; matrix products, arithmetic and copies ran while one was open for 7% -> 4% of each run, Pallas kernels for 21% -> 27%
where the time goes in v2:
time: 343 us; the launch traced here: 337 us
  Pallas kernels  176 us (51%)
  waiting for transfers between devices  66.4 us (19%)
  starting transfers between devices  59.1 us (17%)
  between operations  15 us (4%)
  local copies, waits for them, and re-layouts  13.4 us (4%)
  other arithmetic  7.34 us (2%)
    pallas_call x11, Pallas kernels, call(): return lambda info, *operands: run(info, *after, *operands)  176 us
    ppermute x50, waiting for transfers between devices, send(): return lax.ppermute(value, 'dp', pairs)  66.3 us
    ppermute x50, starting transfers between devices, send(): return lax.ppermute(value, 'dp', pairs)  59.1 us
  transfers between devices with their start and end apart: 51, of which 19 were waited for; matrix products, arithmetic and copies ran while one was open for 4% of the time, Pallas kernels for 27%

profile of v2, /device:TPU:0, one launch (start us, length us, event | category | flops | bytes accessed | tf_op | source)
XLA Modules:
  0.0 337.1 jit_solution(4533027676434863576)
XLA Ops:
  12.8 2.6 collective-permute-start.2
  15.4 2.6 collective-permute-start.3
  18.0 1.3 collective-permute-start.4
  19.5 2.2 collective-permute-done.2
  21.7 5.1 %collective-permute-done.3 = bf16[48,1280]{1,0:T(8,128)(2,1)S(1)} collective-permute-done((bf16[48,1280]{1,0:T(8,128)(2,1)S(1)}, bf16[48,1280]{1,0:T(8,128)(2,1)S(1)}, u32[]{:S(2)}, u32[]{:S(2)}) %collective-permute-start.3) | collective-permute-done | bytes 122912 | tf_op jit(solution)/shard_map/ppermute | solution.py:698
  26.9 1.6 collective-permute-start.8
  28.4 1.5 collective-permute-start.9
  30.0 4.8 %collective-permute-start.5 = (bf16[48,1920]{1,0:T(8,128)(2,1)S(1)}, bf16[48,1920]{1,0:T(8,128)(2,1)S(1)}, u32[]{:S(2)}, u32[]{:S(2)}) collective-permute-start(bf16[48,1920]{1,0:T(8,128)(2,1)S(1)} %maximum_select_fusion), channel_id=1, source_target_pairs={{0,8},{1,9},{2,10},{3,11},{4,12},{5,13},{6,14},{7,15},{8,16},{9,17... | collective-permute-start | bytes 552968 | tf_op jit(solution)/shard_map/ppermute | solution.py:698
  34.8 1.2 collective-permute-start.6
  36.0 1.2 collective-permute-start.7
  37.2 2.7 collective-permute-done.8.refs_4_.refs_7_
  40.0 1.2 collective-permute-done.9.refs_5_.refs_8_
  41.2 1.5 collective-permute-start.10
  43.4 7.6 %collective-permute-done.6 = bf16[48,1920]{1,0:T(8,128)(2,1)S(1)} collective-permute-done((bf16[48,1920]{1,0:T(8,128)(2,1)S(1)}, bf16[48,1920]{1,0:T(8,128)(2,1)S(1)}, u32[]{:S(2)}, u32[]{:S(2)}) %collective-permute-start.6) | collective-permute-done | bytes 184352 | tf_op jit(solution)/shard_map/ppermute | solution.py:698
  52.0 1.5 collective-permute-start.19
  53.8 1.7 collective-permute-start.17
  58.5 3.0 momentum.1
  62.3 21.9 %attention_forward.1 = (f32[16,768]{1,0:T(8,128)}, bf16[2,1536,1152]{2,1,0:T(8,128)(2,1)}, bf16[2,6,6,256,256]{4,3,2,1,0:T(8,128)(2,1)}, bf16[1536,768]{1,0:T(8,128)(2,1)}) custom-call(s32[10]{0:T(128)} %concatenate.45.info, bf16[192,1920]{1,0:T(8,128)(2,1)} %copy-done.2, f32[24,2304]{1,0:T(8,128)} %get-tuple-element.68.refs_1_, bf16[1536,768]{1,0:T(8,128)(2,1)} %refs_1_.7, ...), custom_call_target="tpu_custom_call" | custom-call | flops 7851737 | bytes 30000 | tf_op jit(solution)/shard_map/attention_forward/pallas_call | solution.py:477
  84.8 11.4 %collective-permute-done.18.refs_6_ = bf16[192,1920]{1,0:T(8,128)(2,1)} collective-permute-done((bf16[192,1920]{1,0:T(8,128)(2,1)S(1)}, bf16[192,1920]{1,0:T(8,128)(2,1)}, u32[]{:S(2)}, u32[]{:S(2)}) %collective-permute-start.18) | collective-permute-done | bytes 737312 | tf_op jit(solution)/shard_map/ppermute | solution.py:698
  96.7 2.2 collective-permute-done.22.refs_10_
  99.0 1.8 collective-permute-done.21.refs_9_
  101.6 59.0 %feed_both.1 = (bf16[1536,768]{1,0:T(8,128)(2,1)}, bf16[1536,3072]{1,0:T(8,128)(2,1)}, bf16[1536,3072]{1,0:T(8,128)(2,1)}, bf16[1536,768]{1,0:T(8,128)(2,1)}, bf...) custom-call(s32[10]{0:T(128)} %concatenate.45.info, ...), custom_call_target="tpu_custom_call" | custom-call | flops 32614908 | bytes 53000 | tf_op jit(solution)/shard_map/feed_both/pallas_call | solution.py:477
  160.6 16.3 %weight_gradient.5.refs_0_ = bf16[768,3456]{1,0:T(8,128)(2,1)} custom-call(s32[10]{0:T(128)} %concatenate.45.info, bf16[1536,768]{1,0:T(8,128)(2,1)} %get-tuple-element.83.refs_0_.refs_1_, bf16[1536,768]{1,0:T(8,128)(2,1)} %get-tuple-element.84.refs_1_, bf16[1536,768]{1,0:T(8,128)(2,1)} %get-tuple-element.76.refs_2_, ...), custom_call_target="tpu_custom_call" | custom-call | flops 8153726 | bytes 12000 | tf_op jit(solution)/shard_map/weight_gradient/pallas_call | solution.py:477
  177.1 11.4 %attention_backward.2 = (bf16[1,1536,1152]{2,1,0:T(8,128)(2,1)}, f32[8,1152]{1,0:T(8,128)}) custom-call(s32[10]{0:T(128)} %concatenate.45.info, bf16[768,3456]{1,0:T(8,128)(2,1)} %weight_gradient.5.refs_0_, bf16[2,1536,1152]{2,1,0:T(8,128)(2,1)} %get-tuple-element.88.refs_1_.refs_3_, bf16[1536,768]{1,0:T(8,128)(2,1)} %get-tuple-element.89.refs_2_.refs_4_, ...), custom_call_target="tpu_custom_call" | custom-call | flops 2415919 | bytes 12000 | tf_op jit(solution)/shard_map/attention_backward/pallas_call | solution.py:477
  188.5 9.0 %weight_gradient.6 = (bf16[4,48,1536]{2,1,0:T(8,128)(2,1)}, bf16[4,48,1536]{2,1,0:T(8,128)(2,1)}, bf16[4,48,1536]{2,1,0:T(8,128)(2,1)}, bf16[2,48,1536]{2,1,0:T(8,128)(2,1)}, bf16[2,48,1536]{2,1,0:T(8,128)(2,1)}) custom-call(s32[10]{0:T(128)} %concatenate.45.info, f32[8,1152]{1,0:T(8,128)} %get-tuple-element.91.refs_0_.refs_5_, ...), custom_call_target="tpu_custom_call" | custom-call | flops 3623878 | bytes 12000 | tf_op jit(solution)/shard_map/weight_gradient/pallas_call | solution.py:477
  197.9 1.7 collective-permute-start.26
  199.6 7.9 %weight_gradient.7.refs_0_ = bf16[768,1152]{1,0:T(8,128)(2,1)} custom-call(s32[10]{0:T(128)} %concatenate.45.info, bf16[4,48,1536]{2,1,0:T(8,128)(2,1)} %get-tuple-element.92.refs_0_, bf16[1536,768]{1,0:T(8,128)(2,1)} %refs_1_.7, bf16[1,1536,1152]{2,1,0:T(8,128)(2,1)} %get-tuple-element.95.refs_2_.refs_3_), custom_call_target="tpu_custom_call" | custom-call | flops 2717908 | bytes 12000 | tf_op jit(solution)/shard_map/weight_gradient/pallas_call | solution.py:477
  207.6 11.9 %weight_gradient.8 = (bf16[4,48,1920]{2,1,0:T(8,128)(2,1)}, bf16[4,48,1920]{2,1,0:T(8,128)(2,1)}, bf16[4,48,1920]{2,1,0:T(8,128)(2,1)}, bf16[2,48,1920]{2,1,0:T(8,128)(2,1)}, bf16[2,48,1920]{2,1,0:T(8,128)(2,1)}) custom-call(s32[10]{0:T(128)} %concatenate.45.info, bf16[768,1152]{1,0:T(8,128)(2,1)} %weight_gradient.7.refs_0_, ...), custom_call_target="tpu_custom_call" | custom-call | flops 4529848 | bytes 12000 | tf_op jit(solution)/shard_map/weight_gradient/pallas_call | solution.py:477
  220.4 1.5 collective-permute-start.27
  221.9 11.7 %attention_backward.3 = (bf16[1,1536,1152]{2,1,0:T(8,128)(2,1)}, f32[8,1152]{1,0:T(8,128)}) custom-call(s32[10]{0:T(128)} %concatenate.45.info, bf16[4,48,1920]{2,1,0:T(8,128)(2,1)} %get-tuple-element.96.refs_0_, bf16[2,48,1536]{2,1,0:T(8,128)(2,1)} %copy-done.13, bf16[2,48,1536]{2,1,0:T(8,128)(2,1)} %copy-done.12, ...), custom_call_target="tpu_custom_call" | custom-call | flops 2415919 | bytes 12000 | tf_op jit(solution)/shard_map/attention_backward/pallas_call | solution.py:477
  233.6 1.3 add_convert_fusion.3
  235.0 3.2 collective-permute-start.47
  238.2 3.9 %collective-permute-start.48 = (bf16[48,1536]{1,0:T(8,128)(2,1)S(1)}, bf16[48,1536]{1,0:T(8,128)(2,1)S(1)}, u32[]{:S(2)}, u32[]{:S(2)}) collective-permute-start(bf16[48,1536]{1,0:T(8,128)(2,1)S(1)} %get-tuple-element.149), channel_id=1, source_target_pairs={{0,24},{1,25},{2,26},{3,27},{4,28},{5,29},{6,30},{7,31},{8,16},{9,... | collective-permute-start | bytes 442376 | tf_op jit(solution)/shard_map/ppermute | solution.py:698
  242.7 1.1 collective-permute-start.30
  244.7 5.2 %collective-permute-done.48 = bf16[48,1536]{1,0:T(8,128)(2,1)S(1)} collective-permute-done((bf16[48,1536]{1,0:T(8,128)(2,1)S(1)}, bf16[48,1536]{1,0:T(8,128)(2,1)S(1)}, u32[]{:S(2)}, u32[]{:S(2)}) %collective-permute-start.48) | collective-permute-done | bytes 147488 | tf_op jit(solution)/shard_map/ppermute | solution.py:698
  251.2 9.4 %weight_gradient.9 = (bf16[4,48,1280]{2,1,0:T(8,128)(2,1)}, bf16[4,48,1280]{2,1,0:T(8,128)(2,1)}, bf16[4,48,1280]{2,1,0:T(8,128)(2,1)}, bf16[2,48,1280]{2,1,0:T(8,128)(2,1)}, bf16[2,48,1280]{2,1,0:T(8,128)(2,1)}) custom-call(s32[10]{0:T(128)} %concatenate.45.info, bf16[48,1536]{1,0:T(8,128)(2,1)} %copy-done.22, bf16[1536,768]{1,0:T(8,128)(2,1)} %refs_1_.7, ...), custom_call_target="tpu_custom_call" | custom-call | flops 3019898 | bytes 12000 | tf_op jit(solution)/shard_map/weight_gradient/pallas_call | solution.py:477
  262.2 1.1 add_convert_fusion.1.refs_2_
  265.3 1.3 collective-permute-start.40
  268.4 1.2 collective-permute-start.33
  269.6 14.2 %token_gradient.1 = f32[1536,768]{1,0:T(8,128)} custom-call(s32[10]{0:T(128)} %concatenate.45.info, bf16[4,48,1280]{2,1,0:T(8,128)(2,1)} %get-tuple-element.106.refs_0_, bf16[2,48,1920]{2,1,0:T(8,128)(2,1)} %copy-done.11, bf16[2,48,1920]{2,1,0:T(8,128)(2,1)} %copy-done.10, bf16[1,1536,1152]{2,1,0:T(8,128)(2,1)} %get-tuple-element.95.refs_2_.refs_3_, ...), custom_call_target="tpu_custom_call" | custom-call | flops 5435817 | bytes 20000 | tf_op jit(solution)/shard_map/token_gradient/pallas_call | solution.py:477
  284.0 1.5 add_convert_fusion
  285.5 2.5 collective-permute-start.43
  288.0 6.8 %collective-permute-start.44 = (bf16[48,1920]{1,0:T(8,128)(2,1)S(1)}, bf16[48,1920]{1,0:T(8,128)(2,1)S(1)}, u32[]{:S(2)}, u32[]{:S(2)}) collective-permute-start(bf16[48,1920]{1,0:T(8,128)(2,1)S(1)} %get-tuple-element.145), channel_id=1, source_target_pairs={{0,24},{1,25},{2,26},{3,27},{4,28},{5,29},{6,30},{7,31},{8,16},{9,... | collective-permute-start | bytes 552968 | tf_op jit(solution)/shard_map/ppermute | solution.py:698
  296.3 7.3 %collective-permute-done.44 = bf16[48,1920]{1,0:T(8,128)(2,1)S(1)} collective-permute-done((bf16[48,1920]{1,0:T(8,128)(2,1)S(1)}, bf16[48,1920]{1,0:T(8,128)(2,1)S(1)}, u32[]{:S(2)}, u32[]{:S(2)}) %collective-permute-start.44) | collective-permute-done | bytes 184352 | tf_op jit(solution)/shard_map/ppermute | solution.py:698
  305.3 7.0 %collective-permute-done.34 = bf16[2,48,1280]{2,1,0:T(8,128)(2,1)S(1)} collective-permute-done((bf16[2,48,1280]{2,1,0:T(8,128)(2,1)S(1)}, bf16[2,48,1280]{2,1,0:T(8,128)(2,1)S(1)}, u32[]{:S(2)}, u32[]{:S(2)}) %collective-permute-start.34) | collective-permute-done | bytes 245792 | tf_op jit(solution)/shard_map/ppermute | solution.py:698
  312.5 3.7 %collective-permute-start.37 = (bf16[48,1280]{1,0:T(8,128)(2,1)S(1)}, bf16[48,1280]{1,0:T(8,128)(2,1)S(1)}, u32[]{:S(2)}, u32[]{:S(2)}) collective-permute-start(bf16[48,1280]{1,0:T(8,128)(2,1)S(1)} %get-tuple-element.150), channel_id=1, source_target_pairs={{0,16},{1,17},{2,18},{3,19},{4,20},{5,21},{6,22},{7,23},{8,24},{9,... | collective-permute-start | bytes 368648 | tf_op jit(solution)/shard_map/ppermute | solution.py:698
  316.2 1.1 collective-permute-start.38
  317.7 7.9 %collective-permute-done.37 = bf16[48,1280]{1,0:T(8,128)(2,1)S(1)} collective-permute-done((bf16[48,1280]{1,0:T(8,128)(2,1)S(1)}, bf16[48,1280]{1,0:T(8,128)(2,1)S(1)}, u32[]{:S(2)}, u32[]{:S(2)}) %collective-permute-start.37) | collective-permute-done | bytes 122912 | tf_op jit(solution)/shard_map/ppermute | solution.py:698
  (197 shorter events, 31.0 us)
Async XLA Ops:
  7.2 93.6 %all-gather.2.cloned.1.call-start = ((), (), s32[]{:S(2)}) async-start(), calls=%async_computation | async-start | bytes 4866048 | tf_op jit(solution)/shard_map/all_gather | solution.py:862
  12.8 8.9 %collective-permute-start.2 = (bf16[48,1280]{1,0:T(8,128)(2,1)S(1)}, bf16[48,1280]{1,0:T(8,128)(2,1)S(1)}, u32[]{:S(2)}, u32[]{:S(2)}) collective-permute-start(bf16[48,1280]{1,0:T(8,128)(2,1)S(1)} %maximum_select_fusion.1), channel_id=1, source_target_pairs={{0,8},{1,9},{2,10},{3,11},{4,12},{5,13},{6,14},{7,15},{8,16},{9,17... | collective-permute-start | bytes 368648 | tf_op jit(solution)/shard_map/ppermute | solution.py:698
  15.4 11.4 %collective-permute-start.3 = (bf16[48,1280]{1,0:T(8,128)(2,1)S(1)}, bf16[48,1280]{1,0:T(8,128)(2,1)S(1)}, u32[]{:S(2)}, u32[]{:S(2)}) collective-permute-start(bf16[48,1280]{1,0:T(8,128)(2,1)S(1)} %maximum_select_fusion.1), channel_id=1, source_target_pairs={{0,16},{1,17},{2,18},{3,19},{4,20},{5,21},{6,22},{7,23},{8,24},{9,... | collective-permute-start | bytes 368648 | tf_op jit(solution)/shard_map/ppermute | solution.py:698
  18.0 8.8 %collective-permute-start.4 = (bf16[48,1280]{1,0:T(8,128)(2,1)S(1)}, bf16[48,1280]{1,0:T(8,128)(2,1)S(1)}, u32[]{:S(2)}, u32[]{:S(2)}) collective-permute-start(bf16[48,1280]{1,0:T(8,128)(2,1)S(1)} %maximum_select_fusion.1), channel_id=1, source_target_pairs={{0,24},{1,25},{2,26},{3,27},{4,28},{5,29},{6,30},{7,31},{8,0},{9,1... | collective-permute-start | bytes 368648 | tf_op jit(solution)/shard_map/ppermute | solution.py:698
  19.4 10.6 %collective-permute-start = (bf16[24,1920]{1,0:T(8,128)(2,1)S(1)}, bf16[24,1920]{1,0:T(8,128)(2,1)S(1)}, u32[]{:S(2)}, u32[]{:S(2)}) collective-permute-start(bf16[24,1920]{1,0:T(8,128)(2,1)S(1)} %get-tuple-element.153), channel_id=1, source_target_pairs={{0,1},{1,0},{2,3},{3,2},{4,5},{5,4},{6,7},{7,6},{8,9},{9,8},{10,11... | collective-permute-start | bytes 276488 | tf_op jit(solution)/shard_map/ppermute | solution.py:698
  26.9 13.1 %collective-permute-start.8 = (bf16[192,1280]{1,0:T(8,128)(2,1)S(1)}, bf16[192,1280]{1,0:T(8,128)(2,1)S(1)}, u32[]{:S(2)}, u32[]{:S(2)}) collective-permute-start(bf16[192,1280]{1,0:T(8,128)(2,1)S(1)} %pad_maximum_fusion.refs_0_.refs_3_.refs_6_), channel_id=1, source_target_pairs={{0,2},{1,3},{2,0},{3,1},{4,6},{5,7},{6,4},{7,5},{8,10},{9,11},{10,... | collective-permute-start | bytes 1474568 | tf_op jit(solution)/shard_map/ppermute | solution.py:698
  28.4 12.8 %collective-permute-start.9 = (bf16[192,1280]{1,0:T(8,128)(2,1)S(1)}, bf16[192,1280]{1,0:T(8,128)(2,1)S(1)}, u32[]{:S(2)}, u32[]{:S(2)}) collective-permute-start(bf16[192,1280]{1,0:T(8,128)(2,1)S(1)} %pad_maximum_fusion.refs_0_.refs_3_.refs_6_), channel_id=1, source_target_pairs={{0,4},{1,5},{2,6},{3,7},{4,0},{5,1},{6,2},{7,3},{8,12},{9,13},{10,... | collective-permute-start | bytes 1474568 | tf_op jit(solution)/shard_map/ppermute | solution.py:698
  30.0 12.7 %collective-permute-start.5 = (bf16[48,1920]{1,0:T(8,128)(2,1)S(1)}, bf16[48,1920]{1,0:T(8,128)(2,1)S(1)}, u32[]{:S(2)}, u32[]{:S(2)}) collective-permute-start(bf16[48,1920]{1,0:T(8,128)(2,1)S(1)} %maximum_select_fusion), channel_id=1, source_target_pairs={{0,8},{1,9},{2,10},{3,11},{4,12},{5,13},{6,14},{7,15},{8,16},{9,17... | collective-permute-start | bytes 552968 | tf_op jit(solution)/shard_map/ppermute | solution.py:698
  34.8 16.2 %collective-permute-start.6 = (bf16[48,1920]{1,0:T(8,128)(2,1)S(1)}, bf16[48,1920]{1,0:T(8,128)(2,1)S(1)}, u32[]{:S(2)}, u32[]{:S(2)}) collective-permute-start(bf16[48,1920]{1,0:T(8,128)(2,1)S(1)} %maximum_select_fusion), channel_id=1, source_target_pairs={{0,16},{1,17},{2,18},{3,19},{4,20},{5,21},{6,22},{7,23},{8,24},{9,... | collective-permute-start | bytes 552968 | tf_op jit(solution)/shard_map/ppermute | solution.py:698
  36.0 16.0 %collective-permute-start.7 = (bf16[48,1920]{1,0:T(8,128)(2,1)S(1)}, bf16[48,1920]{1,0:T(8,128)(2,1)S(1)}, u32[]{:S(2)}, u32[]{:S(2)}) collective-permute-start(bf16[48,1920]{1,0:T(8,128)(2,1)S(1)} %maximum_select_fusion), channel_id=1, source_target_pairs={{0,24},{1,25},{2,26},{3,27},{4,28},{5,29},{6,30},{7,31},{8,0},{9,1... | collective-permute-start | bytes 552968 | tf_op jit(solution)/shard_map/ppermute | solution.py:698
  40.0 13.9 %collective-permute-start.12 = (bf16[192,1280]{1,0:T(8,128)(2,1)S(1)}, bf16[192,1280]{1,0:T(8,128)(2,1)S(1)}, u32[]{:S(2)}, u32[]{:S(2)}) collective-permute-start(bf16[192,1280]{1,0:T(8,128)(2,1)S(1)} %pad_maximum_fusion.refs_0_.refs_3_.refs_6_), channel_id=1, source_target_pairs={{0,1},{1,0},{2,3},{3,2},{4,5},{5,4},{6,7},{7,6},{8,9},{9,8},{10,11... | collective-permute-start | bytes 1474568 | tf_op jit(solution)/shard_map/ppermute | solution.py:698
  41.2 9.8 %collective-permute-start.10 = (bf16[96,1280]{1,0:T(8,128)(2,1)S(1)}, bf16[96,1280]{1,0:T(8,128)(2,1)S(1)}, u32[]{:S(2)}, u32[]{:S(2)}) collective-permute-start(bf16[96,1280]{1,0:T(8,128)(2,1)S(1)} %slice.243), channel_id=1, source_target_pairs={{0,4},{1,5},{2,6},{3,7},{4,0},{5,1},{6,2},{7,3},{8,12},{9,13},{10,... | collective-permute-start | bytes 737288 | tf_op jit(solution)/shard_map/ppermute | solution.py:698
  42.7 9.2 %collective-permute-start.11 = (bf16[96,1280]{1,0:T(8,128)(2,1)S(1)}, bf16[96,1280]{1,0:T(8,128)(2,1)S(1)}, u32[]{:S(2)}, u32[]{:S(2)}) collective-permute-start(bf16[96,1280]{1,0:T(8,128)(2,1)S(1)} %slice.244), channel_id=1, source_target_pairs={{0,2},{1,3},{2,0},{3,1},{4,6},{5,7},{6,4},{7,5},{8,10},{9,11},{10,... | collective-permute-start | bytes 737288 | tf_op jit(solution)/shard_map/ppermute | solution.py:698
  51.0 4.6 %collective-permute-start.15 = (bf16[96,1280]{1,0:T(8,128)(2,1)S(1)}, bf16[96,1280]{1,0:T(8,128)(2,1)}, u32[]{:S(2)}, u32[]{:S(2)}) collective-permute-start(bf16[96,1280]{1,0:T(8,128)(2,1)S(1)} %collective-permute-done.10.refs_6_.refs_9_), channel_id=1, source_target_pairs={{0,1},{1,0},{2,3},{3,2},{4,5},{5,4},{6,7},{7,6},{8,9},{9,8},{10,11... | collective-permute-start | bytes 737288 | tf_op jit(solution)/shard_map/ppermute | solution.py:698
  51.9 3.6 %collective-permute-start.16 = (bf16[96,1280]{1,0:T(8,128)(2,1)S(1)}, bf16[96,1280]{1,0:T(8,128)(2,1)S(1)}, u32[]{:S(2)}, u32[]{:S(2)}) collective-permute-start(bf16[96,1280]{1,0:T(8,128)(2,1)S(1)} %collective-permute-done.11.refs_7_.refs_10_), channel_id=1, source_target_pairs={{0,1},{1,0},{2,3},{3,2},{4,5},{5,4},{6,7},{7,6},{8,9},{9,8},{10,11... | collective-permute-start | bytes 737288 | tf_op jit(solution)/shard_map/ppermute | solution.py:698
  52.0 32.4 %collective-permute-start.19 = (bf16[192,1920]{1,0:T(8,128)(2,1)S(1)}, bf16[192,1920]{1,0:T(8,128)(2,1)}, u32[]{:S(2)}, u32[]{:S(2)}) collective-permute-start(bf16[192,1920]{1,0:T(8,128)(2,1)S(1)} %constant_dynamic-update-slice_fusion.refs_0_.refs_4_), channel_id=1, source_target_pairs={{0,6},{1,7},{2,4},{3,5},{4,2},{5,3},{6,0},{7,1},{8,14},{9,15},{10,... | collective-permute-start | bytes 2211848 | tf_op jit(solution)/shard_map/ppermute | solution.py:698
  53.5 42.7 %collective-permute-start.18 = (bf16[192,1920]{1,0:T(8,128)(2,1)S(1)}, bf16[192,1920]{1,0:T(8,128)(2,1)}, u32[]{:S(2)}, u32[]{:S(2)}) collective-permute-start(bf16[192,1920]{1,0:T(8,128)(2,1)S(1)} %constant_dynamic-update-slice_fusion.refs_0_.refs_4_), channel_id=1, source_target_pairs={{0,4},{1,5},{2,6},{3,7},{4,0},{5,1},{6,2},{7,3},{8,12},{9,13},{10,... | collective-permute-start | bytes 2211848 | tf_op jit(solution)/shard_map/ppermute | solution.py:698
  53.8 42.4 %collective-permute-start.17 = (bf16[192,1920]{1,0:T(8,128)(2,1)S(1)}, bf16[192,1920]{1,0:T(8,128)(2,1)}, u32[]{:S(2)}, u32[]{:S(2)}) collective-permute-start(bf16[192,1920]{1,0:T(8,128)(2,1)S(1)} %constant_dynamic-update-slice_fusion.refs_0_.refs_4_), channel_id=1, source_target_pairs={{0,2},{1,3},{2,0},{3,1},{4,6},{5,7},{6,4},{7,5},{8,10},{9,11},{10,... | collective-permute-start | bytes 2211848 | tf_op jit(solution)/shard_map/ppermute | solution.py:698
  55.5 6.0 %collective-permute-start.13 = (bf16[192,1280]{1,0:T(8,128)(2,1)S(1)}, bf16[192,1280]{1,0:T(8,128)(2,1)S(1)}, u32[]{:S(2)}, u32[]{:S(2)}) collective-permute-start(bf16[192,1280]{1,0:T(8,128)(2,1)S(1)} %collective-permute-done.8.refs_4_.refs_7_), channel_id=1, source_target_pairs={{0,1},{1,0},{2,3},{3,2},{4,5},{5,4},{6,7},{7,6},{8,9},{9,8},{10,11... | collective-permute-start | bytes 1474568 | tf_op jit(solution)/shard_map/ppermute | solution.py:698
  56.3 5.2 %collective-permute-start.14 = (bf16[192,1280]{1,0:T(8,128)(2,1)S(1)}, bf16[192,1280]{1,0:T(8,128)(2,1)}, u32[]{:S(2)}, u32[]{:S(2)}) collective-permute-start(bf16[192,1280]{1,0:T(8,128)(2,1)S(1)} %collective-permute-done.9.refs_5_.refs_8_), channel_id=1, source_target_pairs={{0,1},{1,0},{2,3},{3,2},{4,5},{5,4},{6,7},{7,6},{8,9},{9,8},{10,11... | collective-permute-start | bytes 1474568 | tf_op jit(solution)/shard_map/ppermute | solution.py:698
  84.2 12.5 %collective-permute-start.20 = (bf16[192,1920]{1,0:T(8,128)(2,1)}, bf16[192,1920]{1,0:T(8,128)(2,1)S(1)}, u32[]{:S(2)}, u32[]{:S(2)}) collective-permute-start(bf16[192,1920]{1,0:T(8,128)(2,1)} %copy-done.2), channel_id=1, source_target_pairs={{0,1},{1,0},{2,3},{3,2},{4,5},{5,4},{6,7},{7,6},{8,9},{9,8},{10,11... | collective-permute-start | bytes 2211848 | tf_op jit(solution)/shard_map/ppermute | solution.py:698
  84.3 12.3 %collective-permute-start.23 = (bf16[192,1920]{1,0:T(8,128)(2,1)}, bf16[192,1920]{1,0:T(8,128)(2,1)S(1)}, u32[]{:S(2)}, u32[]{:S(2)}) collective-permute-start(bf16[192,1920]{1,0:T(8,128)(2,1)} %collective-permute-done.19.refs_7_), channel_id=1, source_target_pairs={{0,1},{1,0},{2,3},{3,2},{4,5},{5,4},{6,7},{7,6},{8,9},{9,8},{10,11... | collective-permute-start | bytes 2211848 | tf_op jit(solution)/shard_map/ppermute | solution.py:698
  96.2 2.8 collective-permute-start.22
  96.2 4.5 %collective-permute-start.21 = (bf16[192,1920]{1,0:T(8,128)(2,1)}, bf16[192,1920]{1,0:T(8,128)(2,1)S(1)}, u32[]{:S(2)}, u32[]{:S(2)}) collective-permute-start(bf16[192,1920]{1,0:T(8,128)(2,1)} %collective-permute-done.17.refs_5_), channel_id=1, source_target_pairs={{0,1},{1,0},{2,3},{3,2},{4,5},{5,4},{6,7},{7,6},{8,9},{9,8},{10,11... | collective-permute-start | bytes 2211848 | tf_op jit(solution)/shard_map/ppermute | solution.py:698
  176.9 11.6 %collective-permute-start.24 = (bf16[768,3456]{1,0:T(8,128)(2,1)}, bf16[768,3456]{1,0:T(8,128)(2,1)}, u32[]{:S(2)}, u32[]{:S(2)}) collective-permute-start(bf16[768,3456]{1,0:T(8,128)(2,1)} %weight_gradient.5.refs_0_), channel_id=1, source_target_pairs={{0,1},{1,0},{2,3},{3,2},{4,5},{5,4},{6,7},{7,6},{8,9},{9,8},{10,11... | collective-permute-start | bytes 15925256 | tf_op jit(solution)/shard_map/ppermute | solution.py:698
  197.6 21.9 %collective-permute-start.25 = (bf16[4,48,1536]{2,1,0:T(8,128)(2,1)}, bf16[4,48,1536]{2,1,0:T(8,128)(2,1)S(1)}, u32[]{:S(2)}, u32[]{:S(2)}) collective-permute-start(bf16[4,48,1536]{2,1,0:T(8,128)(2,1)} %get-tuple-element.93), channel_id=1, source_target_pairs={{0,2},{1,3},{2,0},{3,1},{4,6},{5,7},{6,4},{7,5},{8,10},{9,11},{10,... | collective-permute-start | bytes 1769480 | tf_op jit(solution)/shard_map/ppermute | solution.py:698
  197.9 21.6 %collective-permute-start.26 = (bf16[4,48,1536]{2,1,0:T(8,128)(2,1)}, bf16[4,48,1536]{2,1,0:T(8,128)(2,1)S(1)}, u32[]{:S(2)}, u32[]{:S(2)}) collective-permute-start(bf16[4,48,1536]{2,1,0:T(8,128)(2,1)} %get-tuple-element.94), channel_id=1, source_target_pairs={{0,4},{1,5},{2,6},{3,7},{4,0},{5,1},{6,2},{7,3},{8,12},{9,13},{10,... | collective-permute-start | bytes 1769480 | tf_op jit(solution)/shard_map/ppermute | solution.py:698
  219.6 14.0 %collective-permute-start.28 = (bf16[2,48,1536]{2,1,0:T(8,128)(2,1)S(1)}, bf16[2,48,1536]{2,1,0:T(8,128)(2,1)}, u32[]{:S(2)}, u32[]{:S(2)}) collective-permute-start(bf16[2,48,1536]{2,1,0:T(8,128)(2,1)S(1)} %add_convert_fusion.4.refs_2_), channel_id=1, source_target_pairs={{0,4},{1,5},{2,6},{3,7},{4,0},{5,1},{6,2},{7,3},{8,12},{9,13},{10,... | collective-permute-start | bytes 884744 | tf_op jit(solution)/shard_map/ppermute | solution.py:698
  220.4 13.2 %collective-permute-start.27 = (bf16[2,48,1536]{2,1,0:T(8,128)(2,1)S(1)}, bf16[2,48,1536]{2,1,0:T(8,128)(2,1)}, u32[]{:S(2)}, u32[]{:S(2)}) collective-permute-start(bf16[2,48,1536]{2,1,0:T(8,128)(2,1)S(1)} %add_convert_fusion.5.refs_1_), channel_id=1, source_target_pairs={{0,2},{1,3},{2,0},{3,1},{4,6},{5,7},{6,4},{7,5},{8,10},{9,11},{10,... | collective-permute-start | bytes 884744 | tf_op jit(solution)/shard_map/ppermute | solution.py:698
  221.9 29.3 %collective-permute-start.29 = (bf16[768,1152]{1,0:T(8,128)(2,1)S(1)}, bf16[768,1152]{1,0:T(8,128)(2,1)}, u32[]{:S(2)}, u32[]{:S(2)}) collective-permute-start(bf16[768,1152]{1,0:T(8,128)(2,1)S(1)} %copy-done.1), channel_id=1, source_target_pairs={{0,1},{1,0},{2,3},{3,2},{4,5},{5,4},{6,7},{7,6},{8,9},{9,8},{10,11... | collective-permute-start | bytes 5308424 | tf_op jit(solution)/shard_map/ppermute | solution.py:698
  235.0 8.9 %collective-permute-start.47 = (bf16[48,1536]{1,0:T(8,128)(2,1)S(1)}, bf16[48,1536]{1,0:T(8,128)(2,1)S(1)}, u32[]{:S(2)}, u32[]{:S(2)}) collective-permute-start(bf16[48,1536]{1,0:T(8,128)(2,1)S(1)} %get-tuple-element.148), channel_id=1, source_target_pairs={{0,16},{1,17},{2,18},{3,19},{4,20},{5,21},{6,22},{7,23},{8,24},{9,... | collective-permute-start | bytes 442376 | tf_op jit(solution)/shard_map/ppermute | solution.py:698
  238.2 11.7 %collective-permute-start.48 = (bf16[48,1536]{1,0:T(8,128)(2,1)S(1)}, bf16[48,1536]{1,0:T(8,128)(2,1)S(1)}, u32[]{:S(2)}, u32[]{:S(2)}) collective-permute-start(bf16[48,1536]{1,0:T(8,128)(2,1)S(1)} %get-tuple-element.149), channel_id=1, source_target_pairs={{0,24},{1,25},{2,26},{3,27},{4,28},{5,29},{6,30},{7,31},{8,16},{9,... | collective-permute-start | bytes 442376 | tf_op jit(solution)/shard_map/ppermute | solution.py:698
  242.1 8.8 %collective-permute-start.46 = (bf16[48,1536]{1,0:T(8,128)(2,1)S(1)}, bf16[48,1536]{1,0:T(8,128)(2,1)S(1)}, u32[]{:S(2)}, u32[]{:S(2)}) collective-permute-start(bf16[48,1536]{1,0:T(8,128)(2,1)S(1)} %fusion.10.refs_0_), channel_id=1, source_target_pairs={{0,8},{1,9},{2,10},{3,11},{4,12},{5,13},{6,14},{7,15},{8,0},{9,1},... | collective-permute-start | bytes 442376 | tf_op jit(solution)/shard_map/ppermute | solution.py:698
  242.7 18.6 %collective-permute-start.30 = (bf16[4,48,1920]{2,1,0:T(8,128)(2,1)}, bf16[4,48,1920]{2,1,0:T(8,128)(2,1)}, u32[]{:S(2)}, u32[]{:S(2)}) collective-permute-start(bf16[4,48,1920]{2,1,0:T(8,128)(2,1)} %get-tuple-element.108), channel_id=1, source_target_pairs={{0,2},{1,3},{2,0},{3,1},{4,6},{5,7},{6,4},{7,5},{8,10},{9,11},{10,... | collective-permute-start | bytes 2211848 | tf_op jit(solution)/shard_map/ppermute | solution.py:698
  243.8 18.4 %collective-permute-start.31 = (bf16[4,48,1920]{2,1,0:T(8,128)(2,1)}, bf16[4,48,1920]{2,1,0:T(8,128)(2,1)}, u32[]{:S(2)}, u32[]{:S(2)}) collective-permute-start(bf16[4,48,1920]{2,1,0:T(8,128)(2,1)} %get-tuple-element.109), channel_id=1, source_target_pairs={{0,4},{1,5},{2,6},{3,7},{4,0},{5,1},{6,2},{7,3},{8,12},{9,13},{10,... | collective-permute-start | bytes 2211848 | tf_op jit(solution)/shard_map/ppermute | solution.py:698
  251.1 15.5 %collective-permute-start.49 = (f32[24,1536]{1,0:T(8,128)S(1)}, f32[24,1536]{1,0:T(8,128)S(1)}, u32[]{:S(2)}, u32[]{:S(2)}) collective-permute-start(f32[24,1536]{1,0:T(8,128)S(1)} %slice_select_fusion.2), channel_id=1, source_target_pairs={{0,1},{1,0},{2,3},{3,2},{4,5},{5,4},{6,7},{7,6},{8,9},{9,8},{10,11... | collective-permute-start | bytes 442376 | tf_op jit(solution)/shard_map/ppermute | solution.py:698
  263.3 20.6 %collective-permute-start.41 = (bf16[2,48,1920]{2,1,0:T(8,128)(2,1)S(1)}, bf16[2,48,1920]{2,1,0:T(8,128)(2,1)S(1)}, u32[]{:S(2)}, u32[]{:S(2)}) collective-permute-start(bf16[2,48,1920]{2,1,0:T(8,128)(2,1)S(1)} %add_convert_fusion.1.refs_2_), channel_id=1, source_target_pairs={{0,4},{1,5},{2,6},{3,7},{4,0},{5,1},{6,2},{7,3},{8,12},{9,13},{10,... | collective-permute-start | bytes 1105928 | tf_op jit(solution)/shard_map/ppermute | solution.py:698
  265.3 18.7 %collective-permute-start.40 = (bf16[2,48,1920]{2,1,0:T(8,128)(2,1)S(1)}, bf16[2,48,1920]{2,1,0:T(8,128)(2,1)S(1)}, u32[]{:S(2)}, u32[]{:S(2)}) collective-permute-start(bf16[2,48,1920]{2,1,0:T(8,128)(2,1)S(1)} %add_convert_fusion.2.refs_1_), channel_id=1, source_target_pairs={{0,2},{1,3},{2,0},{3,1},{4,6},{5,7},{6,4},{7,5},{8,10},{9,11},{10,... | collective-permute-start | bytes 1105928 | tf_op jit(solution)/shard_map/ppermute | solution.py:698
  267.7 27.7 %collective-permute-start.32 = (bf16[4,48,1280]{2,1,0:T(8,128)(2,1)}, bf16[4,48,1280]{2,1,0:T(8,128)(2,1)S(1)}, u32[]{:S(2)}, u32[]{:S(2)}) collective-permute-start(bf16[4,48,1280]{2,1,0:T(8,128)(2,1)} %get-tuple-element.114), channel_id=1, source_target_pairs={{0,2},{1,3},{2,0},{3,1},{4,6},{5,7},{6,4},{7,5},{8,10},{9,11},{10,... | collective-permute-start | bytes 1474568 | tf_op jit(solution)/shard_map/ppermute | solution.py:698
  268.4 26.9 %collective-permute-start.33 = (bf16[4,48,1280]{2,1,0:T(8,128)(2,1)}, bf16[4,48,1280]{2,1,0:T(8,128)(2,1)S(1)}, u32[]{:S(2)}, u32[]{:S(2)}) collective-permute-start(bf16[4,48,1280]{2,1,0:T(8,128)(2,1)} %get-tuple-element.115), channel_id=1, source_target_pairs={{0,4},{1,5},{2,6},{3,7},{4,0},{5,1},{6,2},{7,3},{8,12},{9,13},{10,... | collective-permute-start | bytes 1474568 | tf_op jit(solution)/shard_map/ppermute | solution.py:698
  285.5 10.8 %collective-permute-start.43 = (bf16[48,1920]{1,0:T(8,128)(2,1)S(1)}, bf16[48,1920]{1,0:T(8,128)(2,1)S(1)}, u32[]{:S(2)}, u32[]{:S(2)}) collective-permute-start(bf16[48,1920]{1,0:T(8,128)(2,1)S(1)} %get-tuple-element.144), channel_id=1, source_target_pairs={{0,16},{1,17},{2,18},{3,19},{4,20},{5,21},{6,22},{7,23},{8,24},{9,... | collective-permute-start | bytes 552968 | tf_op jit(solution)/shard_map/ppermute | solution.py:698
  288.0 15.6 %collective-permute-start.44 = (bf16[48,1920]{1,0:T(8,128)(2,1)S(1)}, bf16[48,1920]{1,0:T(8,128)(2,1)S(1)}, u32[]{:S(2)}, u32[]{:S(2)}) collective-permute-start(bf16[48,1920]{1,0:T(8,128)(2,1)S(1)} %get-tuple-element.145), channel_id=1, source_target_pairs={{0,24},{1,25},{2,26},{3,27},{4,28},{5,29},{6,30},{7,31},{8,16},{9,... | collective-permute-start | bytes 552968 | tf_op jit(solution)/shard_map/ppermute | solution.py:698
  294.8 8.8 %collective-permute-start.42 = (bf16[48,1920]{1,0:T(8,128)(2,1)S(1)}, bf16[48,1920]{1,0:T(8,128)(2,1)S(1)}, u32[]{:S(2)}, u32[]{:S(2)}) collective-permute-start(bf16[48,1920]{1,0:T(8,128)(2,1)S(1)} %fusion.9), channel_id=1, source_target_pairs={{0,8},{1,9},{2,10},{3,11},{4,12},{5,13},{6,14},{7,15},{8,0},{9,1},... | collective-permute-start | bytes 552968 | tf_op jit(solution)/shard_map/ppermute | solution.py:698
  295.5 9.8 %collective-permute-start.35 = (bf16[2,48,1280]{2,1,0:T(8,128)(2,1)S(1)}, bf16[2,48,1280]{2,1,0:T(8,128)(2,1)S(1)}, u32[]{:S(2)}, u32[]{:S(2)}) collective-permute-start(bf16[2,48,1280]{2,1,0:T(8,128)(2,1)S(1)} %add_convert_fusion.7), channel_id=1, source_target_pairs={{0,4},{1,5},{2,6},{3,7},{4,0},{5,1},{6,2},{7,3},{8,12},{9,13},{10,... | collective-permute-start | bytes 737288 | tf_op jit(solution)/shard_map/ppermute | solution.py:698
  303.9 8.4 %collective-permute-start.34 = (bf16[2,48,1280]{2,1,0:T(8,128)(2,1)S(1)}, bf16[2,48,1280]{2,1,0:T(8,128)(2,1)S(1)}, u32[]{:S(2)}, u32[]{:S(2)}) collective-permute-start(bf16[2,48,1280]{2,1,0:T(8,128)(2,1)S(1)} %add_convert_fusion.8), channel_id=1, source_target_pairs={{0,2},{1,3},{2,0},{3,1},{4,6},{5,7},{6,4},{7,5},{8,10},{9,11},{10,... | collective-permute-start | bytes 737288 | tf_op jit(solution)/shard_map/ppermute | solution.py:698
  312.5 13.2 %collective-permute-start.37 = (bf16[48,1280]{1,0:T(8,128)(2,1)S(1)}, bf16[48,1280]{1,0:T(8,128)(2,1)S(1)}, u32[]{:S(2)}, u32[]{:S(2)}) collective-permute-start(bf16[48,1280]{1,0:T(8,128)(2,1)S(1)} %get-tuple-element.150), channel_id=1, source_target_pairs={{0,16},{1,17},{2,18},{3,19},{4,20},{5,21},{6,22},{7,23},{8,24},{9,... | collective-permute-start | bytes 368648 | tf_op jit(solution)/shard_map/ppermute | solution.py:698
  316.2 9.5 %collective-permute-start.38 = (bf16[48,1280]{1,0:T(8,128)(2,1)S(1)}, bf16[48,1280]{1,0:T(8,128)(2,1)S(1)}, u32[]{:S(2)}, u32[]{:S(2)}) collective-permute-start(bf16[48,1280]{1,0:T(8,128)(2,1)S(1)} %get-tuple-element.151), channel_id=1, source_target_pairs={{0,24},{1,25},{2,26},{3,27},{4,28},{5,29},{6,30},{7,31},{8,16},{9,... | collective-permute-start | bytes 368648 | tf_op jit(solution)/shard_map/ppermute | solution.py:698
  317.4 8.8 %collective-permute-start.36 = (bf16[48,1280]{1,0:T(8,128)(2,1)S(1)}, bf16[48,1280]{1,0:T(8,128)(2,1)S(1)}, u32[]{:S(2)}, u32[]{:S(2)}) collective-permute-start(bf16[48,1280]{1,0:T(8,128)(2,1)S(1)} %fusion.11), channel_id=1, source_target_pairs={{0,8},{1,9},{2,10},{3,11},{4,12},{5,13},{6,14},{7,15},{8,0},{9,1},... | collective-permute-start | bytes 368648 | tf_op jit(solution)/shard_map/ppermute | solution.py:698
  (36 other events, 459.3 us)
Sparse Core Ops, SparseCore 0:
  11.6 89.2 all-gather.1

commit v3 on v2

--- a/solution.py
+++ b/solution.py
@@ -155,7 +155,7 @@
                 a_ref[:, lo : lo + 128] = (first + part).astype(bf16)
 
 
-def attention_backward(pairs, info, qkv_ref, da_ref, p_ref, out_ref, sums_ref):
+def attention_backward(pairs, info, qkv_ref, da_ref, p_ref, out_ref, sums_ref, keep=None):
     half_width = pairs * 128
     lane = lax.broadcasted_iota(jnp.int32, (1, 128), 1)
     sides = (
@@ -200,6 +200,9 @@
                     lo = part * half_width + p * 128
                     rounded = total[part].astype(bf16)
                     out_ref[0, :, lo : lo + 128] = rounded
+                    if keep is not None:
+                        rows = pl.ds(pl.program_id(0) * rounded.shape[0], rounded.shape[0])
+                        keep[part, rows, p * 128 : (p + 1) * 128] = rounded
                     if part != 1:
                         sums_ref[:, lo : lo + 128] += fold_rows(rounded.astype(f32))
 
@@ -387,7 +390,6 @@
     return rows + [total(sums_ref[i]) for i in (2, 0, 1, 3, 4, 5, 6, 7, 8, 9)]
 
 
-DIRECT = tuple([(a, k) for k in range(4)] for a in range(4))
 RELAYED = (
     [(0, k) for k in range(4)],
     [(3, 0), (3, 1), (1, 0), (1, 1)],
@@ -397,7 +399,46 @@
 )
 
 
-def weight_gradient(starts, sizes, has_recv, buffers, has_ext, info, *refs):
+def store_parts(info, value, outs, acc, recv, buffers):
+    size = value.shape[1]
+    if buffers is None:
+        outs[0][:, :size] = value.astype(outs[0].dtype)
+        return
+    acc[:, :size] = value
+    for out, slots in zip(outs, buffers):
+        for j, (a, k) in enumerate(slots):
+            row = chip_row(info, a, k, True)
+            mine = acc[pl.ds(row, 48), :size]
+            if recv is not None:
+                mine = mine + recv[pl.ds(row, 48), :size].astype(f32)
+            out[j, :, :size] = mine.astype(bf16)
+
+
+def attention_weight(pairs, crops, buffers, info, qkv_ref, da_ref, p_ref, x_ref, *refs):
+    if buffers is not None:
+        recv, all_sums_ref, other_ref, spread_ref, pick_ref, *refs = refs
+    out_ref, sums_ref, *outs, keep, acc = refs
+    step = pl.program_id(0)
+
+    @pl.when(step < crops)
+    def _():
+        attention_backward(pairs, info, qkv_ref, da_ref, p_ref, out_ref, sums_ref, keep)
+
+    @pl.when((step >= crops) & (step < crops + 3))
+    def _():
+        value = mm_tn(x_ref[...], keep[jnp.clip(step - crops, 0, 2)])
+        store_parts(info, value, outs, acc, None if buffers is None else recv, buffers)
+
+    if buffers is not None:
+
+        @pl.when(step == crops + 3)
+        def _():
+            rows = vector_rows(info, all_sums_ref, other_ref, sums_ref)
+            picked = jnp.concatenate([(r * pick_ref[...]).astype(bf16) for r in rows], axis=0)
+            store_parts(info, mm_nt(picked, spread_ref[...]), outs, acc, None, buffers)
+
+
+def weight_gradient(starts, sizes, has_recv, buffers, info, *refs):
     count = len(starts)
     lhs = refs[:count]
     rhs = refs[count : 2 * count]
@@ -406,46 +447,22 @@
     if has_recv:
         recv = refs[at]
         at += 1
-    if has_ext:
-        sums_ref, other_ref, mine_ref, spread_ref, pick_ref = refs[at : at + 5]
-        at += 5
     (*outs, acc) = refs[at:]
     step = pl.program_id(0)
 
     def store(value, add):
-        size = value.shape[1]
-        if buffers is None:
-            outs[0][:, :size] = value.astype(outs[0].dtype)
-            return
-        acc[:, :size] = value
-        for out, slots in zip(outs, buffers):
-            for j, (a, k) in enumerate(slots):
-                row = chip_row(info, a, k, True)
-                mine = acc[pl.ds(row, 48), :size]
-                if add:
-                    mine = mine + recv[pl.ds(row, 48), :size].astype(f32)
-                out[j, :, :size] = mine.astype(bf16)
+        store_parts(info, value, outs, acc, recv if add else None, buffers)
 
     for number, start in enumerate(starts):
         here = step >= start
         if number + 1 < count:
             here = here & (step < starts[number + 1])
-        elif has_ext:
-            here = here & (step < pl.num_programs(0) - 1)
 
         @pl.when(here)
         def _(number=number):
             right = rhs[number]
             right = right[0] if len(right.shape) == 3 else right[...]
             store(mm_tn(lhs[number][...], right), True)
-
-    if has_ext:
-
-        @pl.when(step == pl.num_programs(0) - 1)
-        def _():
-            rows = vector_rows(info, sums_ref, other_ref, mine_ref)
-            picked = jnp.concatenate([(r * pick_ref[...]).astype(bf16) for r in rows], axis=0)
-            store(mm_nt(picked, spread_ref[...]), False)
 
 
 def params():
@@ -571,6 +588,58 @@
     )(info, qkv, da, probs)
 
 
+def run_attention_weight(info, qkv, da, probs, x, crops, which, more, after):
+    _, rows, columns = qkv.shape
+    width = x.shape[1]
+    slots = rows // crops
+    half = columns // 3
+    pick = lambda info: info[0] if which else 1 - info[0]
+    crop = lambda i: jnp.minimum(i, crops - 1)
+    part = lambda i, last: jnp.clip(i - crops, 0, last)
+    in_specs = [
+        pl.BlockSpec((1, slots, columns), lambda i, info: (pick(info), crop(i), 0)),
+        pl.BlockSpec((slots, half), lambda i, info: (crop(i), pick(info))),
+        pl.BlockSpec(
+            (1, 1, H // 2, slots, slots), lambda i, info: (pick(info), crop(i), 0, 0, 0)
+        ),
+        pl.BlockSpec((rows, width), lambda i, info: (0, 0), pipeline_mode=pl.Buffered(1)),
+    ]
+    operands = [qkv, da, probs, x]
+    out_specs = [
+        pl.BlockSpec((1, slots, columns), lambda i, info: (0, crop(i), 0)),
+        whole_block((8, columns)),
+    ]
+    out_shape = [struct((1, rows, columns), bf16), struct((8, columns), f32)]
+    if which:
+        recv, sums, other = more
+        spread, pick_rows = spread_tables(width)
+        rest = [sums, other, jnp.asarray(spread, bf16), jnp.asarray(pick_rows, f32)]
+        operands += [recv] + rest
+        in_specs.append(pl.BlockSpec((width, half), lambda i, info: (0, part(i, 2))))
+        in_specs += [whole_block(v.shape) for v in rest]
+        out_specs += [
+            pl.BlockSpec((len(b), 48, half), lambda i, info: (0, 0, part(i, 3))) for b in RELAYED
+        ]
+        out_shape += [struct((len(b), 48, columns + EXT), bf16) for b in RELAYED]
+    else:
+        out_specs.append(pl.BlockSpec((width, half), lambda i, info: (0, part(i, 2))))
+        out_shape.append(struct((width, columns), bf16))
+    kernel = functools.partial(attention_weight, half // 128, crops, RELAYED if which else None)
+    out = call(
+        kernel,
+        (crops + 3 + which,),
+        in_specs,
+        out_specs,
+        out_shape,
+        [pltpu.VMEM((3, rows, half), bf16), pltpu.VMEM((width, half), f32)],
+        16 * rows * slots * half + 2 * rows * width * columns,
+        20e6,
+        "attention_weight",
+        after,
+    )(info, *operands)
+    return out[0], out[1], out[2:]
+
+
 def run_feed(info, vec, x, attended, cot, pieces_a, pieces_b, block, sub, after):
     rows, width = x.shape
     ff = 2 * pieces_b[0].shape[-1]
@@ -624,7 +693,7 @@
     )(info, *dqkv_by, dr1, *pieces)
 
 
-def run_weight_gradient(info, pairs, columns, block, pick, recv, ext, full, after, buffers=None):
+def run_weight_gradient(info, pairs, columns, block, pick, recv, full, after, buffers=None):
     rows, width = pairs[0][0].shape
     once = pl.Buffered(1)
     starts, sizes, step = [], [], 0
@@ -656,12 +725,6 @@
         specs.append(
             pl.BlockSpec((width, block), lambda i, info: (0, base + jnp.minimum(i, last)))
         )
-    if ext is not None:
-        spread, pick_rows = spread_tables(width)
-        more = list(ext) + [jnp.asarray(spread, bf16), jnp.asarray(pick_rows, f32)]
-        operands += more
-        specs += [whole_block(v.shape) for v in more]
-        step += 1
     if recv is None:
         out_specs = [pl.BlockSpec((width, block), lambda i, info: (0, i))]
         out_shape = [struct((width, columns), f32 if full else bf16)]
@@ -671,7 +734,7 @@
         ]
         out_shape = [struct((len(b), 48, columns), bf16) for b in buffers]
     kernel = functools.partial(
-        weight_gradient, tuple(starts), tuple(sizes), recv is not None, buffers, ext is not None
+        weight_gradient, tuple(starts), tuple(sizes), recv is not None, buffers
     )
     return call(
         kernel,
@@ -732,25 +795,33 @@
     return lax.optimization_barrier((value,) + others)[0]
 
 
-def sum_first(parts, n, *gates):
+def sum_first(chunks, n, *gates):
     flips, _ = neighbours(n)
-    got_x, got_y = send(parts[1], flips["x"]), send(parts[2], flips["y"])
-    got_x, got_y = lax.optimization_barrier((got_x, got_y) + gates)[:2]
-    to_x = (parts[3].astype(f32) + got_y[:2].astype(f32)).astype(bf16)
-    to_y = (parts[4].astype(f32) + got_x[:2].astype(f32)).astype(bf16)
-    return got_x, got_y, to_x, to_y
-
-
-def sum_rest(parts, first, n, *gates):
+    got = [(send(parts[1], flips["x"]), send(parts[2], flips["y"])) for parts in chunks]
+    got = lax.optimization_barrier((got,) + gates)[0]
+    beside = lambda values: jnp.concatenate(values, axis=2).astype(bf16)
+    to_x = beside(
+        [p[3].astype(f32) + got_y[:2].astype(f32) for p, (_, got_y) in zip(chunks, got)]
+    )
+    to_y = beside(
+        [p[4].astype(f32) + got_x[:2].astype(f32) for p, (got_x, _) in zip(chunks, got)]
+    )
+    return got, to_x, to_y
+
+
+def sum_rest(chunks, first, n, *gates):
     flips, _ = neighbours(n)
-    got_x, got_y, to_x, to_y = first
+    got, to_x, to_y = first
     rest_x, rest_y = send(to_x, flips["x"]), send(to_y, flips["y"])
-    got_x, got_y, rest_x, rest_y = lax.optimization_barrier(
-        (got_x, got_y, rest_x, rest_y) + gates
-    )[:4]
-    low = parts[0][:2].astype(f32) + got_x[2:].astype(f32) + rest_y.astype(f32)
-    high = parts[0][2:].astype(f32) + got_y[2:].astype(f32) + rest_x.astype(f32)
-    return [low[0]] + [v.astype(bf16) for v in (low[1], high[0], high[1])]
+    got, rest_x, rest_y = lax.optimization_barrier((got, rest_x, rest_y) + gates)[:3]
+    beside = lambda values: jnp.concatenate(values, axis=2)
+    low = beside(
+        [p[0][:2].astype(f32) + got_x[2:].astype(f32) for p, (got_x, _) in zip(chunks, got)]
+    ) + rest_y.astype(f32)
+    high = beside(
+        [p[0][2:].astype(f32) + got_y[2:].astype(f32) for p, (_, got_y) in zip(chunks, got)]
+    ) + rest_x.astype(f32)
+    return [low[0]] + [v.astype(bf16) for v in (low[1], high[0], high[1])], rest_x
 
 
 def share_rows(core, done, n):
@@ -762,12 +833,18 @@
     return jnp.where(core == 0, keep, got), jnp.where(core == 0, got, keep)
 
 
-def sum_along(total, n):
+def sum_to_owner(total, ways, n, *gates):
     flips, _ = neighbours(n)
-    done = total[0]
-    for value, way in zip(total[1:], ("z", "zz", "zzz")):
-        done = done + send(value, flips[way]).astype(f32)
-    return done
+    got = [send(value, flips[way]) for value, way in zip(total[1:], ways)]
+    got = lax.optimization_barrier((got,) + gates)[0]
+    return total[0] + sum(v.astype(f32) for v in got)
+
+
+def sum_by_halves(total, n):
+    flips, _ = neighbours(n)
+    got = send(jnp.stack([total[1], total[3]]), flips["z"]).astype(f32)
+    far = send((total[2].astype(f32) + got[1]).astype(bf16), flips["zz"])
+    return total[0] + got[0] + far.astype(f32), far
 
 
 def halves(matrix, groups):
@@ -860,13 +937,7 @@
         p_mixed = across_direct(behind(base_mixed, *p_qkv), n)
         p_qkv = both_cores(p_qkv, n)
         p_down = [lax.all_gather(jnp.stack(down_halves), "dp", axis=1, tiled=True)]
-        deltas = run_momentum(
-            info,
-            (w_qkv, w_out, w_in, w_down, vector.reshape(1, -1)),
-            (key_qkv, key_out, key_in, key_down, key_vector.reshape(1, -1)),
-            (base,),
-        )
-        order = [base_mixed, deltas[0]]
+        order = [base_mixed]
         vec = None
     else:
         everywhere = lambda pair: [
@@ -883,57 +954,79 @@
 
     vec, qkv, probs, attended = run_attention_forward(info, tokens, p_qkv, vec, crops, order)
     if near:
-        p_mixed = both_cores([behind(v, attended) for v in p_mixed], n)
+        deltas = run_momentum(
+            info,
+            (w_qkv, w_out, w_in, w_down, vector.reshape(1, -1)),
+            (key_qkv, key_out, key_in, key_down, key_vector.reshape(1, -1)),
+            (attended,),
+        )
+        p_mixed = both_cores([behind(v, deltas[0]) for v in p_mixed], n)
     output, active, du, n1, df, db, da, dr1, sums = run_feed(
-        info, vec, tokens, attended, cotangent, p_mixed, p_down, 512, 256, ()
+        info, vec, tokens, attended, cotangent, p_mixed, p_down, 512, 256, (deltas[0],)
     )
     down_pairs = [(df, active, ff // 2, width)]
     mixed_pairs = [(n1, du, ff // 2, width), (attended, db, half, half)]
     if near:
         flips, _ = neighbours(n)
 
-        def away(pairs, columns, block, after):
+        def mine(pairs, columns, base, after):
             return run_weight_gradient(
-                info, pairs, columns, block, lambda info: 1 - info[0], None, None, False, after
-            )[0]
-
-        def mine(pairs, columns, block, got, ext, after, buffers=RELAYED):
-            return run_weight_gradient(
-                info, pairs, columns, block, lambda info: info[0], got, ext, False, after, buffers
+                info,
+                pairs,
+                columns,
+                width,
+                lambda info: info[0],
+                (got_ff, base),
+                False,
+                after,
+                RELAYED,
             )
 
-        away_ff = away(down_pairs + mixed_pairs, half + ff, width, ())
+        away_ff = run_weight_gradient(
+            info,
+            down_pairs + mixed_pairs,
+            half + ff,
+            width,
+            lambda info: 1 - info[0],
+            None,
+            False,
+            (),
+        )[0]
         got_ff = send(away_ff, flips["core"])
-        dqkv_other, sums_other = run_attention_backward(
-            info, qkv, da, probs, crops, 0, (away_ff,)
+        dqkv_other, sums_other, (away_qkv,) = run_attention_weight(
+            info, qkv, da, probs, tokens, crops, 0, None, (away_ff,)
         )
-        parts_down = mine(down_pairs, ff // 2, width, (got_ff, 0), None, (sums_other,))
-        qkv_pairs = lambda dqkv: [(tokens, dqkv, 3 * half, half)]
-        away_qkv = away(qkv_pairs(dqkv_other), 3 * half, half, (parts_down[0],))
         got_qkv = send(away_qkv, flips["core"])
-        parts_mixed = mine(
-            mixed_pairs, half + ff // 2, width, (got_ff, ff // 2 // width), None, (away_qkv,)
+        parts_down = mine(down_pairs, ff // 2, 0, (sums_other,))
+        parts_mixed = mine(mixed_pairs, half + ff // 2, ff // 2 // width, (parts_down[0],))
+        first_down = sum_first([parts_down], n, parts_mixed[0])
+        dqkv_mine, sums_mine, parts_qkv = run_attention_weight(
+            info,
+            qkv,
+            da,
+            probs,
+            tokens,
+            crops,
+            1,
+            (got_qkv, sums, sums_other),
+            (parts_mixed[0],) + first_down[1:],
         )
-        first_down = sum_first(parts_down, n, parts_mixed[0])
-        dqkv_mine, sums_mine = run_attention_backward(
-            info, qkv, da, probs, crops, 1, (parts_mixed[0],) + first_down[2:]
+        first_mixed = sum_first([parts_mixed], n, sums_mine)
+        total_down, _ = sum_rest([parts_down], first_down, n, sums_mine)
+        total_mixed, arrived = sum_rest([parts_mixed], first_mixed, n)
+        first_qkv = sum_first([parts_qkv], n, arrived)
+        grad_tokens = run_token_gradient(
+            info, [dqkv_other, dqkv_mine], dr1, p_qkv, 256, first_qkv[1:]
         )
-        total_down = sum_rest(parts_down, first_down, n, sums_mine)
-        sums_all = (sums, sums_other, sums_mine)
-        parts_qkv = mine(
-            qkv_pairs(dqkv_mine), 3 * half + EXT, half, (got_qkv, 0), sums_all, (total_down[1],)
-        )
-        first_mixed = sum_first(parts_mixed, n, parts_qkv[0])
-        grad_tokens = run_token_gradient(
-            info, [dqkv_other, dqkv_mine], dr1, p_qkv, 256, (parts_qkv[0],) + first_mixed[2:]
-        )
-        total_mixed = sum_rest(parts_mixed, first_mixed, n, grad_tokens)
-        first_qkv = sum_first(parts_qkv, n, grad_tokens)
-        g_down = share_rows(core, sum_along(total_down, n), n)
-        g_mixed = share_rows(core, sum_along(total_mixed, n), n)
+        total_qkv, _ = sum_rest([parts_qkv], first_qkv, n, grad_tokens)
+        done_down, _ = sum_by_halves(total_down, n)
+        done_mixed, last = sum_by_halves(total_mixed, n)
+        done_qkv = sum_to_owner(total_qkv, ("z", "zz", "zzz"), n, last)
+        g_down = share_rows(core, done_down, n)
+        g_mixed = share_rows(core, done_mixed, n)
         g_in = [v[:, : ff // 2] for v in g_mixed]
         g_out = [v[:, ff // 2 :] for v in g_mixed]
-        g_qkv = share_rows(core, sum_along(sum_rest(parts_qkv, first_qkv, n), n), n)
+        g_qkv = share_rows(core, done_qkv, n)
         per = vector.shape[0] // w_qkv.shape[0]
         grad_down = join(g_down[0], g_down[1], 1)
         grad_vector = (g_qkv[0] + g_qkv[1])[:, 3 * half : 3 * half + per].reshape(-1)
@@ -943,7 +1036,7 @@
         def gradient(pairs_of, columns, block):
             return [
                 run_weight_gradient(
-                    info, pairs_of(h), columns, block, lambda info, h=h: h, None, None, True, ()
+                    info, pairs_of(h), columns, block, lambda info, h=h: h, None, True, ()
                 )[0]
                 for h in range(2)
             ]

time: 343 us -> 341 us (level)
  starting transfers between devices: 59.1 us -> 47.1 us
  waiting for transfers between devices: 66.4 us -> 72.5 us
  other arithmetic: 7.34 us -> 12.8 us
  Pallas kernels: 176 us -> 171 us
    ppermute x50 -> x48, starting transfers between devices: 59.1 us -> 47.1 us  [send(): return lax.ppermute(value, 'dp', pairs)]
    ppermute x50 -> x48, waiting for transfers between devices: 66.3 us -> 72.5 us  [send(): return lax.ppermute(value, 'dp', pairs)]
    pallas_call x11 -> x9, Pallas kernels: 176 us -> 171 us  [call(): return lambda info, *operands: run(info, *after, *operands)]
    add x3 -> x5, other arithmetic: 0.21 us -> 3.78 us  [the longest x2 2.7 us: sum_rest(): beside([p[0][:2].astype(f32) + got_x[2:].astype(f32) for p, (got_x, _) in...]
    unnamed x72 -> x70, local copies, waits for them, and re-layouts: 4.88 us -> 7.25 us
  transfers between devices with their start and end apart: 51 -> 49, of which waited for: 19 -> 16; matrix products, arithmetic and copies ran while one was open for 4% -> 7% of each run, Pallas kernels for 27% -> 29%
where the time goes in v3:
time: 341 us; the launch traced here: 335 us
  Pallas kernels  171 us (50%)
  waiting for transfers between devices  72.5 us (21%)
  starting transfers between devices  47.1 us (14%)
  local copies, waits for them, and re-layouts  16.5 us (5%)
  between operations  14.9 us (4%)
  other arithmetic  12.8 us (4%)
    pallas_call x9, Pallas kernels, call(): return lambda info, *operands: run(info, *after, *operands)  171 us
    ppermute x48, waiting for transfers between devices, send(): return lax.ppermute(value, 'dp', pairs)  72.5 us
    ppermute x48, starting transfers between devices, send(): return lax.ppermute(value, 'dp', pairs)  47.1 us
    unnamed x70, local copies, waits for them, and re-layouts  7.25 us
  transfers between devices with their start and end apart: 49, of which 16 were waited for; matrix products, arithmetic and copies ran while one was open for 7% of the time, Pallas kernels for 29%

profile of v3, /device:TPU:0, one launch (start us, length us, event | category | flops | bytes accessed | tf_op | source)
XLA Modules:
  0.0 335.3 jit_solution(17144107635505432883)
XLA Ops:
  12.8 4.7 %collective-permute-start.4 = (bf16[48,1280]{1,0:T(8,128)(2,1)S(1)}, bf16[48,1280]{1,0:T(8,128)(2,1)S(1)}, u32[]{:S(2)}, u32[]{:S(2)}) collective-permute-start(bf16[48,1280]{1,0:T(8,128)(2,1)S(1)} %maximum_select_fusion.1), channel_id=1, source_target_pairs={{0,24},{1,25},{2,26},{3,27},{4,28},{5,29},{6,30},{7,31},{8,0},{9,1... | collective-permute-start | bytes 368648 | tf_op jit(solution)/shard_map/ppermute | solution.py:761
  18.6 2.6 collective-permute-done.4
  21.2 9.2 %collective-permute-done.3 = bf16[48,1280]{1,0:T(8,128)(2,1)S(1)} collective-permute-done((bf16[48,1280]{1,0:T(8,128)(2,1)S(1)}, bf16[48,1280]{1,0:T(8,128)(2,1)S(1)}, u32[]{:S(2)}, u32[]{:S(2)}) %collective-permute-start.3) | collective-permute-done | bytes 122912 | tf_op jit(solution)/shard_map/ppermute | solution.py:761
  30.4 1.6 collective-permute-start.9
  32.0 1.9 collective-permute-start.8
  34.5 2.2 collective-permute-start.6
  36.7 1.9 collective-permute-start.5
  39.3 3.9 %collective-permute-done.9.refs_4_.refs_7_ = bf16[192,1280]{1,0:T(8,128)(2,1)S(1)} collective-permute-done((bf16[192,1280]{1,0:T(8,128)(2,1)S(1)}, bf16[192,1280]{1,0:T(8,128)(2,1)S(1)}, u32[]{:S(2)}, u32[]{:S(2)}) %collective-permute-start.9) | collective-permute-done | bytes 491552 | tf_op jit(solution)/shard_map/ppermute | solution.py:761
  43.2 5.5 %collective-permute-done.5 = bf16[48,1920]{1,0:T(8,128)(2,1)S(1)} collective-permute-done((bf16[48,1920]{1,0:T(8,128)(2,1)S(1)}, bf16[48,1920]{1,0:T(8,128)(2,1)S(1)}, u32[]{:S(2)}, u32[]{:S(2)}) %collective-permute-start.5) | collective-permute-done | bytes 184352 | tf_op jit(solution)/shard_map/ppermute | solution.py:761
  50.8 3.8 %collective-permute-done.6 = bf16[48,1920]{1,0:T(8,128)(2,1)S(1)} collective-permute-done((bf16[48,1920]{1,0:T(8,128)(2,1)S(1)}, bf16[48,1920]{1,0:T(8,128)(2,1)S(1)}, u32[]{:S(2)}, u32[]{:S(2)}) %collective-permute-start.6) | collective-permute-done | bytes 184352 | tf_op jit(solution)/shard_map/ppermute | solution.py:761
  55.3 2.2 collective-permute-done.11.refs_6_.refs_9_
  58.2 1.4 collective-permute-start.19
  60.0 1.7 collective-permute-start.17
  65.0 21.7 %attention_forward.1 = (f32[16,768]{1,0:T(8,128)}, bf16[2,1536,1152]{2,1,0:T(8,128)(2,1)}, bf16[2,6,6,256,256]{4,3,2,1,0:T(8,128)(2,1)}, bf16[1536,768]{1,0:T(8,128)(2,1)}) custom-call(s32[10]{0:T(128)} %concatenate.45.info, bf16[192,1920]{1,0:T(8,128)(2,1)} %constant_dynamic-update-slice_fusion.refs_0_.refs_5_, bf16[1536,768]{1,0:T(8,128)(2,1)} %refs_6_.3, ...), custom_call_target="tpu_custom_call" | custom-call | flops 7851737 | bytes 30000 | tf_op jit(solution)/shard_map/attention_forward/pallas_call | solution.py:494
  86.7 3.0 momentum.1
  90.0 12.5 %collective-permute-done.18.refs_7_ = bf16[192,1920]{1,0:T(8,128)(2,1)} collective-permute-done((bf16[192,1920]{1,0:T(8,128)(2,1)}, bf16[192,1920]{1,0:T(8,128)(2,1)}, u32[]{:S(2)}, u32[]{:S(2)}) %collective-permute-start.18) | collective-permute-done | bytes 737312 | tf_op jit(solution)/shard_map/ppermute | solution.py:761
  103.1 1.9 collective-permute-done.21.refs_10_
  105.0 2.1 collective-permute-done.22.refs_11_
  107.1 1.4 collective-permute-done.23.refs_12_
  109.3 59.0 %feed_both.1 = (bf16[1536,768]{1,0:T(8,128)(2,1)}, bf16[1536,3072]{1,0:T(8,128)(2,1)}, bf16[1536,3072]{1,0:T(8,128)(2,1)}, bf16[1536,768]{1,0:T(8,128)(2,1)}, bf...) custom-call(s32[10]{0:T(128)} %concatenate.45.info, ...), custom_call_target="tpu_custom_call" | custom-call | flops 32614908 | bytes 53000 | tf_op jit(solution)/shard_map/feed_both/pallas_call | solution.py:494
  168.3 16.3 %weight_gradient.3.refs_0_ = bf16[768,3456]{1,0:T(8,128)(2,1)} custom-call(s32[10]{0:T(128)} %concatenate.45.info, bf16[1536,768]{1,0:T(8,128)(2,1)} %get-tuple-element.87.refs_0_.refs_1_, bf16[1536,768]{1,0:T(8,128)(2,1)} %get-tuple-element.88.refs_1_, bf16[1536,768]{1,0:T(8,128)(2,1)} %get-tuple-element.78.refs_0_.refs_3_.refs_2_, ...), custom_call_target="tpu_custom_call" | custom-call | flops 8153726 | bytes 12000 | tf_op jit(solution)/shard_map/weight_gradient/pallas_call | solution.py:494
  184.8 17.1 %attention_weight.2 = (bf16[1,1536,1152]{2,1,0:T(8,128)(2,1)}, f32[8,1152]{1,0:T(8,128)}, bf16[768,1152]{1,0:T(8,128)(2,1)}) custom-call(s32[10]{0:T(128)} %concatenate.45.info, bf16[768,3456]{1,0:T(8,128)(2,1)} %weight_gradient.3.refs_0_, bf16[2,1536,1152]{2,1,0:T(8,128)(2,1)} %get-tuple-element.92.refs_1_.refs_3_, ...), custom_call_target="tpu_custom_call" | custom-call | flops 5133828 | bytes 20000 | tf_op jit(solution)/shard_map/attention_weight/pallas_call | solution.py:494
  202.3 9.2 %weight_gradient.4 = (bf16[4,48,1536]{2,1,0:T(8,128)(2,1)}, bf16[4,48,1536]{2,1,0:T(8,128)(2,1)}, bf16[4,48,1536]{2,1,0:T(8,128)(2,1)}, bf16[2,48,1536]{2,1,0:T(8,128)(2,1)}, bf16[2,48,1536]{2,1,0:T(8,128)(2,1)}) custom-call(s32[10]{0:T(128)} %concatenate.45.info, f32[8,1152]{1,0:T(8,128)} %get-tuple-element.95.refs_0_.refs_9_, ...), custom_call_target="tpu_custom_call" | custom-call | flops 3623878 | bytes 12000 | tf_op jit(solution)/shard_map/weight_gradient/pallas_call | solution.py:494
  212.0 1.1 collective-permute-start.26
  213.7 11.8 %weight_gradient.5 = (bf16[4,48,1920]{2,1,0:T(8,128)(2,1)}, bf16[4,48,1920]{2,1,0:T(8,128)(2,1)}, bf16[4,48,1920]{2,1,0:T(8,128)(2,1)}, bf16[2,48,1920]{2,1,0:T(8,128)(2,1)}, bf16[2,48,1920]{2,1,0:T(8,128)(2,1)}) custom-call(s32[10]{0:T(128)} %concatenate.45.info, bf16[4,48,1536]{2,1,0:T(8,128)(2,1)} %get-tuple-element.96.refs_0_, ...), custom_call_target="tpu_custom_call" | custom-call | flops 4529848 | bytes 12000 | tf_op jit(solution)/shard_map/weight_gradient/pallas_call | solution.py:494
  226.6 1.4 collective-permute-start.31
  228.0 1.0 add_convert_fusion.4.refs_2_
  231.9 1.2 copy-done.8
  233.1 19.0 %attention_weight.3 = (bf16[1,1536,1152]{2,1,0:T(8,128)(2,1)}, f32[8,1152]{1,0:T(8,128)}, bf16[4,48,1280]{2,1,0:T(8,128)(2,1)}, bf16[4,48,1280]{2,1,0:T(8,128)(2...) custom-call(s32[10]{0:T(128)} %concatenate.45.info, ...), custom_call_target="tpu_custom_call" | custom-call | flops 5133828 | bytes 20000 | tf_op jit(solution)/shard_map/attention_weight/pallas_call | solution.py:494
  252.1 1.2 collective-permute-start.28
  253.3 1.3 collective-permute-start.29
  254.6 1.2 add_convert_fusion.2
  257.7 1.4 convert_add_fusion.1
  259.2 2.7 collective-permute-start.45
  262.0 10.1 %collective-permute-done.32 = bf16[2,48,1920]{2,1,0:T(8,128)(2,1)S(1)} collective-permute-done((bf16[2,48,1920]{2,1,0:T(8,128)(2,1)S(1)}, bf16[2,48,1920]{2,1,0:T(8,128)(2,1)S(1)}, u32[]{:S(2)}, u32[]{:S(2)}) %collective-permute-start.32) | collective-permute-done | bytes 368672 | tf_op jit(solution)/shard_map/ppermute | solution.py:761
  272.9 1.3 convert_add_fusion
  275.0 2.5 collective-permute-start.39
  279.0 2.8 collective-permute-start.46
  281.9 1.2 collective-permute-start.34
  283.2 14.3 %token_gradient.1 = f32[1536,768]{1,0:T(8,128)} custom-call(s32[10]{0:T(128)} %concatenate.45.info, bf16[2,48,1280]{2,1,0:T(8,128)(2,1)} %copy-done.12, bf16[2,48,1280]{2,1,0:T(8,128)(2,1)} %copy-done.11, bf16[1,1536,1152]{2,1,0:T(8,128)(2,1)} %get-tuple-element.120.refs_2_, bf16[1,1536,1152]{2,1,0:T(8,128)(2,1)} %get-tuple-element.121.refs_3_, ...), custom_call_target="tpu_custom_call" | custom-call | flops 5435817 | bytes 20000 | tf_op jit(solution)/shard_map/token_gradient/pallas_call | solution.py:494
  298.6 1.2 add_convert_fusion.6
  299.8 2.1 collective-permute-start.36
  302.0 1.5 collective-permute-start.37
  303.5 1.0 convert_element_type.209
  304.6 1.6 collective-permute-start.40
  307.2 2.8 collective-permute-done.38
  310.1 9.4 %collective-permute-done.37 = bf16[48,1280]{1,0:T(8,128)(2,1)S(1)} collective-permute-done((bf16[48,1280]{1,0:T(8,128)(2,1)S(1)}, bf16[48,1280]{1,0:T(8,128)(2,1)S(1)}, u32[]{:S(2)}, u32[]{:S(2)}) %collective-permute-start.37) | collective-permute-done | bytes 122912 | tf_op jit(solution)/shard_map/ppermute | solution.py:761
  319.4 3.5 %collective-permute-done.40 = bf16[48,1920]{1,0:T(8,128)(2,1)S(1)} collective-permute-done((bf16[48,1920]{1,0:T(8,128)(2,1)S(1)}, bf16[48,1920]{1,0:T(8,128)(2,1)S(1)}, u32[]{:S(2)}, u32[]{:S(2)}) %collective-permute-start.40) | collective-permute-done | bytes 184352 | tf_op jit(solution)/shard_map/ppermute | solution.py:761
  (195 shorter events, 34.8 us)
Async XLA Ops:
  7.2 101.2 %all-gather.2.cloned.1.call-start = ((), (), s32[]{:S(2)}) async-start(), calls=%async_computation | async-start | bytes 4866048 | tf_op jit(solution)/shard_map/all_gather | solution.py:939
  10.5 2.2 collective-permute-start.1
  12.8 8.4 %collective-permute-start.4 = (bf16[48,1280]{1,0:T(8,128)(2,1)S(1)}, bf16[48,1280]{1,0:T(8,128)(2,1)S(1)}, u32[]{:S(2)}, u32[]{:S(2)}) collective-permute-start(bf16[48,1280]{1,0:T(8,128)(2,1)S(1)} %maximum_select_fusion.1), channel_id=1, source_target_pairs={{0,24},{1,25},{2,26},{3,27},{4,28},{5,29},{6,30},{7,31},{8,0},{9,1... | collective-permute-start | bytes 368648 | tf_op jit(solution)/shard_map/ppermute | solution.py:761
  17.4 13.0 %collective-permute-start.3 = (bf16[48,1280]{1,0:T(8,128)(2,1)S(1)}, bf16[48,1280]{1,0:T(8,128)(2,1)S(1)}, u32[]{:S(2)}, u32[]{:S(2)}) collective-permute-start(bf16[48,1280]{1,0:T(8,128)(2,1)S(1)} %maximum_select_fusion.1), channel_id=1, source_target_pairs={{0,16},{1,17},{2,18},{3,19},{4,20},{5,21},{6,22},{7,23},{8,24},{9,... | collective-permute-start | bytes 368648 | tf_op jit(solution)/shard_map/ppermute | solution.py:761
  17.4 13.0 %collective-permute-start.2 = (bf16[48,1280]{1,0:T(8,128)(2,1)S(1)}, bf16[48,1280]{1,0:T(8,128)(2,1)S(1)}, u32[]{:S(2)}, u32[]{:S(2)}) collective-permute-start(bf16[48,1280]{1,0:T(8,128)(2,1)S(1)} %maximum_select_fusion.1), channel_id=1, source_target_pairs={{0,8},{1,9},{2,10},{3,11},{4,12},{5,13},{6,14},{7,15},{8,16},{9,17... | collective-permute-start | bytes 368648 | tf_op jit(solution)/shard_map/ppermute | solution.py:761
  18.5 15.5 %collective-permute-start = (bf16[24,1920]{1,0:T(8,128)(2,1)S(1)}, bf16[24,1920]{1,0:T(8,128)(2,1)S(1)}, u32[]{:S(2)}, u32[]{:S(2)}) collective-permute-start(bf16[24,1920]{1,0:T(8,128)(2,1)S(1)} %get-tuple-element.157), channel_id=1, source_target_pairs={{0,1},{1,0},{2,3},{3,2},{4,5},{5,4},{6,7},{7,6},{8,9},{9,8},{10,11... | collective-permute-start | bytes 276488 | tf_op jit(solution)/shard_map/ppermute | solution.py:761
  30.4 12.8 %collective-permute-start.9 = (bf16[192,1280]{1,0:T(8,128)(2,1)S(1)}, bf16[192,1280]{1,0:T(8,128)(2,1)S(1)}, u32[]{:S(2)}, u32[]{:S(2)}) collective-permute-start(bf16[192,1280]{1,0:T(8,128)(2,1)S(1)} %pad_maximum_fusion.refs_2_.refs_5_), channel_id=1, source_target_pairs={{0,4},{1,5},{2,6},{3,7},{4,0},{5,1},{6,2},{7,3},{8,12},{9,13},{10,... | collective-permute-start | bytes 1474568 | tf_op jit(solution)/shard_map/ppermute | solution.py:761
  32.0 17.8 %collective-permute-start.8 = (bf16[192,1280]{1,0:T(8,128)(2,1)S(1)}, bf16[192,1280]{1,0:T(8,128)(2,1)S(1)}, u32[]{:S(2)}, u32[]{:S(2)}) collective-permute-start(bf16[192,1280]{1,0:T(8,128)(2,1)S(1)} %pad_maximum_fusion.refs_2_.refs_5_), channel_id=1, source_target_pairs={{0,2},{1,3},{2,0},{3,1},{4,6},{5,7},{6,4},{7,5},{8,10},{9,11},{10,... | collective-permute-start | bytes 1474568 | tf_op jit(solution)/shard_map/ppermute | solution.py:761
  34.0 23.5 %collective-permute-start.7 = (bf16[48,1920]{1,0:T(8,128)(2,1)S(1)}, bf16[48,1920]{1,0:T(8,128)(2,1)S(1)}, u32[]{:S(2)}, u32[]{:S(2)}) collective-permute-start(bf16[48,1920]{1,0:T(8,128)(2,1)S(1)} %maximum_select_fusion), channel_id=1, source_target_pairs={{0,24},{1,25},{2,26},{3,27},{4,28},{5,29},{6,30},{7,31},{8,0},{9,1... | collective-permute-start | bytes 552968 | tf_op jit(solution)/shard_map/ppermute | solution.py:761
  34.5 20.1 %collective-permute-start.6 = (bf16[48,1920]{1,0:T(8,128)(2,1)S(1)}, bf16[48,1920]{1,0:T(8,128)(2,1)S(1)}, u32[]{:S(2)}, u32[]{:S(2)}) collective-permute-start(bf16[48,1920]{1,0:T(8,128)(2,1)S(1)} %maximum_select_fusion), channel_id=1, source_target_pairs={{0,16},{1,17},{2,18},{3,19},{4,20},{5,21},{6,22},{7,23},{8,24},{9,... | collective-permute-start | bytes 552968 | tf_op jit(solution)/shard_map/ppermute | solution.py:761
  36.7 12.0 %collective-permute-start.5 = (bf16[48,1920]{1,0:T(8,128)(2,1)S(1)}, bf16[48,1920]{1,0:T(8,128)(2,1)S(1)}, u32[]{:S(2)}, u32[]{:S(2)}) collective-permute-start(bf16[48,1920]{1,0:T(8,128)(2,1)S(1)} %maximum_select_fusion), channel_id=1, source_target_pairs={{0,8},{1,9},{2,10},{3,11},{4,12},{5,13},{6,14},{7,15},{8,16},{9,17... | collective-permute-start | bytes 552968 | tf_op jit(solution)/shard_map/ppermute | solution.py:761
  43.2 16.8 %collective-permute-start.12 = (bf16[192,1280]{1,0:T(8,128)(2,1)S(1)}, bf16[192,1280]{1,0:T(8,128)(2,1)S(1)}, u32[]{:S(2)}, u32[]{:S(2)}) collective-permute-start(bf16[192,1280]{1,0:T(8,128)(2,1)S(1)} %pad_maximum_fusion.refs_2_.refs_5_), channel_id=1, source_target_pairs={{0,1},{1,0},{2,3},{3,2},{4,5},{5,4},{6,7},{7,6},{8,9},{9,8},{10,11... | collective-permute-start | bytes 1474568 | tf_op jit(solution)/shard_map/ppermute | solution.py:761
  48.7 8.8 %collective-permute-start.11 = (bf16[96,1280]{1,0:T(8,128)(2,1)S(1)}, bf16[96,1280]{1,0:T(8,128)(2,1)S(1)}, u32[]{:S(2)}, u32[]{:S(2)}) collective-permute-start(bf16[96,1280]{1,0:T(8,128)(2,1)S(1)} %slice.260), channel_id=1, source_target_pairs={{0,2},{1,3},{2,0},{3,1},{4,6},{5,7},{6,4},{7,5},{8,10},{9,11},{10,... | collective-permute-start | bytes 737288 | tf_op jit(solution)/shard_map/ppermute | solution.py:761
  49.9 8.4 %collective-permute-start.10 = (bf16[96,1280]{1,0:T(8,128)(2,1)S(1)}, bf16[96,1280]{1,0:T(8,128)(2,1)S(1)}, u32[]{:S(2)}, u32[]{:S(2)}) collective-permute-start(bf16[96,1280]{1,0:T(8,128)(2,1)S(1)} %slice.259), channel_id=1, source_target_pairs={{0,4},{1,5},{2,6},{3,7},{4,0},{5,1},{6,2},{7,3},{8,12},{9,13},{10,... | collective-permute-start | bytes 737288 | tf_op jit(solution)/shard_map/ppermute | solution.py:761
  55.3 6.5 %collective-permute-start.14 = (bf16[192,1280]{1,0:T(8,128)(2,1)S(1)}, bf16[192,1280]{1,0:T(8,128)(2,1)S(1)}, u32[]{:S(2)}, u32[]{:S(2)}) collective-permute-start(bf16[192,1280]{1,0:T(8,128)(2,1)S(1)} %collective-permute-done.9.refs_4_.refs_7_), channel_id=1, source_target_pairs={{0,1},{1,0},{2,3},{3,2},{4,5},{5,4},{6,7},{7,6},{8,9},{9,8},{10,11... | collective-permute-start | bytes 1474568 | tf_op jit(solution)/shard_map/ppermute | solution.py:761
  57.5 4.3 %collective-permute-start.16 = (bf16[96,1280]{1,0:T(8,128)(2,1)S(1)}, bf16[96,1280]{1,0:T(8,128)(2,1)}, u32[]{:S(2)}, u32[]{:S(2)}) collective-permute-start(bf16[96,1280]{1,0:T(8,128)(2,1)S(1)} %collective-permute-done.11.refs_6_.refs_9_), channel_id=1, source_target_pairs={{0,1},{1,0},{2,3},{3,2},{4,5},{5,4},{6,7},{7,6},{8,9},{9,8},{10,11... | collective-permute-start | bytes 737288 | tf_op jit(solution)/shard_map/ppermute | solution.py:761
  58.2 31.8 %collective-permute-start.19 = (bf16[192,1920]{1,0:T(8,128)(2,1)}, bf16[192,1920]{1,0:T(8,128)(2,1)}, u32[]{:S(2)}, u32[]{:S(2)}) collective-permute-start(bf16[192,1920]{1,0:T(8,128)(2,1)} %constant_dynamic-update-slice_fusion.refs_0_.refs_5_), channel_id=1, source_target_pairs={{0,6},{1,7},{2,4},{3,5},{4,2},{5,3},{6,0},{7,1},{8,14},{9,15},{10,... | collective-permute-start | bytes 2211848 | tf_op jit(solution)/shard_map/ppermute | solution.py:761
  59.6 42.9 %collective-permute-start.18 = (bf16[192,1920]{1,0:T(8,128)(2,1)}, bf16[192,1920]{1,0:T(8,128)(2,1)}, u32[]{:S(2)}, u32[]{:S(2)}) collective-permute-start(bf16[192,1920]{1,0:T(8,128)(2,1)} %constant_dynamic-update-slice_fusion.refs_0_.refs_5_), channel_id=1, source_target_pairs={{0,4},{1,5},{2,6},{3,7},{4,0},{5,1},{6,2},{7,3},{8,12},{9,13},{10,... | collective-permute-start | bytes 2211848 | tf_op jit(solution)/shard_map/ppermute | solution.py:761
  60.0 42.5 %collective-permute-start.17 = (bf16[192,1920]{1,0:T(8,128)(2,1)}, bf16[192,1920]{1,0:T(8,128)(2,1)}, u32[]{:S(2)}, u32[]{:S(2)}) collective-permute-start(bf16[192,1920]{1,0:T(8,128)(2,1)} %constant_dynamic-update-slice_fusion.refs_0_.refs_5_), channel_id=1, source_target_pairs={{0,2},{1,3},{2,0},{3,1},{4,6},{5,7},{6,4},{7,5},{8,10},{9,11},{10,... | collective-permute-start | bytes 2211848 | tf_op jit(solution)/shard_map/ppermute | solution.py:761
  61.7 2.4 collective-permute-start.13
  61.8 2.3 collective-permute-start.15
  89.7 13.4 %collective-permute-start.20 = (bf16[192,1920]{1,0:T(8,128)(2,1)}, bf16[192,1920]{1,0:T(8,128)(2,1)S(1)}, u32[]{:S(2)}, u32[]{:S(2)}) collective-permute-start(bf16[192,1920]{1,0:T(8,128)(2,1)} %constant_dynamic-update-slice_fusion.refs_0_.refs_5_), channel_id=1, source_target_pairs={{0,1},{1,0},{2,3},{3,2},{4,5},{5,4},{6,7},{7,6},{8,9},{9,8},{10,11... | collective-permute-start | bytes 2211848 | tf_op jit(solution)/shard_map/ppermute | solution.py:761
  102.5 2.4 collective-permute-start.21
  102.6 4.5 %collective-permute-start.22 = (bf16[192,1920]{1,0:T(8,128)(2,1)}, bf16[192,1920]{1,0:T(8,128)(2,1)S(1)}, u32[]{:S(2)}, u32[]{:S(2)}) collective-permute-start(bf16[192,1920]{1,0:T(8,128)(2,1)} %collective-permute-done.18.refs_7_), channel_id=1, source_target_pairs={{0,1},{1,0},{2,3},{3,2},{4,5},{5,4},{6,7},{7,6},{8,9},{9,8},{10,11... | collective-permute-start | bytes 2211848 | tf_op jit(solution)/shard_map/ppermute | solution.py:761
  103.0 5.4 %collective-permute-start.23 = (bf16[192,1920]{1,0:T(8,128)(2,1)}, bf16[192,1920]{1,0:T(8,128)(2,1)S(1)}, u32[]{:S(2)}, u32[]{:S(2)}) collective-permute-start(bf16[192,1920]{1,0:T(8,128)(2,1)} %collective-permute-done.19.refs_8_), channel_id=1, source_target_pairs={{0,1},{1,0},{2,3},{3,2},{4,5},{5,4},{6,7},{7,6},{8,9},{9,8},{10,11... | collective-permute-start | bytes 2211848 | tf_op jit(solution)/shard_map/ppermute | solution.py:761
  184.6 17.6 %collective-permute-start.24 = (bf16[768,3456]{1,0:T(8,128)(2,1)}, bf16[768,3456]{1,0:T(8,128)(2,1)}, u32[]{:S(2)}, u32[]{:S(2)}) collective-permute-start(bf16[768,3456]{1,0:T(8,128)(2,1)} %weight_gradient.3.refs_0_), channel_id=1, source_target_pairs={{0,1},{1,0},{2,3},{3,2},{4,5},{5,4},{6,7},{7,6},{8,9},{9,8},{10,11... | collective-permute-start | bytes 15925256 | tf_op jit(solution)/shard_map/ppermute | solution.py:761
  201.9 30.0 %collective-permute-start.27 = (bf16[768,1152]{1,0:T(8,128)(2,1)}, bf16[768,1152]{1,0:T(8,128)(2,1)S(1)}, u32[]{:S(2)}, u32[]{:S(2)}) collective-permute-start(bf16[768,1152]{1,0:T(8,128)(2,1)} %get-tuple-element.104), channel_id=1, source_target_pairs={{0,1},{1,0},{2,3},{3,2},{4,5},{5,4},{6,7},{7,6},{8,9},{9,8},{10,11... | collective-permute-start | bytes 5308424 | tf_op jit(solution)/shard_map/ppermute | solution.py:761
  211.5 16.6 %collective-permute-start.25 = (bf16[4,48,1536]{2,1,0:T(8,128)(2,1)}, bf16[4,48,1536]{2,1,0:T(8,128)(2,1)}, u32[]{:S(2)}, u32[]{:S(2)}) collective-permute-start(bf16[4,48,1536]{2,1,0:T(8,128)(2,1)} %get-tuple-element.99), channel_id=1, source_target_pairs={{0,2},{1,3},{2,0},{3,1},{4,6},{5,7},{6,4},{7,5},{8,10},{9,11},{10,... | collective-permute-start | bytes 1769480 | tf_op jit(solution)/shard_map/ppermute | solution.py:761
  212.0 16.0 %collective-permute-start.26 = (bf16[4,48,1536]{2,1,0:T(8,128)(2,1)}, bf16[4,48,1536]{2,1,0:T(8,128)(2,1)}, u32[]{:S(2)}, u32[]{:S(2)}) collective-permute-start(bf16[4,48,1536]{2,1,0:T(8,128)(2,1)} %get-tuple-element.100), channel_id=1, source_target_pairs={{0,4},{1,5},{2,6},{3,7},{4,0},{5,1},{6,2},{7,3},{8,12},{9,13},{10,... | collective-permute-start | bytes 1769480 | tf_op jit(solution)/shard_map/ppermute | solution.py:761
  225.5 27.7 %collective-permute-start.30 = (bf16[4,48,1920]{2,1,0:T(8,128)(2,1)}, bf16[4,48,1920]{2,1,0:T(8,128)(2,1)S(1)}, u32[]{:S(2)}, u32[]{:S(2)}) collective-permute-start(bf16[4,48,1920]{2,1,0:T(8,128)(2,1)} %get-tuple-element.109), channel_id=1, source_target_pairs={{0,2},{1,3},{2,0},{3,1},{4,6},{5,7},{6,4},{7,5},{8,10},{9,11},{10,... | collective-permute-start | bytes 2211848 | tf_op jit(solution)/shard_map/ppermute | solution.py:761
  226.6 28.0 %collective-permute-start.31 = (bf16[4,48,1920]{2,1,0:T(8,128)(2,1)}, bf16[4,48,1920]{2,1,0:T(8,128)(2,1)}, u32[]{:S(2)}, u32[]{:S(2)}) collective-permute-start(bf16[4,48,1920]{2,1,0:T(8,128)(2,1)} %get-tuple-element.110), channel_id=1, source_target_pairs={{0,4},{1,5},{2,6},{3,7},{4,0},{5,1},{6,2},{7,3},{8,12},{9,13},{10,... | collective-permute-start | bytes 2211848 | tf_op jit(solution)/shard_map/ppermute | solution.py:761
  229.1 27.8 %collective-permute-start.44 = (bf16[2,48,1536]{2,1,0:T(8,128)(2,1)S(1)}, bf16[2,48,1536]{2,1,0:T(8,128)(2,1)}, u32[]{:S(2)}, u32[]{:S(2)}) collective-permute-start(bf16[2,48,1536]{2,1,0:T(8,128)(2,1)S(1)} %add_convert_fusion.4.refs_2_), channel_id=1, source_target_pairs={{0,4},{1,5},{2,6},{3,7},{4,0},{5,1},{6,2},{7,3},{8,12},{9,13},{10,... | collective-permute-start | bytes 884744 | tf_op jit(solution)/shard_map/ppermute | solution.py:761
  230.9 26.8 %collective-permute-start.43 = (bf16[2,48,1536]{2,1,0:T(8,128)(2,1)S(1)}, bf16[2,48,1536]{2,1,0:T(8,128)(2,1)}, u32[]{:S(2)}, u32[]{:S(2)}) collective-permute-start(bf16[2,48,1536]{2,1,0:T(8,128)(2,1)S(1)} %add_convert_fusion.5.refs_1_), channel_id=1, source_target_pairs={{0,2},{1,3},{2,0},{3,1},{4,6},{5,7},{6,4},{7,5},{8,10},{9,11},{10,... | collective-permute-start | bytes 884744 | tf_op jit(solution)/shard_map/ppermute | solution.py:761
  252.1 25.4 %collective-permute-start.28 = (bf16[4,48,1280]{2,1,0:T(8,128)(2,1)}, bf16[4,48,1280]{2,1,0:T(8,128)(2,1)S(1)}, u32[]{:S(2)}, u32[]{:S(2)}) collective-permute-start(bf16[4,48,1280]{2,1,0:T(8,128)(2,1)} %get-tuple-element.107), channel_id=1, source_target_pairs={{0,2},{1,3},{2,0},{3,1},{4,6},{5,7},{6,4},{7,5},{8,10},{9,11},{10,... | collective-permute-start | bytes 1474568 | tf_op jit(solution)/shard_map/ppermute | solution.py:761
  253.3 24.2 %collective-permute-start.29 = (bf16[4,48,1280]{2,1,0:T(8,128)(2,1)}, bf16[4,48,1280]{2,1,0:T(8,128)(2,1)S(1)}, u32[]{:S(2)}, u32[]{:S(2)}) collective-permute-start(bf16[4,48,1280]{2,1,0:T(8,128)(2,1)} %get-tuple-element.108), channel_id=1, source_target_pairs={{0,4},{1,5},{2,6},{3,7},{4,0},{5,1},{6,2},{7,3},{8,12},{9,13},{10,... | collective-permute-start | bytes 1474568 | tf_op jit(solution)/shard_map/ppermute | solution.py:761
  255.8 16.3 %collective-permute-start.32 = (bf16[2,48,1920]{2,1,0:T(8,128)(2,1)S(1)}, bf16[2,48,1920]{2,1,0:T(8,128)(2,1)S(1)}, u32[]{:S(2)}, u32[]{:S(2)}) collective-permute-start(bf16[2,48,1920]{2,1,0:T(8,128)(2,1)S(1)} %add_convert_fusion.2), channel_id=1, source_target_pairs={{0,2},{1,3},{2,0},{3,1},{4,6},{5,7},{6,4},{7,5},{8,10},{9,11},{10,... | collective-permute-start | bytes 1105928 | tf_op jit(solution)/shard_map/ppermute | solution.py:761
  256.9 16.0 %collective-permute-start.33 = (bf16[2,48,1920]{2,1,0:T(8,128)(2,1)S(1)}, bf16[2,48,1920]{2,1,0:T(8,128)(2,1)S(1)}, u32[]{:S(2)}, u32[]{:S(2)}) collective-permute-start(bf16[2,48,1920]{2,1,0:T(8,128)(2,1)S(1)} %add_convert_fusion.1), channel_id=1, source_target_pairs={{0,4},{1,5},{2,6},{3,7},{4,0},{5,1},{6,2},{7,3},{8,12},{9,13},{10,... | collective-permute-start | bytes 1105928 | tf_op jit(solution)/shard_map/ppermute | solution.py:761
  259.2 19.1 %collective-permute-start.45 = (bf16[2,48,1536]{2,1,0:T(8,128)(2,1)S(1)}, bf16[2,48,1536]{2,1,0:T(8,128)(2,1)S(1)}, u32[]{:S(2)}, u32[]{:S(2)}) collective-permute-start(bf16[2,48,1536]{2,1,0:T(8,128)(2,1)S(1)} %pad_maximum_fusion.4), channel_id=1, source_target_pairs={{0,8},{1,9},{2,10},{3,11},{4,12},{5,13},{6,14},{7,15},{8,0},{9,1},... | collective-permute-start | bytes 884744 | tf_op jit(solution)/shard_map/ppermute | solution.py:761
  275.0 28.5 %collective-permute-start.39 = (bf16[2,48,1920]{2,1,0:T(8,128)(2,1)}, bf16[2,48,1920]{2,1,0:T(8,128)(2,1)}, u32[]{:S(2)}, u32[]{:S(2)}) collective-permute-start(bf16[2,48,1920]{2,1,0:T(8,128)(2,1)} %pad_maximum_fusion.1), channel_id=1, source_target_pairs={{0,8},{1,9},{2,10},{3,11},{4,12},{5,13},{6,14},{7,15},{8,0},{9,1},... | collective-permute-start | bytes 1105928 | tf_op jit(solution)/shard_map/ppermute | solution.py:761
  277.6 20.9 %collective-permute-start.35 = (bf16[2,48,1280]{2,1,0:T(8,128)(2,1)S(1)}, bf16[2,48,1280]{2,1,0:T(8,128)(2,1)S(1)}, u32[]{:S(2)}, u32[]{:S(2)}) collective-permute-start(bf16[2,48,1280]{2,1,0:T(8,128)(2,1)S(1)} %add_convert_fusion.7.refs_1_), channel_id=1, source_target_pairs={{0,4},{1,5},{2,6},{3,7},{4,0},{5,1},{6,2},{7,3},{8,12},{9,13},{10,... | collective-permute-start | bytes 737288 | tf_op jit(solution)/shard_map/ppermute | solution.py:761
  279.0 18.4 %collective-permute-start.46 = (bf16[48,1536]{1,0:T(8,128)(2,1)}, bf16[48,1536]{1,0:T(8,128)(2,1)}, u32[]{:S(2)}, u32[]{:S(2)}) collective-permute-start(bf16[48,1536]{1,0:T(8,128)(2,1)} %fusion.8), channel_id=1, source_target_pairs={{0,16},{1,17},{2,18},{3,19},{4,20},{5,21},{6,22},{7,23},{8,24},{9,... | collective-permute-start | bytes 442376 | tf_op jit(solution)/shard_map/ppermute | solution.py:761
  281.9 16.6 %collective-permute-start.34 = (bf16[2,48,1280]{2,1,0:T(8,128)(2,1)S(1)}, bf16[2,48,1280]{2,1,0:T(8,128)(2,1)}, u32[]{:S(2)}, u32[]{:S(2)}) collective-permute-start(bf16[2,48,1280]{2,1,0:T(8,128)(2,1)S(1)} %add_convert_fusion.8.refs_0_), channel_id=1, source_target_pairs={{0,2},{1,3},{2,0},{3,1},{4,6},{5,7},{6,4},{7,5},{8,10},{9,11},{10,... | collective-permute-start | bytes 737288 | tf_op jit(solution)/shard_map/ppermute | solution.py:761
  298.5 7.7 %collective-permute-start.47 = (f32[24,1536]{1,0:T(8,128)S(1)}, f32[24,1536]{1,0:T(8,128)S(1)}, u32[]{:S(2)}, u32[]{:S(2)}) collective-permute-start(f32[24,1536]{1,0:T(8,128)S(1)} %slice_select_fusion.2), channel_id=1, source_target_pairs={{0,1},{1,0},{2,3},{3,2},{4,5},{5,4},{6,7},{7,6},{8,9},{9,8},{10,11... | collective-permute-start | bytes 442376 | tf_op jit(solution)/shard_map/ppermute | solution.py:761
  299.8 7.4 %collective-permute-start.36 = (bf16[48,1280]{1,0:T(8,128)(2,1)S(1)}, bf16[48,1280]{1,0:T(8,128)(2,1)S(1)}, u32[]{:S(2)}, u32[]{:S(2)}) collective-permute-start(bf16[48,1280]{1,0:T(8,128)(2,1)S(1)} %fusion.9), channel_id=1, source_target_pairs={{0,8},{1,9},{2,10},{3,11},{4,12},{5,13},{6,14},{7,15},{8,0},{9,1},... | collective-permute-start | bytes 368648 | tf_op jit(solution)/shard_map/ppermute | solution.py:761
  301.9 8.1 %collective-permute-start.38 = (bf16[48,1280]{1,0:T(8,128)(2,1)S(1)}, bf16[48,1280]{1,0:T(8,128)(2,1)S(1)}, u32[]{:S(2)}, u32[]{:S(2)}) collective-permute-start(bf16[48,1280]{1,0:T(8,128)(2,1)S(1)} %get-tuple-element.154), channel_id=1, source_target_pairs={{0,24},{1,25},{2,26},{3,27},{4,28},{5,29},{6,30},{7,31},{8,16},{9,... | collective-permute-start | bytes 368648 | tf_op jit(solution)/shard_map/ppermute | solution.py:761
  302.0 17.4 %collective-permute-start.37 = (bf16[48,1280]{1,0:T(8,128)(2,1)S(1)}, bf16[48,1280]{1,0:T(8,128)(2,1)S(1)}, u32[]{:S(2)}, u32[]{:S(2)}) collective-permute-start(bf16[48,1280]{1,0:T(8,128)(2,1)S(1)} %get-tuple-element.155), channel_id=1, source_target_pairs={{0,16},{1,17},{2,18},{3,19},{4,20},{5,21},{6,22},{7,23},{8,24},{9,... | collective-permute-start | bytes 368648 | tf_op jit(solution)/shard_map/ppermute | solution.py:761
  304.6 18.4 %collective-permute-start.40 = (bf16[48,1920]{1,0:T(8,128)(2,1)S(1)}, bf16[48,1920]{1,0:T(8,128)(2,1)S(1)}, u32[]{:S(2)}, u32[]{:S(2)}) collective-permute-start(bf16[48,1920]{1,0:T(8,128)(2,1)S(1)} %fusion.7), channel_id=1, source_target_pairs={{0,16},{1,17},{2,18},{3,19},{4,20},{5,21},{6,22},{7,23},{8,24},{9,... | collective-permute-start | bytes 552968 | tf_op jit(solution)/shard_map/ppermute | solution.py:761
  323.2 3.2 collective-permute-start.42
  (33 other events, 473.4 us)
Sparse Core Ops, SparseCore 0:
  11.6 96.5 all-gather.1
